TPU v7x, 256 devices: a whole 4x4x8 slice. The times are simulated.
256 devices in a mesh: grp: 16 (over z_hi, x), seq: 16 (over y, z_lo, core).
Axes of the slice: x: 4, y: 4, z: 8 (z_hi: 4, z_lo: 2; z = z_hi * 2 + z_lo), core: 2. Of those that a mesh axis runs over, the one named last changes fastest.
Arguments:
- t5_context: bfloat16 [16, 512, 4096], P('grp', None, 'seq'), may hold values from -6 to 6
- t5_resid: bfloat16 [16, 512, 4096], P('grp', 'seq'), may hold values from -6 to 6
- t5_out_weight: bfloat16 [4096, 4096], P('seq'), may hold values from -0.09375 to 0.09375
- t5_gain: float32 [4096], replicated, may hold values from 0.1 to 1.9
- text_weight: bfloat16 [4096, 6144], P(None, 'seq'), may hold values from -0.09375 to 0.09375
- prompt_len: int32 [16], P('grp'), may hold values from 1 to 512
- text_order: int32 [16, 32], P('grp'), may hold values from 0 to 31, each once within a row
- img_qkv: bfloat16 [16, 2048, 6144], P('grp', 'seq'), may hold values from -8 to 8
- d_img_out: bfloat16 [16, 2048, 2048], P('grp', 'seq'), may hold values from -6 to 6
- d_txt_out: bfloat16 [16, 512, 2048], P('grp', 'seq'), may hold values from -6 to 6
Outputs:
- img_attn_out: bfloat16 [16, 2048, 2048], P('grp', 'seq')
- text_attn_out: bfloat16 [16, 512, 2048], P('grp', 'seq')
- image_qkv_grad: bfloat16 [16, 2048, 6144], P('grp', 'seq')
- text_weight_grad: float32 [4096, 6144], P('grp', 'seq')
Inputs may be any that keep to these rules, and one draw needn't show every extreme that they name: `text_order`: each row holds every block slot 0 to 31 once.
All inputs are finite; a program needn't handle non-finite values.
Results may differ from a plain program's by a relative error of at most 0.02.
Values may be sent and summed in bfloat16 or wider, within the bound.
No kernel may reach another device: no remote copies, remote signals or barrier semaphores. Data moves between devices by JAX's collectives and lax.ppermute only.
A program may use at most 128 MiB of HBM per device.

v0:
```python
import jax
import jax.numpy as jnp
from jax import lax
from jax.experimental import pallas as pl
from jax.experimental.pallas import tpu as pltpu
from jax.sharding import Mesh
from jax.sharding import PartitionSpec as P

HEAD_DIM = 128
HEADS = 16
PROMPT = 512
IMAGE = 2048
TOTAL = PROMPT + IMAGE
BLOCK_ROWS = 16
TEXT_BLOCKS = 32
SHARE = IMAGE // HEADS
PACK_ROWS = SHARE + BLOCK_ROWS
PACK_COLS = 4 * HEAD_DIM
QUERY_BLOCK = 256
EXPONENT = HEAD_DIM**-0.5 * 1.4426950408889634
FORWARD_ROWS = 512
PACK_HEADS = 4
CHAINS = 2
WIDTH = 4096
FEATURES = WIDTH // HEADS
TEXT_SHARE = PROMPT // HEADS
HALF_PROMPT = PROMPT // 2
TEXT_DEPTH = 1024
CHIPS = [(ahead, across) for ahead in range(4) for across in range(2)]

BF16 = jnp.bfloat16
F32 = jnp.float32
SEQ = ("y", "z_lo", "core")
GRP = ("z_hi", "x")
CONTRACT_LAST = (((1,), (1,)), ((), ()))
CONTRACT_FIRST = (((0,), (0,)), ((), ()))
VMEM_LIMIT = 48 * 2**20
WHOLE_VMEM = 60 * 2**20


def matmul(a, b, dims=(((1,), (0,)), ((), ()))):
    return lax.dot_general(a, b, dims, preferred_element_type=F32)


def pack_kernel(qkv_hbm, grad_hbm, text_hbm, packed_hbm, *refs):
    qkv_ref, grad_ref, text_ref, packed_ref, loaded, stored = refs
    loads = []
    for source, target in ((grad_hbm, grad_ref), (text_hbm, text_ref)):
        loads.append(pltpu.make_async_copy(source, target, loaded.at[len(loads)]))
    width = 3 * HEAD_DIM * PACK_HEADS
    for group in range(HEADS // PACK_HEADS):
        columns = slice(group * width, (group + 1) * width)
        source, target = qkv_hbm.at[:, columns], qkv_ref.at[:, columns]
        loads.append(pltpu.make_async_copy(source, target, loaded.at[len(loads)]))
    for load in loads:
        load.start()
    loads[0].wait()
    loads[1].wait()
    stores = []
    for group in range(HEADS // PACK_HEADS):
        loads[2 + group].wait()
        heads = slice(group * PACK_HEADS, (group + 1) * PACK_HEADS)
        for head in range(heads.start, heads.stop):
            columns = slice(head * HEAD_DIM, (head + 1) * HEAD_DIM)
            wide = slice(3 * head * HEAD_DIM, 3 * (head + 1) * HEAD_DIM)
            packed_ref[head, :SHARE, : 3 * HEAD_DIM] = qkv_ref[:, wide]
            packed_ref[head, :SHARE, 3 * HEAD_DIM :] = grad_ref[:, columns]
            packed_ref[head, SHARE:, :HEAD_DIM] = text_ref[:BLOCK_ROWS, columns]
            packed_ref[head, SHARE:, HEAD_DIM : 2 * HEAD_DIM] = text_ref[BLOCK_ROWS:, columns]
            packed_ref[head, SHARE:, 2 * HEAD_DIM :] = jnp.zeros(
                (BLOCK_ROWS, 2 * HEAD_DIM), BF16
            )
        store = pltpu.make_async_copy(
            packed_ref.at[heads], packed_hbm.at[heads], stored.at[group]
        )
        store.start()
        stores.append(store)
    for store in stores:
        store.wait()


def unpack_kernel(packed_ref, out_ref, text_ref, qkv_ref):
    for head in range(HEADS):
        columns = slice(head * HEAD_DIM, (head + 1) * HEAD_DIM)
        wide = slice(3 * head * HEAD_DIM, 3 * (head + 1) * HEAD_DIM)
        out_ref[:, columns] = packed_ref[head, :SHARE, :HEAD_DIM]
        qkv_ref[:, wide] = packed_ref[head, :SHARE, HEAD_DIM:]
        text_ref[:BLOCK_ROWS, columns] = packed_ref[head, SHARE:, :HEAD_DIM]
        text_ref[BLOCK_ROWS:, columns] = packed_ref[head, SHARE:, HEAD_DIM : 2 * HEAD_DIM]


def whole_call(kernel, out_shape, smem_inputs, vmem_inputs, scratch, flops, moved, limit=None):
    in_vmem = pl.BlockSpec(memory_space=pltpu.VMEM)
    in_smem = pl.BlockSpec(memory_space=pltpu.SMEM)
    return pl.pallas_call(
        kernel,
        out_shape=out_shape,
        in_specs=[in_smem] * smem_inputs + [in_vmem] * vmem_inputs,
        out_specs=jax.tree.map(lambda _: in_vmem, out_shape),
        scratch_shapes=scratch,
        compiler_params=pltpu.CompilerParams(vmem_limit_bytes=limit or VMEM_LIMIT),
        cost_estimate=pl.CostEstimate(flops=flops, bytes_accessed=moved, transcendentals=0),
    )


def rows_of(*shape):
    return jax.ShapeDtypeStruct(shape, BF16)


def pack(qkv, grad, text):
    anywhere = pl.BlockSpec(memory_space=pltpu.HBM)
    groups = HEADS // PACK_HEADS
    return pl.pallas_call(
        pack_kernel,
        out_shape=rows_of(HEADS, PACK_ROWS, PACK_COLS),
        in_specs=[anywhere] * 3,
        out_specs=anywhere,
        scratch_shapes=[
            pltpu.VMEM(qkv.shape, BF16),
            pltpu.VMEM(grad.shape, BF16),
            pltpu.VMEM(text.shape, BF16),
            pltpu.VMEM((HEADS, PACK_ROWS, PACK_COLS), BF16),
            pltpu.SemaphoreType.DMA((2 + groups,)),
            pltpu.SemaphoreType.DMA((groups,)),
        ],
        compiler_params=pltpu.CompilerParams(vmem_limit_bytes=WHOLE_VMEM),
        cost_estimate=pl.CostEstimate(flops=0, bytes_accessed=2**22, transcendentals=0),
    )(qkv, grad, text)


def unpack(packed):
    shapes = [
        rows_of(SHARE, HEADS * HEAD_DIM),
        rows_of(2 * BLOCK_ROWS, HEADS * HEAD_DIM),
        rows_of(SHARE, HEADS * 3 * HEAD_DIM),
    ]
    return whole_call(unpack_kernel, shapes, 0, 1, [], 0, 2**22)(packed)


def row_block(place_ref, ahead, across, other_core):
    y = lax.rem(place_ref[0] + ahead, 4)
    z = 1 - place_ref[1] if across else place_ref[1]
    core = 1 - place_ref[2] if other_core else place_ref[2]
    return (y * 2 + z) * 2 + core


def partial_kernel(place_ref, own_ref, other_ref, own_weight_ref, other_weight_ref, *refs):
    chunk_refs, rows_ref = refs[:8], refs[8]
    for index, (ahead, across) in enumerate(CHIPS):
        block = row_block(place_ref, ahead, across, False)
        rows = pl.ds(pl.multiple_of(block * TEXT_SHARE, TEXT_SHARE), TEXT_SHARE)
        to = slice(index * TEXT_SHARE, (index + 1) * TEXT_SHARE)
        rows_ref[to, :FEATURES] = own_ref[rows, :]
        rows_ref[to, FEATURES:] = other_ref[rows, :]

    def body(step, carry):
        columns = pl.ds(pl.multiple_of(step * 512, 512), 512)
        sums = matmul(rows_ref[:, :FEATURES], own_weight_ref[:, columns])
        sums += matmul(rows_ref[:, FEATURES:], other_weight_ref[:, columns])
        for index, chunk_ref in enumerate(chunk_refs):
            rows = slice(index * TEXT_SHARE, (index + 1) * TEXT_SHARE)
            chunk_ref[:, columns] = sums[rows].astype(BF16)
        return carry

    lax.fori_loop(0, WIDTH // 512, body, 0)


def text_kernel(place_ref, *refs):
    block_refs, weight_ref, text_ref = refs[:16], refs[16], refs[17]
    kept_hbm, sent_hbms, encoded_ref, total_ref, stored = refs[18], refs[19:22], *refs[22:]
    for index, block_ref in enumerate(block_refs):
        ahead, across = CHIPS[index % 8]
        block = row_block(place_ref, ahead, across, index >= 8)
        rows = pl.ds(pl.multiple_of(block * TEXT_SHARE, TEXT_SHARE), TEXT_SHARE)
        encoded_ref[rows, :] = block_ref[...]
    half = pl.ds(pl.multiple_of(place_ref[2] * HALF_PROMPT, HALF_PROMPT), HALF_PROMPT)
    stores = []
    for ahead in range(4):
        x = lax.rem(place_ref[4] + ahead, 4)
        for z_hi in range(4):
            at = pl.ds(pl.multiple_of((z_hi * 4 + x) * FEATURES, FEATURES), FEATURES)
            to = slice(z_hi * FEATURES, (z_hi + 1) * FEATURES)
            if ahead:
                source, target = encoded_ref.at[half, at], sent_hbms[ahead - 1].at[:, to]
            else:
                source, target = encoded_ref.at[:, at], kept_hbm.at[:, to]
            store = pltpu.make_async_copy(source, target, stored.at[len(stores)])
            store.start()
            stores.append(store)
    total_ref[...] = jnp.zeros_like(total_ref)

    def body(step, carry):
        depth = pl.ds(pl.multiple_of(step * TEXT_DEPTH, TEXT_DEPTH), TEXT_DEPTH)
        total_ref[...] += matmul(encoded_ref[:, depth], weight_ref[depth, :])
        return carry

    lax.fori_loop(0, WIDTH // TEXT_DEPTH, body, 0)
    text_ref[...] = total_ref[...].astype(BF16)
    for store in stores:
        store.wait()


def weight_kernel(place_ref, kept_ref, *refs):
    near_refs, far_refs, grad_refs = refs[:3], refs[3:6], refs[6:10]
    kept_sum_ref, sent_refs, totals_ref = refs[10], refs[11:14], refs[14]
    near = pl.ds(pl.multiple_of(place_ref[2] * HALF_PROMPT, HALF_PROMPT), HALF_PROMPT)
    far = pl.ds(pl.multiple_of((1 - place_ref[2]) * HALF_PROMPT, HALF_PROMPT), HALF_PROMPT)

    def body(ahead, carry):
        z_hi = lax.rem(place_ref[3] + ahead, 4)
        at = pl.ds(pl.multiple_of(z_hi * FEATURES, FEATURES), FEATURES)
        total = matmul(grad_refs[0][...], kept_ref[:, at], CONTRACT_FIRST)
        for grad_ref, near_ref, far_ref in zip(grad_refs[1:], near_refs, far_refs):
            total += matmul(grad_ref[near, :], near_ref[:, at], CONTRACT_FIRST)
            total += matmul(grad_ref[far, :], far_ref[:, at], CONTRACT_FIRST)
        totals_ref[ahead] = total
        return carry

    lax.fori_loop(0, 4, body, 0)
    kept_sum_ref[...] = totals_ref[0]
    for step, sent_ref in enumerate(sent_refs):
        sent_ref[...] = totals_ref[step + 1].astype(BF16)


def total_kernel(kept_ref, *refs):
    total = kept_ref[...]
    for part_ref in refs[:3]:
        total += part_ref[...].astype(F32)
    refs[3][...] = total.T


def exp_rows(scores, maximum):
    return jnp.exp2((scores - maximum) * EXPONENT).astype(BF16)


def spread(rows, columns):
    return jnp.concatenate([rows] * (columns // HEAD_DIM), axis=1)


def row_sums(out_grad, output):
    total = jnp.sum(out_grad.astype(F32) * output, axis=-1, keepdims=True)
    return jnp.broadcast_to(total, output.shape)


def score_gradient(weights, prob_grad, row_delta):
    wide = spread(row_delta, weights.shape[1])
    return (weights.astype(F32) * (prob_grad - wide)).astype(BF16)


def chains(count, first, then):
    ahead = first(0)
    for chain in range(count):
        current = ahead
        if chain + 1 < count:
            ahead = first(chain + 1)
        then(chain, current)


def chain_rows(chain):
    return slice(chain * QUERY_BLOCK, (chain + 1) * QUERY_BLOCK)


def image_forward_kernel(
    order_ref,
    packed_ref,
    weights_ref,
    rows_ref,
    output_ref,
    maximum_ref,
    total_ref,
    text_do_ref,
    k_ref,
    v_ref,
):
    step = pl.program_id(0)

    @pl.when(step == 0)
    def _():
        v_ref[:, HEAD_DIM:] = jnp.ones((IMAGE, HEAD_DIM), BF16)
        for src in range(HEADS):
            at = slice(src * SHARE, (src + 1) * SHARE)
            k_ref[at, :] = packed_ref[src, :SHARE, HEAD_DIM : 2 * HEAD_DIM]
            v_ref[at, :HEAD_DIM] = packed_ref[src, :SHARE, 2 * HEAD_DIM : 3 * HEAD_DIM]
        for block in range(TEXT_BLOCKS):
            slot = order_ref[block]
            columns = pl.ds(pl.multiple_of((slot % 2) * HEAD_DIM, HEAD_DIM), HEAD_DIM)
            text_do_ref[block * BLOCK_ROWS : (block + 1) * BLOCK_ROWS, :] = packed_ref[
                slot // 2, SHARE:, columns
            ]

    parts = FORWARD_ROWS // SHARE
    for part in range(parts):
        at = slice(part * SHARE, (part + 1) * SHARE)
        rows_ref[at, :] = packed_ref[step * parts + part, :SHARE, :]

    def first(chain):
        return matmul(rows_ref[chain_rows(chain), :HEAD_DIM], k_ref[...], CONTRACT_LAST)

    def then(chain, scores):
        at = chain_rows(chain)
        maximum = jnp.max(scores, axis=-1, keepdims=True)
        weights = exp_rows(scores, maximum)
        weights_ref[at, :] = weights
        both = matmul(weights, v_ref[...])
        output_ref[at, :] = both[:, :HEAD_DIM]
        total_ref[at, :] = both[:, HEAD_DIM:]
        maximum_ref[at, :] = jnp.broadcast_to(maximum, (QUERY_BLOCK, HEAD_DIM))

    chains(FORWARD_ROWS // QUERY_BLOCK, first, then)


def attention_kernel(
    length_ref,
    order_ref,
    text_ref,
    text_do_ref,
    rows_ref,
    weights_ref,
    output_ref,
    maximum_ref,
    total_ref,
    sent_hbm,
    text_grad_ref,
    sent_ref,
    dkt_ref,
    dvt_ref,
    image_dkt_ref,
    image_dvt_ref,
    tv_ref,
    stored,
):
    step = pl.program_id(0)
    factor = HEAD_DIM**-0.5
    text_keys = text_ref[:, HEAD_DIM : 2 * HEAD_DIM]
    text_values = text_ref[:, 2 * HEAD_DIM :]
    keys = rows_ref[:, HEAD_DIM : 2 * HEAD_DIM]
    values = rows_ref[:, 2 * HEAD_DIM : 3 * HEAD_DIM]
    live = lax.broadcasted_iota(jnp.int32, (1, PROMPT), 1) < length_ref[0]
    sums = (dkt_ref, dvt_ref, image_dkt_ref, image_dvt_ref)

    def text_scores(queries):
        return jnp.where(live, matmul(queries, text_keys, CONTRACT_LAST), -1e30)

    @pl.when(step == 0)
    def _():
        tv_ref[:, :HEAD_DIM] = text_values
        tv_ref[:, HEAD_DIM:] = jnp.ones((PROMPT, HEAD_DIM), BF16)
        sent_ref[:, SHARE:, 2 * HEAD_DIM :] = jnp.zeros((HEADS, BLOCK_ROWS, 2 * HEAD_DIM), BF16)
        for sum_ref in sums:
            sum_ref[...] = jnp.zeros_like(sum_ref)

        def body(chain, carry):
            rows = pl.ds(pl.multiple_of(chain * QUERY_BLOCK, QUERY_BLOCK), QUERY_BLOCK)
            queries = text_ref[rows, :HEAD_DIM]
            to_text = text_scores(queries)
            to_image = matmul(queries, keys, CONTRACT_LAST)
            maximum = jnp.maximum(
                jnp.max(to_text, axis=-1, keepdims=True), jnp.max(to_image, axis=-1, keepdims=True)
            )
            text_weights, image_weights = exp_rows(to_text, maximum), exp_rows(to_image, maximum)
            total = jnp.sum(image_weights.astype(F32), axis=-1, keepdims=True)
            both = matmul(text_weights, tv_ref[...])
            inverse = 1.0 / (both[:, HEAD_DIM:] + total)
            output = (both[:, :HEAD_DIM] + matmul(image_weights, values)) * inverse
            out_grad = (text_do_ref[rows, :].astype(F32) * inverse).astype(BF16)
            row_delta = row_sums(out_grad, output)
            prob_grads = [matmul(out_grad, part, CONTRACT_LAST) for part in (text_values, values)]
            text_scored = score_gradient(text_weights, prob_grads[0], row_delta)
            image_scored = score_gradient(image_weights, prob_grads[1], row_delta)
            query_grad = matmul(text_scored, text_keys) + matmul(image_scored, keys)
            text_grad_ref[rows, :HEAD_DIM] = (query_grad * factor).astype(BF16)
            dkt_ref[...] += matmul(queries, text_scored, CONTRACT_FIRST)
            dvt_ref[...] += matmul(out_grad, text_weights, CONTRACT_FIRST)
            image_dkt_ref[...] += matmul(queries, image_scored, CONTRACT_FIRST)
            image_dvt_ref[...] += matmul(out_grad, image_weights, CONTRACT_FIRST)
            output = output.astype(BF16)
            blocks = QUERY_BLOCK // BLOCK_ROWS
            for block in range(blocks):
                slot = order_ref[chain * blocks + block]
                columns = pl.ds(pl.multiple_of((slot % 2) * HEAD_DIM, HEAD_DIM), HEAD_DIM)
                sent_ref[slot // 2, SHARE:, columns] = output[
                    block * BLOCK_ROWS : (block + 1) * BLOCK_ROWS
                ]
            return carry

        lax.fori_loop(0, PROMPT // QUERY_BLOCK, body, 0)

    @pl.when(step > 0)
    def _():
        def place(chain):
            start = (step - 1) * FORWARD_ROWS + chain * QUERY_BLOCK
            return pl.ds(pl.multiple_of(start, QUERY_BLOCK), QUERY_BLOCK)

        places = [chain_rows(chain) for chain in range(CHAINS)]
        scores = [text_scores(rows_ref[place(chain), :HEAD_DIM]) for chain in range(CHAINS)]
        weights = []
        for at, to_text in zip(places, scores):
            image_maximum = maximum_ref[at, :]
            maximum = jnp.maximum(image_maximum, jnp.max(to_text, axis=-1, keepdims=True))
            scale = jnp.exp2((image_maximum - maximum) * EXPONENT)
            weights.append((exp_rows(to_text, spread(maximum, PROMPT)), scale))
        middle = []
        for chain, (at, (text_weights, scale)) in enumerate(zip(places, weights)):
            both = matmul(text_weights, tv_ref[...])
            inverse = 1.0 / (both[:, HEAD_DIM:] + scale * total_ref[at, :])
            output = (scale * output_ref[at, :] + both[:, :HEAD_DIM]) * inverse
            cotangent = rows_ref[place(chain), 3 * HEAD_DIM :].astype(F32)
            out_grad = (cotangent * inverse).astype(BF16)
            image_out_grad = (cotangent * (scale * inverse)).astype(BF16)
            prob_grad = matmul(out_grad, text_values, CONTRACT_LAST)
            image_prob_grad = matmul(image_out_grad, values, CONTRACT_LAST)
            middle.append(
                (
                    (out_grad, row_sums(out_grad, output), prob_grad),
                    (image_out_grad, row_sums(image_out_grad, output), image_prob_grad),
                )
            )
            output = output.astype(BF16)
            for part in range(QUERY_BLOCK // SHARE):
                dest = ((step - 1) * FORWARD_ROWS + chain * QUERY_BLOCK) // SHARE + part
                sent_ref[dest, :SHARE, :HEAD_DIM] = output[part * SHARE : (part + 1) * SHARE]
        for chain, at in enumerate(places):
            queries = rows_ref[place(chain), :HEAD_DIM]
            (out_grad, row_delta, prob_grad), image_parts = middle[chain]
            image_out_grad, image_delta, image_prob_grad = image_parts
            text_weights, image_weights = weights[chain][0], weights_ref[at, :]
            text_scored = score_gradient(text_weights, prob_grad, row_delta)
            image_scored = score_gradient(image_weights, image_prob_grad, image_delta)
            query_grad = matmul(text_scored, text_keys) + matmul(image_scored, keys)
            query_grad = (query_grad * factor).astype(BF16)
            for part in range(QUERY_BLOCK // SHARE):
                dest = ((step - 1) * FORWARD_ROWS + chain * QUERY_BLOCK) // SHARE + part
                sent_ref[dest, :SHARE, HEAD_DIM : 2 * HEAD_DIM] = query_grad[
                    part * SHARE : (part + 1) * SHARE
                ]
            dkt_ref[...] += matmul(queries, text_scored, CONTRACT_FIRST)
            dvt_ref[...] += matmul(out_grad, text_weights, CONTRACT_FIRST)
            image_dkt_ref[...] += matmul(queries, image_scored, CONTRACT_FIRST)
            image_dvt_ref[...] += matmul(image_out_grad, image_weights, CONTRACT_FIRST)

    @pl.when(step == IMAGE // FORWARD_ROWS)
    def _():
        text_grad_ref[:, HEAD_DIM : 2 * HEAD_DIM] = (dkt_ref[...] * factor).T.astype(BF16)
        text_grad_ref[:, 2 * HEAD_DIM :] = dvt_ref[...].T.astype(BF16)
        stores = []
        for dest in range(HEADS):
            at = slice(dest * SHARE, (dest + 1) * SHARE)
            sent_ref[dest, :SHARE, 2 * HEAD_DIM : 3 * HEAD_DIM] = (
                (image_dkt_ref[:, at] * factor).T.astype(BF16)
            )
            sent_ref[dest, :SHARE, 3 * HEAD_DIM :] = image_dvt_ref[:, at].T.astype(BF16)
            if dest % 4 == 3:
                group = slice(dest - 3, dest + 1)
                store = pltpu.make_async_copy(
                    sent_ref.at[group], sent_hbm.at[group], stored.at[dest // 4]
                )
                store.start()
                stores.append(store)
        for store in stores:
            store.wait()


def grid_call(kernel, steps, in_specs, out_shape, out_specs, scratch, products):
    return pl.pallas_call(
        kernel,
        grid=(steps,),
        out_shape=out_shape,
        in_specs=in_specs,
        out_specs=out_specs,
        scratch_shapes=scratch,
        compiler_params=pltpu.CompilerParams(vmem_limit_bytes=WHOLE_VMEM),
        cost_estimate=pl.CostEstimate(
            flops=60 * products * HEAD_DIM, bytes_accessed=2**29, transcendentals=0
        ),
    )


IN_SMEM = pl.BlockSpec(memory_space=pltpu.SMEM)


def fixed(*shape):
    return pl.BlockSpec(shape, lambda step: (0,) * len(shape))


def per_block(rows, columns, skip=0):
    return pl.BlockSpec((rows, columns), lambda step: (jnp.maximum(step - skip, 0), 0))


def image_forward(order, packed):
    floats = jax.ShapeDtypeStruct((IMAGE, HEAD_DIM), F32)
    block = per_block(FORWARD_ROWS, HEAD_DIM)
    return grid_call(
        image_forward_kernel,
        IMAGE // FORWARD_ROWS,
        [IN_SMEM, fixed(HEADS, PACK_ROWS, PACK_COLS)],
        [rows_of(IMAGE, IMAGE), rows_of(IMAGE, PACK_COLS)] + [floats] * 3
        + [rows_of(PROMPT, HEAD_DIM)],
        [per_block(FORWARD_ROWS, IMAGE), per_block(FORWARD_ROWS, PACK_COLS)] + [block] * 3
        + [fixed(PROMPT, HEAD_DIM)],
        [pltpu.VMEM((IMAGE, HEAD_DIM), BF16), pltpu.VMEM((IMAGE, 2 * HEAD_DIM), BF16)],
        2 * IMAGE * IMAGE,
    )(order, packed)


def attention(length, order, text_rows, text_do, rows, weights, output, maximum, total):
    block = per_block(FORWARD_ROWS, HEAD_DIM, 1)
    text_sum = pltpu.VMEM((HEAD_DIM, PROMPT), F32)
    image_sum = pltpu.VMEM((HEAD_DIM, IMAGE), F32)
    return grid_call(
        attention_kernel,
        1 + IMAGE // FORWARD_ROWS,
        [IN_SMEM, IN_SMEM, fixed(PROMPT, 3 * HEAD_DIM), fixed(PROMPT, HEAD_DIM)]
        + [fixed(IMAGE, PACK_COLS), per_block(FORWARD_ROWS, IMAGE, 1)] + [block] * 3,
        [rows_of(HEADS, PACK_ROWS, PACK_COLS), rows_of(PROMPT, 3 * HEAD_DIM)],
        [pl.BlockSpec(memory_space=pltpu.HBM), fixed(PROMPT, 3 * HEAD_DIM)],
        [pltpu.VMEM((HEADS, PACK_ROWS, PACK_COLS), BF16), text_sum, text_sum, image_sum, image_sum]
        + [pltpu.VMEM((PROMPT, 2 * HEAD_DIM), BF16), pltpu.SemaphoreType.DMA((4,))],
        6 * TOTAL * TOTAL - 2 * IMAGE * IMAGE,
    )(length, order, text_rows, text_do, rows, weights, output, maximum, total)


def shift(rows, axis, step):
    size = 2 if axis in ("z_lo", "core") else 4
    return lax.ppermute(rows, axis, [(i, (i + step) % size) for i in range(size)])


def add(*rows):
    return sum(part.astype(F32) for part in rows)


def encode(place, context, residual, weight, gain, packed, order):
    other_weight = shift(weight, "core", 1)
    other = shift(context, "core", 1)
    other_weight, packed = lax.optimization_barrier((other_weight, packed))
    packed = lax.all_to_all(packed, SEQ, split_axis=0, concat_axis=0, tiled=True)
    chunks = whole_call(
        partial_kernel,
        [rows_of(TEXT_SHARE, WIDTH)] * 8,
        1,
        4,
        [pltpu.VMEM((8 * TEXT_SHARE, 2 * FEATURES), BF16)],
        2 * 8 * TEXT_SHARE * 2 * FEATURES * WIDTH,
        2**23,
    )(place, context, other, weight, other_weight)
    part = dict(zip(CHIPS, chunks))
    from_across = shift(part[2, 1], "z_lo", 1)
    from_below = shift(part[1, 1], "y", 1)
    from_above = shift(part[3, 1], "y", -1)
    below = shift(part[1, 0], "y", 1)
    above = shift(part[3, 0], "y", -1)
    opposite = add(part[2, 0], from_across).astype(BF16)
    across = add(part[0, 1], from_below, from_above).astype(BF16)
    packed, opposite, across = lax.optimization_barrier((packed, opposite, across))
    forward = image_forward(order, packed)
    opposite = shift(opposite, "y", 2)
    across = shift(across, "z_lo", 1)
    forward, opposite, across = lax.optimization_barrier((forward, opposite, across))
    stream = add(residual, part[0, 0], below, above, opposite, across)
    inv_norm = lax.rsqrt(jnp.mean(stream * stream, axis=-1, keepdims=True) + 1e-06)
    encoded = (stream * inv_norm * gain).astype(BF16)
    held = {(0, 0): encoded}
    held[0, 1] = shift(encoded, "z_lo", 1)
    held[3, 0] = shift(encoded, "y", 1)
    held[1, 0] = shift(encoded, "y", -1)
    held[2, 0] = shift(encoded, "y", 2)
    held[3, 1] = shift(held[0, 1], "y", 1)
    held[1, 1] = shift(held[0, 1], "y", -1)
    held[2, 1] = shift(held[2, 0], "z_lo", 1)
    early = [held[chip] for chip in CHIPS[:5] + CHIPS[6:7]]
    early = lax.optimization_barrier(early)
    held.update(zip(CHIPS[:5] + CHIPS[6:7], early))
    own = [held[chip] for chip in CHIPS]
    return own + [shift(rows, "core", 1) for rows in own], forward


def project(place, blocks, weight):
    columns = weight.shape[1]
    quarter = 4 * FEATURES
    in_vmem = pl.BlockSpec(memory_space=pltpu.VMEM)
    in_hbm = pl.BlockSpec(memory_space=pltpu.HBM)
    return pl.pallas_call(
        text_kernel,
        out_shape=[rows_of(PROMPT, columns), rows_of(PROMPT, quarter)]
        + [rows_of(HALF_PROMPT, quarter)] * 3,
        in_specs=[IN_SMEM] + [in_vmem] * 17,
        out_specs=[in_vmem] + [in_hbm] * 4,
        scratch_shapes=[
            pltpu.VMEM((PROMPT, WIDTH), BF16),
            pltpu.VMEM((PROMPT, columns), F32),
            pltpu.SemaphoreType.DMA((16,)),
        ],
        compiler_params=pltpu.CompilerParams(vmem_limit_bytes=VMEM_LIMIT),
        cost_estimate=pl.CostEstimate(
            flops=2 * PROMPT * WIDTH * columns, bytes_accessed=2**23, transcendentals=0
        ),
    )(place, *blocks, weight)


def weight_sums(place, kept, near, far, grads):
    columns = grads[0].shape[1]
    total = jax.ShapeDtypeStruct((columns, FEATURES), F32)
    kept_sum, *sent = whole_call(
        weight_kernel,
        [total] + [rows_of(columns, FEATURES)] * 3,
        1,
        11,
        [pltpu.VMEM((4, columns, FEATURES), F32)],
        12 * 2 * 4 * PROMPT * 4 * FEATURES * columns,
        2**23,
        WHOLE_VMEM,
    )(place, kept, *near, *far, *grads)
    return [kept_sum] + [shift(rows, "z_hi", step + 1) for step, rows in enumerate(sent)]


def weight_total(kept_sum, *parts):
    shape = jax.ShapeDtypeStruct(kept_sum.shape[::-1], F32)
    return whole_call(total_kernel, shape, 0, 4, [], 0, 2**20)(kept_sum, *parts)


def on_device(
    t5_context,
    t5_resid,
    t5_out_weight,
    t5_gain,
    text_weight,
    prompt_len,
    text_order,
    img_qkv,
    d_img_out,
    d_txt_out,
):
    packed = pack(img_qkv[0], d_img_out[0], d_txt_out[0])
    place = jnp.stack([lax.axis_index(axis) for axis in SEQ + GRP])
    blocks, forward = encode(
        place, t5_context[0], t5_resid[0], t5_out_weight, t5_gain, packed, text_order[0]
    )
    weights, rows, *stats, text_do = forward
    text_rows, kept, *slices = project(place, blocks, text_weight)
    near = [shift(rows, "x", step + 1) for step, rows in enumerate(slices)]
    sent, text_grad = attention(
        prompt_len, text_order[0], text_rows, text_do, rows, weights, *stats
    )
    *near, sent = lax.optimization_barrier((*near, sent))
    grads = [text_grad] + [shift(text_grad, "x", step) for step in (1, 2)] + [None]
    far = [shift(rows, "core", 1) for rows in near]
    last, far = lax.optimization_barrier((text_grad, far))
    grads[3] = shift(last, "x", 3)
    sums = weight_sums(place, kept, near, far, grads)
    received = lax.all_to_all(sent, SEQ, split_axis=0, concat_axis=0, tiled=True)
    outputs = unpack(received)
    sums, outputs = lax.optimization_barrier((sums, outputs))
    image_out, text_out, image_qkv_grad = outputs
    text_weight_grad = weight_total(*sums)
    return (image_out[None], text_out[None], image_qkv_grad[None], text_weight_grad)


def solution(mesh):
    fine = Mesh(mesh.devices.reshape(4, 4, 4, 2, 2), GRP + SEQ)
    in_specs = (
        P(GRP, None, SEQ),
        P(GRP, SEQ, None),
        P(SEQ, None),
        P(),
        P(None, SEQ),
        P(GRP),
        P(GRP, None),
        P(GRP, SEQ, None),
        P(GRP, SEQ, None),
        P(GRP, SEQ, None),
    )
    out_specs = (
        P(GRP, SEQ, None),
        P(GRP, SEQ, None),
        P(GRP, SEQ, None),
        P(GRP, SEQ),
    )
    return jax.shard_map(
        on_device, mesh=fine, in_specs=in_specs, out_specs=out_specs, check_vma=False
    )
```

profile of v0, /device:TPU:8, one launch (start us, length us, event | category | flops | bytes accessed | tf_op | source)
XLA Modules:
  0.0 179.0 jit_solution(3921950398270117288)
XLA Ops:
  0.7 2.8 %shard_map.129 = bf16[16,144,512]{2,1,0:T(8,128)(2,1)} custom-call(bf16[128,6144]{1,0:T(8,128)(2,1)} %bitcast.22, bf16[128,2048]{1,0:T(8,128)(2,1)} %bitcast.23, bf16[32,2048]{1,0:T(8,128)(2,1)} %bitcast.24), custom_call_target="tpu_custom_call" | custom-call | bytes 4194304 | tf_op jit(solution)/shard_map/pallas_call | solution.py:113
  3.5 1.7 collective-permute-done.1.other_weight_ref
  5.2 6.4 %all-to-all-start = ((bf16[16,144,512]{2,1,0:T(8,128)(2,1)}), bf16[16,144,512]{2,1,0:T(8,128)(2,1)}, u32[]{:S(2)}, u32[]{:S(2)}) async-start(bf16[16,144,512]{2,1,0:T(8,128)(2,1)} %shard_map.129), calls=%async_computation | async-start | bytes 4718592 | tf_op jit(solution)/shard_map/all_to_all | solution.py:535
  11.9 1.3 collective-permute-done.other_ref
  13.3 4.1 %shard_map.130 = (bf16[32,4096]{1,0:T(8,128)(2,1)S(1)}, bf16[32,4096]{1,0:T(8,128)(2,1)S(1)}, bf16[32,4096]{1,0:T(8,128)(2,1)S(1)}, bf16[32,4096]{1,0:T(8,128)(2...) custom-call(s32[5]{0:T(128)S(1)} %stack.23.place_ref, ...), custom_call_target="tpu_custom_call" | custom-call | flops 1073741824 | bytes 8388608 | tf_op jit(solution)/shard_map/pallas_call | solution.py:536
  17.3 1.6 collective-permute-start.4
  18.9 1.5 collective-permute-start.5
  20.4 0.5 collective-permute-start.6
  20.9 1.5 collective-permute-start.2
  22.4 0.5 collective-permute-start.3
  22.9 22.5 %collective-permute-done.4 = bf16[32,4096]{1,0:T(8,128)(2,1)S(1)} collective-permute-done((bf16[32,4096]{1,0:T(8,128)(2,1)S(1)}, bf16[32,4096]{1,0:T(8,128)(2,1)S(1)}, u32[]{:S(2)}, u32[]{:S(2)}) %collective-permute-start.4) | collective-permute-done | bytes 262176 | tf_op jit(solution)/shard_map/ppermute | solution.py:524
  45.8 2.0 %collective-permute-start.7 = (bf16[32,4096]{1,0:T(8,128)(2,1)S(1)}, bf16[32,4096]{1,0:T(8,128)(2,1)S(1)}, u32[]{:S(2)}, u32[]{:S(2)}) collective-permute-start(bf16[32,4096]{1,0:T(8,128)(2,1)S(1)} %add_convert_fusion.1), channel_id=1, source_target_pairs={{0,8},{4,12},{8,0},{12,4},{1,9},{5,13},{9,1},{13,5},{2,10},{6,14},... | collective-permute-start | bytes 786440 | tf_op jit(solution)/shard_map/ppermute | solution.py:524
  47.8 0.7 collective-permute-start.8
  48.5 9.7 %shard_map.131 = (bf16[2048,2048]{1,0:T(8,128)(2,1)}, bf16[2048,512]{1,0:T(8,128)(2,1)}, f32[2048,128]{1,0:T(8,128)}, f32[2048,128]{1,0:T(8,128)}, f32[2048,128]{1,0:T(8,128)}, /*index=5*/bf16[512,128]{1,0:T(8,128)(2,1)}) custom-call(s32[32]{0:T(128)} %bitcast.28, bf16[16,144,512]{2,1,0:T(8,128)(2,1)} %all-to-all-done.packed_ref), custom_call_target="tpu_custom_call" | custom-call | flops 64424509440 | bytes 536870912 | tf_op jit(solution)/shard_map/pallas_call | solution.py:492
  58.9 1.4 collective-permute-start.9
  60.3 1.6 collective-permute-start.12
  61.9 1.8 %collective-permute-start.10 = (bf16[32,4096]{1,0:T(8,128)(2,1)S(1)}, bf16[32,4096]{1,0:T(8,128)(2,1)S(1)}, u32[]{:S(2)}, u32[]{:S(2)}) collective-permute-start(bf16[32,4096]{1,0:T(8,128)(2,1)S(1)} %multiply_convert_fusion.refs_0_), channel_id=1, source_target_pairs={{0,12},{4,0},{8,4},{12,8},{1,13},{5,1},{9,5},{13,9},{2,14},{6,2},{... | collective-permute-start | bytes 786440 | tf_op jit(solution)/shard_map/ppermute | solution.py:524
  63.9 2.7 %collective-permute-done.9.refs_1_ = bf16[32,4096]{1,0:T(8,128)(2,1)S(1)} collective-permute-done((bf16[32,4096]{1,0:T(8,128)(2,1)S(1)}, bf16[32,4096]{1,0:T(8,128)(2,1)S(1)}, u32[]{:S(2)}, u32[]{:S(2)}) %collective-permute-start.9) | collective-permute-done | bytes 262176 | tf_op jit(solution)/shard_map/ppermute | solution.py:524
  66.6 1.8 collective-permute-start.11
  68.6 2.4 %collective-permute-done.12.refs_4_ = bf16[32,4096]{1,0:T(8,128)(2,1)S(1)} collective-permute-done((bf16[32,4096]{1,0:T(8,128)(2,1)S(1)}, bf16[32,4096]{1,0:T(8,128)(2,1)S(1)}, u32[]{:S(2)}, u32[]{:S(2)}) %collective-permute-start.12) | collective-permute-done | bytes 262176 | tf_op jit(solution)/shard_map/ppermute | solution.py:524
  71.0 0.8 collective-permute-start.14
  71.8 2.7 %collective-permute-done.10.refs_2_ = bf16[32,4096]{1,0:T(8,128)(2,1)S(1)} collective-permute-done((bf16[32,4096]{1,0:T(8,128)(2,1)S(1)}, bf16[32,4096]{1,0:T(8,128)(2,1)S(1)}, u32[]{:S(2)}, u32[]{:S(2)}) %collective-permute-start.10) | collective-permute-done | bytes 262176 | tf_op jit(solution)/shard_map/ppermute | solution.py:524
  74.5 2.1 %collective-permute-done.13.refs_6_ = bf16[32,4096]{1,0:T(8,128)(2,1)S(1)} collective-permute-done((bf16[32,4096]{1,0:T(8,128)(2,1)S(1)}, bf16[32,4096]{1,0:T(8,128)(2,1)S(1)}, u32[]{:S(2)}, u32[]{:S(2)}) %collective-permute-start.13) | collective-permute-done | bytes 262176 | tf_op jit(solution)/shard_map/ppermute | solution.py:524
  76.6 3.5 %collective-permute-done.11.refs_3_ = bf16[32,4096]{1,0:T(8,128)(2,1)S(1)} collective-permute-done((bf16[32,4096]{1,0:T(8,128)(2,1)S(1)}, bf16[32,4096]{1,0:T(8,128)(2,1)S(1)}, u32[]{:S(2)}, u32[]{:S(2)}) %collective-permute-start.11) | collective-permute-done | bytes 262176 | tf_op jit(solution)/shard_map/ppermute | solution.py:524
  80.0 0.5 collective-permute-start.17
  80.5 0.5 collective-permute-start.19
  81.1 0.4 collective-permute-done.16.refs_8_
  83.8 0.4 collective-permute-done.23.refs_15_
  84.2 5.3 %shard_map.132 = (bf16[512,384]{1,0:T(8,128)(2,1)S(1)}, bf16[512,1024]{1,0:T(8,128)(2,1)}, bf16[256,1024]{1,0:T(8,128)(2,1)}, bf16[256,1024]{1,0:T(8,128)(2,1)}, bf16[256,1024]{1,0:T(8,128)(2,1)}) custom-call(s32[5]{0:T(128)S(1)} %stack.23.place_ref, bf16[32,4096]{1,0:T(8,128)(2,1)S(1)} %multiply_convert_fusion.refs_0_, ...), custom_call_target="tpu_custom_call" | custom-call | flops 1610612736 | bytes 8388608 | tf_op jit(solution)/shard_map/pallas_call | solution.py:581
  89.5 0.7 copy-done.4
  90.3 1.3 collective-permute-start.24
  91.6 2.7 %collective-permute-start.25 = (bf16[256,1024]{1,0:T(8,128)(2,1)}, bf16[256,1024]{1,0:T(8,128)(2,1)}, u32[]{:S(2)}, u32[]{:S(2)}) collective-permute-start(bf16[256,1024]{1,0:T(8,128)(2,1)} %get-tuple-element.95), channel_id=1, source_target_pairs={{0,32},{16,48},{32,0},{48,16},{1,33},{17,49},{33,1},{49,17},{2,34}... | collective-permute-start | bytes 1572872 | tf_op jit(solution)/shard_map/ppermute | solution.py:524
  94.3 1.4 collective-permute-start.26
  95.7 23.2 %shard_map.133 = (bf16[16,144,512]{2,1,0:T(8,128)(2,1)}, bf16[512,384]{1,0:T(8,128)(2,1)}) custom-call(s32[1]{0:T(128)S(6)} %copy.14.length_ref, s32[32]{0:T(128)} %bitcast.29, bf16[512,384]{1,0:T(8,128)(2,1)} %copy-done.4, bf16[512,128]{1,0:T(8,128)(2,1)} %get-tuple-element.98.text_do_ref, bf16[2048,512]{1,0:T(8,128)(2,1)} %get-tuple-element.99.rows_ref, ...), custom_call_target="tpu_custom_call" | custom-call | flops 237565378560 | bytes 536870912 | tf_op jit(solution)/shard_map/pallas_call | solution.py:509
  119.0 4.6 %all-to-all-start.1 = ((bf16[16,144,512]{2,1,0:T(8,128)(2,1)}), bf16[16,144,512]{2,1,0:T(8,128)(2,1)S(1)}, u32[]{:S(2)}, u32[]{:S(2)}) async-start(bf16[16,144,512]{2,1,0:T(8,128)(2,1)} %get-tuple-element.117), calls=%async_computation.1 | async-start | bytes 4718592 | tf_op jit(solution)/shard_map/all_to_all | solution.py:649
  124.2 0.6 collective-permute-start.30
  124.8 2.1 %collective-permute-start.31 = (bf16[512,384]{1,0:T(8,128)(2,1)}, bf16[512,384]{1,0:T(8,128)(2,1)}, u32[]{:S(2)}, u32[]{:S(2)}) collective-permute-start(bf16[512,384]{1,0:T(8,128)(2,1)} %get-tuple-element.112.refs_6_), channel_id=1, source_target_pairs={{0,32},{16,48},{32,0},{48,16},{1,33},{17,49},{33,1},{49,17},{2,34}... | collective-permute-start | bytes 1179656 | tf_op jit(solution)/shard_map/ppermute | solution.py:524
  127.2 1.3 collective-permute-start.32
  128.5 17.1 %collective-permute-done.30.refs_7_ = bf16[512,384]{1,0:T(8,128)(2,1)} collective-permute-done((bf16[512,384]{1,0:T(8,128)(2,1)}, bf16[512,384]{1,0:T(8,128)(2,1)}, u32[]{:S(2)}, u32[]{:S(2)}) %collective-permute-start.30) | collective-permute-done | bytes 393248 | tf_op jit(solution)/shard_map/ppermute | solution.py:524
  145.6 0.6 collective-permute-done.32.refs_9_
  146.2 6.1 %shard_map.134 = (f32[384,256]{1,0:T(8,128)}, bf16[384,256]{1,0:T(8,128)(2,1)}, bf16[384,256]{1,0:T(8,128)(2,1)}, bf16[384,256]{1,0:T(8,128)(2,1)}) custom-call(s32[5]{0:T(128)} %copy-done.3, bf16[512,1024]{1,0:T(8,128)(2,1)} %get-tuple-element.93.kept_ref, bf16[256,1024]{1,0:T(8,128)(2,1)} %collective-permute-done.24.refs_0_, ...), custom_call_target="tpu_custom_call" | custom-call | flops 19327352832 | bytes 8388608 | tf_op jit(solution)/shard_map/pallas_call | solution.py:602
  152.4 3.3 %collective-permute-start.33 = (bf16[384,256]{1,0:T(8,128)(2,1)}, bf16[384,256]{1,0:T(8,128)(2,1)S(1)}, u32[]{:S(2)}, u32[]{:S(2)}) collective-permute-start(bf16[384,256]{1,0:T(8,128)(2,1)} %get-tuple-element.114), channel_id=1, source_target_pairs={{0,64},{64,128},{128,192},{192,0},{1,65},{65,129},{129,193},{193,1... | collective-permute-start | bytes 589832 | tf_op jit(solution)/shard_map/ppermute | solution.py:524
  155.6 4.5 %collective-permute-start.34 = (bf16[384,256]{1,0:T(8,128)(2,1)}, bf16[384,256]{1,0:T(8,128)(2,1)S(1)}, u32[]{:S(2)}, u32[]{:S(2)}) collective-permute-start(bf16[384,256]{1,0:T(8,128)(2,1)} %get-tuple-element.115), channel_id=1, source_target_pairs={{0,128},{64,192},{128,0},{192,64},{1,129},{65,193},{129,1},{193,65... | collective-permute-start | bytes 589832 | tf_op jit(solution)/shard_map/ppermute | solution.py:524
  160.2 2.7 %collective-permute-start.35 = (bf16[384,256]{1,0:T(8,128)(2,1)}, bf16[384,256]{1,0:T(8,128)(2,1)S(1)}, u32[]{:S(2)}, u32[]{:S(2)}) collective-permute-start(bf16[384,256]{1,0:T(8,128)(2,1)} %get-tuple-element.116), channel_id=1, source_target_pairs={{0,192},{64,0},{128,64},{192,128},{1,193},{65,1},{129,65},{193,129... | collective-permute-start | bytes 589832 | tf_op jit(solution)/shard_map/ppermute | solution.py:524
  162.8 1.7 shard_map.135
  164.5 5.4 %collective-permute-done.34.refs_1_ = bf16[384,256]{1,0:T(8,128)(2,1)S(1)} collective-permute-done((bf16[384,256]{1,0:T(8,128)(2,1)}, bf16[384,256]{1,0:T(8,128)(2,1)S(1)}, u32[]{:S(2)}, u32[]{:S(2)}) %collective-permute-start.34) | collective-permute-done | bytes 196640 | tf_op jit(solution)/shard_map/ppermute | solution.py:524
  169.9 8.2 %collective-permute-done.35.refs_2_ = bf16[384,256]{1,0:T(8,128)(2,1)S(1)} collective-permute-done((bf16[384,256]{1,0:T(8,128)(2,1)}, bf16[384,256]{1,0:T(8,128)(2,1)S(1)}, u32[]{:S(2)}, u32[]{:S(2)}) %collective-permute-start.35) | collective-permute-done | bytes 196640 | tf_op jit(solution)/shard_map/ppermute | solution.py:524
  178.1 0.9 shard_map.136
  (62 shorter events, 4.5 us)
Async XLA Ops:
  0.6 4.6 %collective-permute-start.1 = (bf16[256,4096]{1,0:T(8,128)(2,1)}, bf16[256,4096]{1,0:T(8,128)(2,1)}, u32[]{:S(2)}, u32[]{:S(2)}) collective-permute-start(bf16[256,4096]{1,0:T(8,128)(2,1)} %own_weight_ref.1), channel_id=1, source_target_pairs={{0,1},{1,0},{2,3},{3,2},{4,5},{5,4},{6,7},{7,6},{8,9},{9,8},{10,11... | collective-permute-start | bytes 6291464 | tf_op jit(solution)/shard_map/ppermute | solution.py:524
  3.5 8.1 %copy-start.2 = (bf16[1,512,256]{2,1,0:T(8,128)(2,1)S(1)}, bf16[1,512,256]{2,1,0:T(8,128)(2,1)}, u32[]{:S(2)}) copy-start(bf16[1,512,256]{2,1,0:T(8,128)(2,1)} %param.10) | copy-start | bytes 786436
  3.5 9.7 %copy-start = (bf16[256,4096]{1,0:T(8,128)(2,1)S(1)}, bf16[256,4096]{1,0:T(8,128)(2,1)}, u32[]{:S(2)}) copy-start(bf16[256,4096]{1,0:T(8,128)(2,1)} %own_weight_ref.1) | copy-start | bytes 6291460
  5.2 40.6 %all-to-all-start = ((bf16[16,144,512]{2,1,0:T(8,128)(2,1)}), bf16[16,144,512]{2,1,0:T(8,128)(2,1)}, u32[]{:S(2)}, u32[]{:S(2)}) async-start(bf16[16,144,512]{2,1,0:T(8,128)(2,1)} %shard_map.129), calls=%async_computation | async-start | bytes 4718592 | tf_op jit(solution)/shard_map/all_to_all | solution.py:535
  11.6 1.6 collective-permute-start
  11.9 72.2 %copy-start.3 = (s32[5]{0:T(128)}, s32[5]{0:T(128)S(1)}, u32[]{:S(2)}) copy-start(s32[5]{0:T(128)S(1)} %stack.23.place_ref) | copy-start | bytes 64
  17.3 28.1 %collective-permute-start.4 = (bf16[32,4096]{1,0:T(8,128)(2,1)S(1)}, bf16[32,4096]{1,0:T(8,128)(2,1)S(1)}, u32[]{:S(2)}, u32[]{:S(2)}) collective-permute-start(bf16[32,4096]{1,0:T(8,128)(2,1)S(1)} %get-tuple-element.72), channel_id=1, source_target_pairs={{0,2},{2,0},{1,3},{3,1},{4,6},{6,4},{5,7},{7,5},{8,10},{10,8},{9,1... | collective-permute-start | bytes 786440 | tf_op jit(solution)/shard_map/ppermute | solution.py:524
  18.9 26.6 %collective-permute-start.5 = (bf16[32,4096]{1,0:T(8,128)(2,1)S(1)}, bf16[32,4096]{1,0:T(8,128)(2,1)S(1)}, u32[]{:S(2)}, u32[]{:S(2)}) collective-permute-start(bf16[32,4096]{1,0:T(8,128)(2,1)S(1)} %get-tuple-element.74), channel_id=1, source_target_pairs={{0,4},{4,8},{8,12},{12,0},{1,5},{5,9},{9,13},{13,1},{2,6},{6,10},{... | collective-permute-start | bytes 786440 | tf_op jit(solution)/shard_map/ppermute | solution.py:524
  20.4 25.3 %collective-permute-start.6 = (bf16[32,4096]{1,0:T(8,128)(2,1)S(1)}, bf16[32,4096]{1,0:T(8,128)(2,1)S(1)}, u32[]{:S(2)}, u32[]{:S(2)}) collective-permute-start(bf16[32,4096]{1,0:T(8,128)(2,1)S(1)} %get-tuple-element.75), channel_id=1, source_target_pairs={{0,12},{4,0},{8,4},{12,8},{1,13},{5,1},{9,5},{13,9},{2,14},{6,2},{... | collective-permute-start | bytes 786440 | tf_op jit(solution)/shard_map/ppermute | solution.py:524
  20.9 37.4 %collective-permute-start.2 = (bf16[32,4096]{1,0:T(8,128)(2,1)S(1)}, bf16[32,4096]{1,0:T(8,128)(2,1)S(1)}, u32[]{:S(2)}, u32[]{:S(2)}) collective-permute-start(bf16[32,4096]{1,0:T(8,128)(2,1)S(1)} %get-tuple-element.68), channel_id=1, source_target_pairs={{0,4},{4,8},{8,12},{12,0},{1,5},{5,9},{9,13},{13,1},{2,6},{6,10},{... | collective-permute-start | bytes 786440 | tf_op jit(solution)/shard_map/ppermute | solution.py:524
  22.4 35.9 %collective-permute-start.3 = (bf16[32,4096]{1,0:T(8,128)(2,1)S(1)}, bf16[32,4096]{1,0:T(8,128)(2,1)S(1)}, u32[]{:S(2)}, u32[]{:S(2)}) collective-permute-start(bf16[32,4096]{1,0:T(8,128)(2,1)S(1)} %get-tuple-element.69), channel_id=1, source_target_pairs={{0,12},{4,0},{8,4},{12,8},{1,13},{5,1},{9,5},{13,9},{2,14},{6,2},{... | collective-permute-start | bytes 786440 | tf_op jit(solution)/shard_map/ppermute | solution.py:524
  45.8 12.5 %collective-permute-start.7 = (bf16[32,4096]{1,0:T(8,128)(2,1)S(1)}, bf16[32,4096]{1,0:T(8,128)(2,1)S(1)}, u32[]{:S(2)}, u32[]{:S(2)}) collective-permute-start(bf16[32,4096]{1,0:T(8,128)(2,1)S(1)} %add_convert_fusion.1), channel_id=1, source_target_pairs={{0,8},{4,12},{8,0},{12,4},{1,9},{5,13},{9,1},{13,5},{2,10},{6,14},... | collective-permute-start | bytes 786440 | tf_op jit(solution)/shard_map/ppermute | solution.py:524
  47.8 10.5 %collective-permute-start.8 = (bf16[32,4096]{1,0:T(8,128)(2,1)S(1)}, bf16[32,4096]{1,0:T(8,128)(2,1)S(1)}, u32[]{:S(2)}, u32[]{:S(2)}) collective-permute-start(bf16[32,4096]{1,0:T(8,128)(2,1)S(1)} %add_convert_fusion), channel_id=1, source_target_pairs={{0,2},{2,0},{1,3},{3,1},{4,6},{6,4},{5,7},{7,5},{8,10},{10,8},{9,1... | collective-permute-start | bytes 786440 | tf_op jit(solution)/shard_map/ppermute | solution.py:524
  48.5 9.8 %copy-start.5 = (bf16[1,32,4096]{2,1,0:T(8,128)(2,1)S(1)}, bf16[1,32,4096]{2,1,0:T(8,128)(2,1)}, u32[]{:S(2)}) copy-start(bf16[1,32,4096]{2,1,0:T(8,128)(2,1)} %param.11) | copy-start | bytes 786436
  48.5 10.1 %copy-start.6 = (f32[4096]{0:T(1024)S(1)}, f32[4096]{0:T(1024)}, u32[]{:S(2)}) copy-start(f32[4096]{0:T(1024)} %param.13) | copy-start | bytes 49156
  58.9 7.7 %collective-permute-start.9 = (bf16[32,4096]{1,0:T(8,128)(2,1)S(1)}, bf16[32,4096]{1,0:T(8,128)(2,1)S(1)}, u32[]{:S(2)}, u32[]{:S(2)}) collective-permute-start(bf16[32,4096]{1,0:T(8,128)(2,1)S(1)} %multiply_convert_fusion.refs_0_), channel_id=1, source_target_pairs={{0,2},{2,0},{1,3},{3,1},{4,6},{6,4},{5,7},{7,5},{8,10},{10,8},{9,1... | collective-permute-start | bytes 786440 | tf_op jit(solution)/shard_map/ppermute | solution.py:524
  60.3 10.7 %collective-permute-start.12 = (bf16[32,4096]{1,0:T(8,128)(2,1)S(1)}, bf16[32,4096]{1,0:T(8,128)(2,1)S(1)}, u32[]{:S(2)}, u32[]{:S(2)}) collective-permute-start(bf16[32,4096]{1,0:T(8,128)(2,1)S(1)} %multiply_convert_fusion.refs_0_), channel_id=1, source_target_pairs={{0,8},{4,12},{8,0},{12,4},{1,9},{5,13},{9,1},{13,5},{2,10},{6,14},... | collective-permute-start | bytes 786440 | tf_op jit(solution)/shard_map/ppermute | solution.py:524
  61.9 12.6 %collective-permute-start.10 = (bf16[32,4096]{1,0:T(8,128)(2,1)S(1)}, bf16[32,4096]{1,0:T(8,128)(2,1)S(1)}, u32[]{:S(2)}, u32[]{:S(2)}) collective-permute-start(bf16[32,4096]{1,0:T(8,128)(2,1)S(1)} %multiply_convert_fusion.refs_0_), channel_id=1, source_target_pairs={{0,12},{4,0},{8,4},{12,8},{1,13},{5,1},{9,5},{13,9},{2,14},{6,2},{... | collective-permute-start | bytes 786440 | tf_op jit(solution)/shard_map/ppermute | solution.py:524
  63.7 12.9 %collective-permute-start.13 = (bf16[32,4096]{1,0:T(8,128)(2,1)S(1)}, bf16[32,4096]{1,0:T(8,128)(2,1)S(1)}, u32[]{:S(2)}, u32[]{:S(2)}) collective-permute-start(bf16[32,4096]{1,0:T(8,128)(2,1)S(1)} %multiply_convert_fusion.refs_0_), channel_id=1, source_target_pairs={{0,4},{4,8},{8,12},{12,0},{1,5},{5,9},{9,13},{13,1},{2,6},{6,10},{... | collective-permute-start | bytes 786440 | tf_op jit(solution)/shard_map/ppermute | solution.py:524
  66.6 13.4 %collective-permute-start.11 = (bf16[32,4096]{1,0:T(8,128)(2,1)S(1)}, bf16[32,4096]{1,0:T(8,128)(2,1)S(1)}, u32[]{:S(2)}, u32[]{:S(2)}) collective-permute-start(bf16[32,4096]{1,0:T(8,128)(2,1)S(1)} %collective-permute-done.9.refs_1_), channel_id=1, source_target_pairs={{0,12},{4,0},{8,4},{12,8},{1,13},{5,1},{9,5},{13,9},{2,14},{6,2},{... | collective-permute-start | bytes 786440 | tf_op jit(solution)/shard_map/ppermute | solution.py:524
  68.4 12.6 %collective-permute-start.15 = (bf16[32,4096]{1,0:T(8,128)(2,1)S(1)}, bf16[32,4096]{1,0:T(8,128)(2,1)S(1)}, u32[]{:S(2)}, u32[]{:S(2)}) collective-permute-start(bf16[32,4096]{1,0:T(8,128)(2,1)S(1)} %collective-permute-done.9.refs_1_), channel_id=1, source_target_pairs={{0,4},{4,8},{8,12},{12,0},{1,5},{5,9},{9,13},{13,1},{2,6},{6,10},{... | collective-permute-start | bytes 786440 | tf_op jit(solution)/shard_map/ppermute | solution.py:524
  71.0 9.5 %collective-permute-start.14 = (bf16[32,4096]{1,0:T(8,128)(2,1)S(1)}, bf16[32,4096]{1,0:T(8,128)(2,1)S(1)}, u32[]{:S(2)}, u32[]{:S(2)}) collective-permute-start(bf16[32,4096]{1,0:T(8,128)(2,1)S(1)} %collective-permute-done.12.refs_4_), channel_id=1, source_target_pairs={{0,2},{2,0},{1,3},{3,1},{4,6},{6,4},{5,7},{7,5},{8,10},{10,8},{9,1... | collective-permute-start | bytes 786440 | tf_op jit(solution)/shard_map/ppermute | solution.py:524
  80.0 1.5 collective-permute-start.16
  80.0 1.9 %collective-permute-start.17 = (bf16[32,4096]{1,0:T(8,128)(2,1)S(1)}, bf16[32,4096]{1,0:T(8,128)(2,1)S(1)}, u32[]{:S(2)}, u32[]{:S(2)}) collective-permute-start(bf16[32,4096]{1,0:T(8,128)(2,1)S(1)} %collective-permute-done.9.refs_1_), channel_id=1, source_target_pairs={{0,1},{1,0},{2,3},{3,2},{4,5},{5,4},{6,7},{7,6},{8,9},{9,8},{10,11... | collective-permute-start | bytes 786440 | tf_op jit(solution)/shard_map/ppermute | solution.py:524
  80.5 1.8 collective-permute-start.18
  80.5 2.5 %collective-permute-start.19 = (bf16[32,4096]{1,0:T(8,128)(2,1)S(1)}, bf16[32,4096]{1,0:T(8,128)(2,1)S(1)}, u32[]{:S(2)}, u32[]{:S(2)}) collective-permute-start(bf16[32,4096]{1,0:T(8,128)(2,1)S(1)} %collective-permute-done.11.refs_3_), channel_id=1, source_target_pairs={{0,1},{1,0},{2,3},{3,2},{4,5},{5,4},{6,7},{7,6},{8,9},{9,8},{10,11... | collective-permute-start | bytes 786440 | tf_op jit(solution)/shard_map/ppermute | solution.py:524
  81.0 2.1 %collective-permute-start.20 = (bf16[32,4096]{1,0:T(8,128)(2,1)S(1)}, bf16[32,4096]{1,0:T(8,128)(2,1)S(1)}, u32[]{:S(2)}, u32[]{:S(2)}) collective-permute-start(bf16[32,4096]{1,0:T(8,128)(2,1)S(1)} %collective-permute-done.12.refs_4_), channel_id=1, source_target_pairs={{0,1},{1,0},{2,3},{3,2},{4,5},{5,4},{6,7},{7,6},{8,9},{9,8},{10,11... | collective-permute-start | bytes 786440 | tf_op jit(solution)/shard_map/ppermute | solution.py:524
  81.6 1.9 %collective-permute-start.22 = (bf16[32,4096]{1,0:T(8,128)(2,1)S(1)}, bf16[32,4096]{1,0:T(8,128)(2,1)S(1)}, u32[]{:S(2)}, u32[]{:S(2)}) collective-permute-start(bf16[32,4096]{1,0:T(8,128)(2,1)S(1)} %collective-permute-done.13.refs_6_), channel_id=1, source_target_pairs={{0,1},{1,0},{2,3},{3,2},{4,5},{5,4},{6,7},{7,6},{8,9},{9,8},{10,11... | collective-permute-start | bytes 786440 | tf_op jit(solution)/shard_map/ppermute | solution.py:524
  81.9 1.9 %collective-permute-start.21 = (bf16[32,4096]{1,0:T(8,128)(2,1)S(1)}, bf16[32,4096]{1,0:T(8,128)(2,1)S(1)}, u32[]{:S(2)}, u32[]{:S(2)}) collective-permute-start(bf16[32,4096]{1,0:T(8,128)(2,1)S(1)} %collective-permute-done.14.refs_5_), channel_id=1, source_target_pairs={{0,1},{1,0},{2,3},{3,2},{4,5},{5,4},{6,7},{7,6},{8,9},{9,8},{10,11... | collective-permute-start | bytes 786440 | tf_op jit(solution)/shard_map/ppermute | solution.py:524
  82.3 1.9 %collective-permute-start.23 = (bf16[32,4096]{1,0:T(8,128)(2,1)S(1)}, bf16[32,4096]{1,0:T(8,128)(2,1)S(1)}, u32[]{:S(2)}, u32[]{:S(2)}) collective-permute-start(bf16[32,4096]{1,0:T(8,128)(2,1)S(1)} %collective-permute-done.15.refs_7_), channel_id=1, source_target_pairs={{0,1},{1,0},{2,3},{3,2},{4,5},{5,4},{6,7},{7,6},{8,9},{9,8},{10,11... | collective-permute-start | bytes 786440 | tf_op jit(solution)/shard_map/ppermute | solution.py:524
  89.5 0.7 copy-start.4
  90.3 28.7 %collective-permute-start.24 = (bf16[256,1024]{1,0:T(8,128)(2,1)}, bf16[256,1024]{1,0:T(8,128)(2,1)}, u32[]{:S(2)}, u32[]{:S(2)}) collective-permute-start(bf16[256,1024]{1,0:T(8,128)(2,1)} %get-tuple-element.94), channel_id=1, source_target_pairs={{0,16},{16,32},{32,48},{48,0},{1,17},{17,33},{33,49},{49,1},{2,18}... | collective-permute-start | bytes 1572872 | tf_op jit(solution)/shard_map/ppermute | solution.py:524
  91.6 27.4 %collective-permute-start.25 = (bf16[256,1024]{1,0:T(8,128)(2,1)}, bf16[256,1024]{1,0:T(8,128)(2,1)}, u32[]{:S(2)}, u32[]{:S(2)}) collective-permute-start(bf16[256,1024]{1,0:T(8,128)(2,1)} %get-tuple-element.95), channel_id=1, source_target_pairs={{0,32},{16,48},{32,0},{48,16},{1,33},{17,49},{33,1},{49,17},{2,34}... | collective-permute-start | bytes 1572872 | tf_op jit(solution)/shard_map/ppermute | solution.py:524
  94.3 24.7 %collective-permute-start.26 = (bf16[256,1024]{1,0:T(8,128)(2,1)}, bf16[256,1024]{1,0:T(8,128)(2,1)}, u32[]{:S(2)}, u32[]{:S(2)}) collective-permute-start(bf16[256,1024]{1,0:T(8,128)(2,1)} %get-tuple-element.96), channel_id=1, source_target_pairs={{0,48},{16,0},{32,16},{48,32},{1,49},{17,1},{33,17},{49,33},{2,50}... | collective-permute-start | bytes 1572872 | tf_op jit(solution)/shard_map/ppermute | solution.py:524
  119.0 43.8 %all-to-all-start.1 = ((bf16[16,144,512]{2,1,0:T(8,128)(2,1)}), bf16[16,144,512]{2,1,0:T(8,128)(2,1)S(1)}, u32[]{:S(2)}, u32[]{:S(2)}) async-start(bf16[16,144,512]{2,1,0:T(8,128)(2,1)} %get-tuple-element.117), calls=%async_computation.1 | async-start | bytes 4718592 | tf_op jit(solution)/shard_map/all_to_all | solution.py:649
  123.6 3.3 %collective-permute-start.27 = (bf16[256,1024]{1,0:T(8,128)(2,1)}, bf16[256,1024]{1,0:T(8,128)(2,1)S(1)}, u32[]{:S(2)}, u32[]{:S(2)}) collective-permute-start(bf16[256,1024]{1,0:T(8,128)(2,1)} %collective-permute-done.24.refs_0_), channel_id=1, source_target_pairs={{0,1},{1,0},{2,3},{3,2},{4,5},{5,4},{6,7},{7,6},{8,9},{9,8},{10,11... | collective-permute-start | bytes 1572872 | tf_op jit(solution)/shard_map/ppermute | solution.py:524
  123.7 3.2 %collective-permute-start.28 = (bf16[256,1024]{1,0:T(8,128)(2,1)}, bf16[256,1024]{1,0:T(8,128)(2,1)S(1)}, u32[]{:S(2)}, u32[]{:S(2)}) collective-permute-start(bf16[256,1024]{1,0:T(8,128)(2,1)} %collective-permute-done.25.refs_1_), channel_id=1, source_target_pairs={{0,1},{1,0},{2,3},{3,2},{4,5},{5,4},{6,7},{7,6},{8,9},{9,8},{10,11... | collective-permute-start | bytes 1572872 | tf_op jit(solution)/shard_map/ppermute | solution.py:524
  124.1 3.1 %collective-permute-start.29 = (bf16[256,1024]{1,0:T(8,128)(2,1)}, bf16[256,1024]{1,0:T(8,128)(2,1)S(1)}, u32[]{:S(2)}, u32[]{:S(2)}) collective-permute-start(bf16[256,1024]{1,0:T(8,128)(2,1)} %collective-permute-done.26.refs_2_), channel_id=1, source_target_pairs={{0,1},{1,0},{2,3},{3,2},{4,5},{5,4},{6,7},{7,6},{8,9},{9,8},{10,11... | collective-permute-start | bytes 1572872 | tf_op jit(solution)/shard_map/ppermute | solution.py:524
  124.2 21.3 %collective-permute-start.30 = (bf16[512,384]{1,0:T(8,128)(2,1)}, bf16[512,384]{1,0:T(8,128)(2,1)}, u32[]{:S(2)}, u32[]{:S(2)}) collective-permute-start(bf16[512,384]{1,0:T(8,128)(2,1)} %get-tuple-element.112.refs_6_), channel_id=1, source_target_pairs={{0,16},{16,32},{32,48},{48,0},{1,17},{17,33},{33,49},{49,1},{2,18}... | collective-permute-start | bytes 1179656 | tf_op jit(solution)/shard_map/ppermute | solution.py:524
  124.8 20.7 %collective-permute-start.31 = (bf16[512,384]{1,0:T(8,128)(2,1)}, bf16[512,384]{1,0:T(8,128)(2,1)}, u32[]{:S(2)}, u32[]{:S(2)}) collective-permute-start(bf16[512,384]{1,0:T(8,128)(2,1)} %get-tuple-element.112.refs_6_), channel_id=1, source_target_pairs={{0,32},{16,48},{32,0},{48,16},{1,33},{17,49},{33,1},{49,17},{2,34}... | collective-permute-start | bytes 1179656 | tf_op jit(solution)/shard_map/ppermute | solution.py:524
  126.9 19.3 %copy-start.7 = (bf16[256,1024]{1,0:T(8,128)(2,1)}, bf16[256,1024]{1,0:T(8,128)(2,1)S(1)}, u32[]{:S(2)}) copy-start(bf16[256,1024]{1,0:T(8,128)(2,1)S(1)} %collective-permute-done.27.refs_3_) | copy-start | bytes 1572868
  126.9 19.3 %copy-start.8 = (bf16[256,1024]{1,0:T(8,128)(2,1)}, bf16[256,1024]{1,0:T(8,128)(2,1)S(1)}, u32[]{:S(2)}) copy-start(bf16[256,1024]{1,0:T(8,128)(2,1)S(1)} %collective-permute-done.28.refs_4_) | copy-start | bytes 1572868
  127.2 19.0 %copy-start.9 = (bf16[256,1024]{1,0:T(8,128)(2,1)}, bf16[256,1024]{1,0:T(8,128)(2,1)S(1)}, u32[]{:S(2)}) copy-start(bf16[256,1024]{1,0:T(8,128)(2,1)S(1)} %collective-permute-done.29.refs_5_) | copy-start | bytes 1572868
  127.2 19.0 %collective-permute-start.32 = (bf16[512,384]{1,0:T(8,128)(2,1)}, bf16[512,384]{1,0:T(8,128)(2,1)}, u32[]{:S(2)}, u32[]{:S(2)}) collective-permute-start(bf16[512,384]{1,0:T(8,128)(2,1)} %get-tuple-element.112.refs_6_), channel_id=1, source_target_pairs={{0,48},{16,0},{32,16},{48,32},{1,49},{17,1},{33,17},{49,33},{2,50}... | collective-permute-start | bytes 1179656 | tf_op jit(solution)/shard_map/ppermute | solution.py:524
  152.4 25.7 %copy-start.1 = (f32[384,256]{1,0:T(8,128)S(1)}, f32[384,256]{1,0:T(8,128)}, u32[]{:S(2)}) copy-start(f32[384,256]{1,0:T(8,128)} %get-tuple-element.124.kept_ref) | copy-start | bytes 1179652
  152.4 12.1 %collective-permute-start.33 = (bf16[384,256]{1,0:T(8,128)(2,1)}, bf16[384,256]{1,0:T(8,128)(2,1)S(1)}, u32[]{:S(2)}, u32[]{:S(2)}) collective-permute-start(bf16[384,256]{1,0:T(8,128)(2,1)} %get-tuple-element.114), channel_id=1, source_target_pairs={{0,64},{64,128},{128,192},{192,0},{1,65},{65,129},{129,193},{193,1... | collective-permute-start | bytes 589832 | tf_op jit(solution)/shard_map/ppermute | solution.py:524
  155.6 14.2 %collective-permute-start.34 = (bf16[384,256]{1,0:T(8,128)(2,1)}, bf16[384,256]{1,0:T(8,128)(2,1)S(1)}, u32[]{:S(2)}, u32[]{:S(2)}) collective-permute-start(bf16[384,256]{1,0:T(8,128)(2,1)} %get-tuple-element.115), channel_id=1, source_target_pairs={{0,128},{64,192},{128,0},{192,64},{1,129},{65,193},{129,1},{193,65... | collective-permute-start | bytes 589832 | tf_op jit(solution)/shard_map/ppermute | solution.py:524
  160.2 17.9 %collective-permute-start.35 = (bf16[384,256]{1,0:T(8,128)(2,1)}, bf16[384,256]{1,0:T(8,128)(2,1)S(1)}, u32[]{:S(2)}, u32[]{:S(2)}) collective-permute-start(bf16[384,256]{1,0:T(8,128)(2,1)} %get-tuple-element.116), channel_id=1, source_target_pairs={{0,192},{64,0},{128,64},{192,128},{1,193},{65,1},{129,65},{193,129... | collective-permute-start | bytes 589832 | tf_op jit(solution)/shard_map/ppermute | solution.py:524
where the time goes:
time: 180 us; the launch traced here: 179 us
  waiting for transfers between devices  72.5 us (40%)
  Pallas kernels  53.8 us (30%)
  starting transfers between devices  49.5 us (28%)
    ppermute x36, waiting for transfers between devices, shift(): lax.ppermute(rows, axis, [(i, (i + step) % size) for i in range(size)])  72.5 us
    ppermute x36, starting transfers between devices, shift(): lax.ppermute(rows, axis, [(i, (i + step) % size) for i in range(size)])  38.5 us
    pallas_call x1, Pallas kernels, attention(): grid_call(attention_kernel, 1 + IMAGE // FORWARD_ROWS, [IN_SMEM, IN_SMEM,...  23.2 us
    pallas_call x1, Pallas kernels, image_forward(): grid_call(image_forward_kernel, IMAGE // FORWARD_ROWS, [IN_SMEM, fixed(HE...  9.74 us
    all_to_all x1, starting transfers between devices, encode(): lax.all_to_all(packed, SEQ, split_axis=0, concat_axis=0, tiled=True)  6.4 us
    pallas_call x1, Pallas kernels, weight_sums(): whole_call(weight_kernel, [total] + [rows_of(columns, FEATURES)] * 3, 1,...  6.15 us
    pallas_call x1, Pallas kernels, project(): pl.pallas_call(text_kernel, out_shape=[rows_of(PROMPT, columns), rows_of(...  5.32 us
    all_to_all x1, starting transfers between devices, on_device(): lax.all_to_all(sent, SEQ, split_axis=0, concat_axis=0, tiled=True)  4.57 us
  transfers between devices with their start and end apart: 38, of which 20 were waited for; matrix products, arithmetic and copies ran while one was open for 0% of the time, Pallas kernels for 27%

commit v1 on v0

--- a/solution.py
+++ b/solution.py
@@ -25,7 +25,8 @@
 FEATURES = WIDTH // HEADS
 TEXT_SHARE = PROMPT // HEADS
 HALF_PROMPT = PROMPT // 2
-TEXT_DEPTH = 1024
+TEXT_DEPTH = 512
+LATE_COST = 12
 CHIPS = [(ahead, across) for ahead in range(4) for across in range(2)]
 
 BF16 = jnp.bfloat16
@@ -200,17 +201,39 @@
         store.wait()
 
 
-def weight_kernel(place_ref, kept_ref, *refs):
-    near_refs, far_refs, grad_refs = refs[:3], refs[3:6], refs[6:10]
-    kept_sum_ref, sent_refs, totals_ref = refs[10], refs[11:14], refs[14]
+def half_rows(place_ref):
     near = pl.ds(pl.multiple_of(place_ref[2] * HALF_PROMPT, HALF_PROMPT), HALF_PROMPT)
     far = pl.ds(pl.multiple_of((1 - place_ref[2]) * HALF_PROMPT, HALF_PROMPT), HALF_PROMPT)
+    return near, far
+
+
+def feature_block(place_ref, ahead):
+    z_hi = lax.rem(place_ref[3] + ahead, 4)
+    return pl.ds(pl.multiple_of(z_hi * FEATURES, FEATURES), FEATURES)
+
+
+def early_weight_kernel(place_ref, kept_ref, near_ref, far_ref, own_ref, grad_ref, totals_ref):
+    near, far = half_rows(place_ref)
 
     def body(ahead, carry):
-        z_hi = lax.rem(place_ref[3] + ahead, 4)
-        at = pl.ds(pl.multiple_of(z_hi * FEATURES, FEATURES), FEATURES)
-        total = matmul(grad_refs[0][...], kept_ref[:, at], CONTRACT_FIRST)
-        for grad_ref, near_ref, far_ref in zip(grad_refs[1:], near_refs, far_refs):
+        at = feature_block(place_ref, ahead)
+        total = matmul(own_ref[...], kept_ref[:, at], CONTRACT_FIRST)
+        total += matmul(grad_ref[near, :], near_ref[:, at], CONTRACT_FIRST)
+        totals_ref[ahead] = total + matmul(grad_ref[far, :], far_ref[:, at], CONTRACT_FIRST)
+        return carry
+
+    lax.fori_loop(0, 4, body, 0)
+
+
+def late_weight_kernel(place_ref, early_ref, *refs):
+    near_refs, far_refs, grad_refs = refs[:2], refs[2:4], refs[4:6]
+    kept_sum_ref, sent_refs, totals_ref = refs[6], refs[7:10], refs[10]
+    near, far = half_rows(place_ref)
+
+    def body(ahead, carry):
+        at = feature_block(place_ref, ahead)
+        total = early_ref[ahead]
+        for grad_ref, near_ref, far_ref in zip(grad_refs, near_refs, far_refs):
             total += matmul(grad_ref[near, :], near_ref[:, at], CONTRACT_FIRST)
             total += matmul(grad_ref[far, :], far_ref[:, at], CONTRACT_FIRST)
         totals_ref[ahead] = total
@@ -460,7 +483,7 @@
             store.wait()
 
 
-def grid_call(kernel, steps, in_specs, out_shape, out_specs, scratch, products):
+def grid_call(kernel, steps, in_specs, out_shape, out_specs, scratch, products, limit):
     return pl.pallas_call(
         kernel,
         grid=(steps,),
@@ -468,7 +491,7 @@
         in_specs=in_specs,
         out_specs=out_specs,
         scratch_shapes=scratch,
-        compiler_params=pltpu.CompilerParams(vmem_limit_bytes=WHOLE_VMEM),
+        compiler_params=pltpu.CompilerParams(vmem_limit_bytes=limit),
         cost_estimate=pl.CostEstimate(
             flops=60 * products * HEAD_DIM, bytes_accessed=2**29, transcendentals=0
         ),
@@ -499,6 +522,7 @@
         + [fixed(PROMPT, HEAD_DIM)],
         [pltpu.VMEM((IMAGE, HEAD_DIM), BF16), pltpu.VMEM((IMAGE, 2 * HEAD_DIM), BF16)],
         2 * IMAGE * IMAGE,
+        WHOLE_VMEM,
     )(order, packed)
 
 
@@ -516,6 +540,7 @@
         [pltpu.VMEM((HEADS, PACK_ROWS, PACK_COLS), BF16), text_sum, text_sum, image_sum, image_sum]
         + [pltpu.VMEM((PROMPT, 2 * HEAD_DIM), BF16), pltpu.SemaphoreType.DMA((4,))],
         6 * TOTAL * TOTAL - 2 * IMAGE * IMAGE,
+        WHOLE_VMEM,
     )(length, order, text_rows, text_do, rows, weights, output, maximum, total)
 
 
@@ -531,7 +556,6 @@
 def encode(place, context, residual, weight, gain, packed, order):
     other_weight = shift(weight, "core", 1)
     other = shift(context, "core", 1)
-    other_weight, packed = lax.optimization_barrier((other_weight, packed))
     packed = lax.all_to_all(packed, SEQ, split_axis=0, concat_axis=0, tiled=True)
     chunks = whole_call(
         partial_kernel,
@@ -598,18 +622,25 @@
 
 def weight_sums(place, kept, near, far, grads):
     columns = grads[0].shape[1]
-    total = jax.ShapeDtypeStruct((columns, FEATURES), F32)
+    half = 4 * PROMPT * 4 * FEATURES * columns
+    totals = jax.ShapeDtypeStruct((4, columns, FEATURES), F32)
+    early = whole_call(early_weight_kernel, totals, 1, 5, [], half, 2**22, WHOLE_VMEM)(
+        place, kept, near[0], far[0], grads[0], grads[1]
+    )
     kept_sum, *sent = whole_call(
-        weight_kernel,
-        [total] + [rows_of(columns, FEATURES)] * 3,
+        late_weight_kernel,
+        [jax.ShapeDtypeStruct((columns, FEATURES), F32)] + [rows_of(columns, FEATURES)] * 3,
         1,
-        11,
+        7,
         [pltpu.VMEM((4, columns, FEATURES), F32)],
-        12 * 2 * 4 * PROMPT * 4 * FEATURES * columns,
-        2**23,
+        LATE_COST * half,
+        2**22,
         WHOLE_VMEM,
-    )(place, kept, *near, *far, *grads)
-    return [kept_sum] + [shift(rows, "z_hi", step + 1) for step, rows in enumerate(sent)]
+    )(place, early, *near[1:], *far[1:], *grads[2:])
+    parts = [None] * 3
+    for step in (2, 1, 3):
+        parts[step - 1] = shift(sent[step - 1], "z_hi", step)
+    return [kept_sum] + parts
 
 
 def weight_total(kept_sum, *parts):

time: 180 us -> 183 us (1.017)
  Pallas kernels: 53.8 us -> 57.8 us
  waiting for transfers between devices: 72.5 us -> 69.9 us
    pallas_call x1 -> x2, Pallas kernels: 6.15 us -> 9.46 us  [the longest x1 4.88 us: weight_sums(): whole_call(late_weight_kernel, [jax.ShapeDtypeStruct((columns, FEATURES),...]
    ppermute x36, waiting for transfers between devices: 72.5 us -> 69.9 us  [shift(): lax.ppermute(rows, axis, [(i, (i + step) % size) for i in range(size)])]
  transfers between devices with their start and end apart: 38 -> 38, of which waited for: 20 -> 19; matrix products, arithmetic and copies ran while one was open for 0% -> 0% of each run, Pallas kernels for 27% -> 26%
where the time goes in v1:
time: 183 us; the launch traced here: 182 us
  waiting for transfers between devices  69.9 us (38%)
  Pallas kernels  57.8 us (32%)
  starting transfers between devices  49.9 us (27%)
  local copies, waits for them, and re-layouts  2.35 us (1%)
    ppermute x36, waiting for transfers between devices, shift(): lax.ppermute(rows, axis, [(i, (i + step) % size) for i in range(size)])  69.9 us
    ppermute x36, starting transfers between devices, shift(): lax.ppermute(rows, axis, [(i, (i + step) % size) for i in range(size)])  38.7 us
    pallas_call x1, Pallas kernels, attention(): grid_call(attention_kernel, 1 + IMAGE // FORWARD_ROWS, [IN_SMEM, IN_SMEM,...  23.2 us
    pallas_call x1, Pallas kernels, image_forward(): grid_call(image_forward_kernel, IMAGE // FORWARD_ROWS, [IN_SMEM, fixed(HE...  9.67 us
    all_to_all x1, starting transfers between devices, encode(): lax.all_to_all(packed, SEQ, split_axis=0, concat_axis=0, tiled=True)  6.52 us
    pallas_call x1, Pallas kernels, project(): pl.pallas_call(text_kernel, out_shape=[rows_of(PROMPT, columns), rows_of(...  6 us
    pallas_call x1, Pallas kernels, weight_sums(): whole_call(late_weight_kernel, [jax.ShapeDtypeStruct((columns, FEATURES),...  4.88 us
    all_to_all x1, starting transfers between devices, on_device(): lax.all_to_all(sent, SEQ, split_axis=0, concat_axis=0, tiled=True)  4.7 us
  transfers between devices with their start and end apart: 38, of which 19 were waited for; matrix products, arithmetic and copies ran while one was open for 0% of the time, Pallas kernels for 26%

profile of v1, /device:TPU:8, one launch (start us, length us, event | category | flops | bytes accessed | tf_op | source)
XLA Modules:
  0.0 182.2 jit_solution(6281827712026641957)
XLA Ops:
  0.6 2.8 %shard_map.130 = bf16[16,144,512]{2,1,0:T(8,128)(2,1)} custom-call(bf16[128,6144]{1,0:T(8,128)(2,1)} %bitcast.22, bf16[128,2048]{1,0:T(8,128)(2,1)} %bitcast.23, bf16[32,2048]{1,0:T(8,128)(2,1)} %bitcast.24), custom_call_target="tpu_custom_call" | custom-call | bytes 4194304 | tf_op jit(solution)/shard_map/pallas_call | solution.py:114
  3.4 6.5 %all-to-all-start = ((bf16[16,144,512]{2,1,0:T(8,128)(2,1)}), bf16[16,144,512]{2,1,0:T(8,128)(2,1)}, u32[]{:S(2)}, u32[]{:S(2)}) async-start(bf16[16,144,512]{2,1,0:T(8,128)(2,1)} %shard_map.130), calls=%async_computation | async-start | bytes 4718592 | tf_op jit(solution)/shard_map/all_to_all | solution.py:559
  10.6 3.7 %collective-permute-done.other_ref = bf16[512,256]{1,0:T(8,128)(2,1)S(1)} collective-permute-done((bf16[512,256]{1,0:T(8,128)(2,1)S(1)}, bf16[512,256]{1,0:T(8,128)(2,1)S(1)}, u32[]{:S(2)}, u32[]{:S(2)}) %collective-permute-start) | collective-permute-done | bytes 262176 | tf_op jit(solution)/shard_map/ppermute | solution.py:549
  14.7 4.1 %shard_map.129 = (bf16[32,4096]{1,0:T(8,128)(2,1)S(1)}, bf16[32,4096]{1,0:T(8,128)(2,1)S(1)}, bf16[32,4096]{1,0:T(8,128)(2,1)S(1)}, bf16[32,4096]{1,0:T(8,128)(2...) custom-call(s32[5]{0:T(128)S(1)} %stack.23.place_ref, ...), custom_call_target="tpu_custom_call" | custom-call | flops 1073741824 | bytes 8388608 | tf_op jit(solution)/shard_map/pallas_call | solution.py:560
  18.8 1.6 collective-permute-start.4
  20.3 1.5 collective-permute-start.5
  21.8 0.5 collective-permute-start.6
  22.4 1.5 collective-permute-start.2
  23.9 0.5 collective-permute-start.3
  24.4 19.4 %collective-permute-done.4 = bf16[32,4096]{1,0:T(8,128)(2,1)S(1)} collective-permute-done((bf16[32,4096]{1,0:T(8,128)(2,1)S(1)}, bf16[32,4096]{1,0:T(8,128)(2,1)S(1)}, u32[]{:S(2)}, u32[]{:S(2)}) %collective-permute-start.4) | collective-permute-done | bytes 262176 | tf_op jit(solution)/shard_map/ppermute | solution.py:549
  44.1 2.0 %collective-permute-start.7 = (bf16[32,4096]{1,0:T(8,128)(2,1)S(1)}, bf16[32,4096]{1,0:T(8,128)(2,1)S(1)}, u32[]{:S(2)}, u32[]{:S(2)}) collective-permute-start(bf16[32,4096]{1,0:T(8,128)(2,1)S(1)} %add_convert_fusion.1), channel_id=1, source_target_pairs={{0,8},{4,12},{8,0},{12,4},{1,9},{5,13},{9,1},{13,5},{2,10},{6,14},... | collective-permute-start | bytes 786440 | tf_op jit(solution)/shard_map/ppermute | solution.py:549
  46.1 0.7 collective-permute-start.8
  46.8 9.7 %shard_map.131 = (bf16[2048,2048]{1,0:T(8,128)(2,1)}, bf16[2048,512]{1,0:T(8,128)(2,1)}, f32[2048,128]{1,0:T(8,128)}, f32[2048,128]{1,0:T(8,128)}, f32[2048,128]{1,0:T(8,128)}, /*index=5*/bf16[512,128]{1,0:T(8,128)(2,1)}) custom-call(s32[32]{0:T(128)} %bitcast.28, bf16[16,144,512]{2,1,0:T(8,128)(2,1)} %all-to-all-done.packed_ref), custom_call_target="tpu_custom_call" | custom-call | flops 64424509440 | bytes 536870912 | tf_op jit(solution)/shard_map/pallas_call | solution.py:515
  57.2 1.4 collective-permute-start.9
  58.6 1.6 collective-permute-start.12
  60.2 1.8 collective-permute-start.10
  62.2 2.7 %collective-permute-done.9.refs_1_ = bf16[32,4096]{1,0:T(8,128)(2,1)S(1)} collective-permute-done((bf16[32,4096]{1,0:T(8,128)(2,1)S(1)}, bf16[32,4096]{1,0:T(8,128)(2,1)S(1)}, u32[]{:S(2)}, u32[]{:S(2)}) %collective-permute-start.9) | collective-permute-done | bytes 262176 | tf_op jit(solution)/shard_map/ppermute | solution.py:549
  64.9 1.8 collective-permute-start.11
  66.9 2.4 %collective-permute-done.12.refs_4_ = bf16[32,4096]{1,0:T(8,128)(2,1)S(1)} collective-permute-done((bf16[32,4096]{1,0:T(8,128)(2,1)S(1)}, bf16[32,4096]{1,0:T(8,128)(2,1)S(1)}, u32[]{:S(2)}, u32[]{:S(2)}) %collective-permute-start.12) | collective-permute-done | bytes 262176 | tf_op jit(solution)/shard_map/ppermute | solution.py:549
  69.3 0.7 collective-permute-start.14
  70.0 2.8 %collective-permute-done.10.refs_2_ = bf16[32,4096]{1,0:T(8,128)(2,1)S(1)} collective-permute-done((bf16[32,4096]{1,0:T(8,128)(2,1)S(1)}, bf16[32,4096]{1,0:T(8,128)(2,1)S(1)}, u32[]{:S(2)}, u32[]{:S(2)}) %collective-permute-start.10) | collective-permute-done | bytes 262176 | tf_op jit(solution)/shard_map/ppermute | solution.py:549
  72.8 2.1 %collective-permute-done.13.refs_6_ = bf16[32,4096]{1,0:T(8,128)(2,1)S(1)} collective-permute-done((bf16[32,4096]{1,0:T(8,128)(2,1)S(1)}, bf16[32,4096]{1,0:T(8,128)(2,1)S(1)}, u32[]{:S(2)}, u32[]{:S(2)}) %collective-permute-start.13) | collective-permute-done | bytes 262176 | tf_op jit(solution)/shard_map/ppermute | solution.py:549
  74.8 3.5 %collective-permute-done.11.refs_3_ = bf16[32,4096]{1,0:T(8,128)(2,1)S(1)} collective-permute-done((bf16[32,4096]{1,0:T(8,128)(2,1)S(1)}, bf16[32,4096]{1,0:T(8,128)(2,1)S(1)}, u32[]{:S(2)}, u32[]{:S(2)}) %collective-permute-start.11) | collective-permute-done | bytes 262176 | tf_op jit(solution)/shard_map/ppermute | solution.py:549
  78.3 0.5 collective-permute-start.17
  78.8 0.5 collective-permute-start.19
  79.4 0.4 collective-permute-done.16.refs_8_
  82.5 6.0 %shard_map.132 = (bf16[512,384]{1,0:T(8,128)(2,1)S(1)}, bf16[512,1024]{1,0:T(8,128)(2,1)}, bf16[256,1024]{1,0:T(8,128)(2,1)}, bf16[256,1024]{1,0:T(8,128)(2,1)}, bf16[256,1024]{1,0:T(8,128)(2,1)}) custom-call(s32[5]{0:T(128)S(1)} %stack.23.place_ref, bf16[32,4096]{1,0:T(8,128)(2,1)S(1)} %multiply_convert_fusion.refs_0_, ...), custom_call_target="tpu_custom_call" | custom-call | flops 1610612736 | bytes 8388608 | tf_op jit(solution)/shard_map/pallas_call | solution.py:605
  88.5 0.7 copy-done.4
  89.2 1.3 collective-permute-start.24
  90.5 2.7 %collective-permute-start.25 = (bf16[256,1024]{1,0:T(8,128)(2,1)}, bf16[256,1024]{1,0:T(8,128)(2,1)}, u32[]{:S(2)}, u32[]{:S(2)}) collective-permute-start(bf16[256,1024]{1,0:T(8,128)(2,1)} %get-tuple-element.91), channel_id=1, source_target_pairs={{0,32},{16,48},{32,0},{48,16},{1,33},{17,49},{33,1},{49,17},{2,34}... | collective-permute-start | bytes 1572872 | tf_op jit(solution)/shard_map/ppermute | solution.py:549
  93.3 1.4 collective-permute-start.26
  94.7 23.2 %shard_map.133 = (bf16[16,144,512]{2,1,0:T(8,128)(2,1)}, bf16[512,384]{1,0:T(8,128)(2,1)}) custom-call(s32[1]{0:T(128)S(6)} %copy.14.length_ref, s32[32]{0:T(128)} %bitcast.29, bf16[512,384]{1,0:T(8,128)(2,1)} %copy-done.4, bf16[512,128]{1,0:T(8,128)(2,1)} %get-tuple-element.94.text_do_ref, bf16[2048,512]{1,0:T(8,128)(2,1)} %get-tuple-element.95.rows_ref, ...), custom_call_target="tpu_custom_call" | custom-call | flops 237565378560 | bytes 536870912 | tf_op jit(solution)/shard_map/pallas_call | solution.py:533
  118.0 4.7 %all-to-all-start.1 = ((bf16[16,144,512]{2,1,0:T(8,128)(2,1)}), bf16[16,144,512]{2,1,0:T(8,128)(2,1)S(1)}, u32[]{:S(2)}, u32[]{:S(2)}) async-start(bf16[16,144,512]{2,1,0:T(8,128)(2,1)} %get-tuple-element.113), calls=%async_computation.1 | async-start | bytes 4718592 | tf_op jit(solution)/shard_map/all_to_all | solution.py:680
  123.4 0.6 collective-permute-start.30
  124.0 2.0 %collective-permute-start.31 = (bf16[512,384]{1,0:T(8,128)(2,1)S(1)}, bf16[512,384]{1,0:T(8,128)(2,1)S(1)}, u32[]{:S(2)}, u32[]{:S(2)}) collective-permute-start(bf16[512,384]{1,0:T(8,128)(2,1)S(1)} %copy-done.7), channel_id=1, source_target_pairs={{0,32},{16,48},{32,0},{48,16},{1,33},{17,49},{33,1},{49,17},{2,34}... | collective-permute-start | bytes 1179656 | tf_op jit(solution)/shard_map/ppermute | solution.py:549
  126.3 1.2 collective-permute-start.32
  127.6 16.8 %collective-permute-done.30.grad_ref = bf16[512,384]{1,0:T(8,128)(2,1)S(1)} collective-permute-done((bf16[512,384]{1,0:T(8,128)(2,1)S(1)}, bf16[512,384]{1,0:T(8,128)(2,1)S(1)}, u32[]{:S(2)}, u32[]{:S(2)}) %collective-permute-start.30) | collective-permute-done | bytes 393248 | tf_op jit(solution)/shard_map/ppermute | solution.py:549
  144.4 0.7 copy-done.8
  145.1 4.6 %shard_map.134.early_ref = f32[4,384,256]{2,1,0:T(8,128)} custom-call(s32[5]{0:T(128)} %copy-done.3, bf16[512,1024]{1,0:T(8,128)(2,1)} %get-tuple-element.89.kept_ref, bf16[256,1024]{1,0:T(8,128)(2,1)} %collective-permute-done.24.near_ref, bf16[256,1024]{1,0:T(8,128)(2,1)} %copy-done.6, bf16[512,384]{1,0:T(8,128)(2,1)} %get-tuple-element.108.own_ref, ...), custom_call_target="tpu_custom_call" | custom-call | flops 805306368 | bytes 4194304 | tf_op jit(solution)/shard_map/pallas_call | solution.py:627
  149.7 0.7 copy-done.12
  150.5 4.9 %shard_map.135 = (f32[384,256]{1,0:T(8,128)}, bf16[384,256]{1,0:T(8,128)(2,1)}, bf16[384,256]{1,0:T(8,128)(2,1)}, bf16[384,256]{1,0:T(8,128)(2,1)}) custom-call(s32[5]{0:T(128)} %copy-done.3, f32[4,384,256]{2,1,0:T(8,128)} %shard_map.134.early_ref, bf16[256,1024]{1,0:T(8,128)(2,1)} %collective-permute-done.25.refs_0_, ...), custom_call_target="tpu_custom_call" | custom-call | flops 9663676416 | bytes 4194304 | tf_op jit(solution)/shard_map/pallas_call | solution.py:630
  155.4 3.3 %collective-permute-start.33 = (bf16[384,256]{1,0:T(8,128)(2,1)}, bf16[384,256]{1,0:T(8,128)(2,1)S(1)}, u32[]{:S(2)}, u32[]{:S(2)}) collective-permute-start(bf16[384,256]{1,0:T(8,128)(2,1)} %get-tuple-element.110), channel_id=1, source_target_pairs={{0,64},{64,128},{128,192},{192,0},{1,65},{65,129},{129,193},{193,1... | collective-permute-start | bytes 589832 | tf_op jit(solution)/shard_map/ppermute | solution.py:549
  158.6 4.5 %collective-permute-start.34 = (bf16[384,256]{1,0:T(8,128)(2,1)}, bf16[384,256]{1,0:T(8,128)(2,1)S(1)}, u32[]{:S(2)}, u32[]{:S(2)}) collective-permute-start(bf16[384,256]{1,0:T(8,128)(2,1)} %get-tuple-element.111), channel_id=1, source_target_pairs={{0,128},{64,192},{128,0},{192,64},{1,129},{65,193},{129,1},{193,65... | collective-permute-start | bytes 589832 | tf_op jit(solution)/shard_map/ppermute | solution.py:549
  163.1 2.7 %collective-permute-start.35 = (bf16[384,256]{1,0:T(8,128)(2,1)}, bf16[384,256]{1,0:T(8,128)(2,1)S(1)}, u32[]{:S(2)}, u32[]{:S(2)}) collective-permute-start(bf16[384,256]{1,0:T(8,128)(2,1)} %get-tuple-element.112), channel_id=1, source_target_pairs={{0,192},{64,0},{128,64},{192,128},{1,193},{65,1},{129,65},{193,129... | collective-permute-start | bytes 589832 | tf_op jit(solution)/shard_map/ppermute | solution.py:549
  165.8 1.7 shard_map.136
  167.5 5.5 %collective-permute-done.34.refs_1_ = bf16[384,256]{1,0:T(8,128)(2,1)S(1)} collective-permute-done((bf16[384,256]{1,0:T(8,128)(2,1)}, bf16[384,256]{1,0:T(8,128)(2,1)S(1)}, u32[]{:S(2)}, u32[]{:S(2)}) %collective-permute-start.34) | collective-permute-done | bytes 196640 | tf_op jit(solution)/shard_map/ppermute | solution.py:549
  173.0 8.3 %collective-permute-done.35.refs_2_ = bf16[384,256]{1,0:T(8,128)(2,1)S(1)} collective-permute-done((bf16[384,256]{1,0:T(8,128)(2,1)}, bf16[384,256]{1,0:T(8,128)(2,1)S(1)}, u32[]{:S(2)}, u32[]{:S(2)}) %collective-permute-start.35) | collective-permute-done | bytes 196640 | tf_op jit(solution)/shard_map/ppermute | solution.py:549
  181.3 0.9 shard_map.137
  (69 shorter events, 5.6 us)
Async XLA Ops:
  3.4 6.6 %copy-start = (bf16[256,4096]{1,0:T(8,128)(2,1)S(1)}, bf16[256,4096]{1,0:T(8,128)(2,1)}, u32[]{:S(2)}) copy-start(bf16[256,4096]{1,0:T(8,128)(2,1)} %own_weight_ref.1) | copy-start | bytes 6291460
  3.4 6.8 %copy-start.2 = (bf16[1,512,256]{2,1,0:T(8,128)(2,1)S(1)}, bf16[1,512,256]{2,1,0:T(8,128)(2,1)}, u32[]{:S(2)}) copy-start(bf16[1,512,256]{2,1,0:T(8,128)(2,1)} %param.10) | copy-start | bytes 786436
  3.4 40.7 %all-to-all-start = ((bf16[16,144,512]{2,1,0:T(8,128)(2,1)}), bf16[16,144,512]{2,1,0:T(8,128)(2,1)}, u32[]{:S(2)}, u32[]{:S(2)}) async-start(bf16[16,144,512]{2,1,0:T(8,128)(2,1)} %shard_map.130), calls=%async_computation | async-start | bytes 4718592 | tf_op jit(solution)/shard_map/all_to_all | solution.py:559
  9.9 4.8 %collective-permute-start.1 = (bf16[256,4096]{1,0:T(8,128)(2,1)S(1)}, bf16[256,4096]{1,0:T(8,128)(2,1)}, u32[]{:S(2)}, u32[]{:S(2)}) collective-permute-start(bf16[256,4096]{1,0:T(8,128)(2,1)S(1)} %copy-done), channel_id=1, source_target_pairs={{0,1},{1,0},{2,3},{3,2},{4,5},{5,4},{6,7},{7,6},{8,9},{9,8},{10,11... | collective-permute-start | bytes 6291464 | tf_op jit(solution)/shard_map/ppermute | solution.py:549
  10.2 4.2 %collective-permute-start = (bf16[512,256]{1,0:T(8,128)(2,1)S(1)}, bf16[512,256]{1,0:T(8,128)(2,1)S(1)}, u32[]{:S(2)}, u32[]{:S(2)}) collective-permute-start(bf16[512,256]{1,0:T(8,128)(2,1)S(1)} %bitcast.20), channel_id=1, source_target_pairs={{0,1},{1,0},{2,3},{3,2},{4,5},{5,4},{6,7},{7,6},{8,9},{9,8},{10,11... | collective-permute-start | bytes 786440 | tf_op jit(solution)/shard_map/ppermute | solution.py:549
  10.6 71.8 %copy-start.3 = (s32[5]{0:T(128)}, s32[5]{0:T(128)S(1)}, u32[]{:S(2)}) copy-start(s32[5]{0:T(128)S(1)} %stack.23.place_ref) | copy-start | bytes 64
  18.8 25.0 %collective-permute-start.4 = (bf16[32,4096]{1,0:T(8,128)(2,1)S(1)}, bf16[32,4096]{1,0:T(8,128)(2,1)S(1)}, u32[]{:S(2)}, u32[]{:S(2)}) collective-permute-start(bf16[32,4096]{1,0:T(8,128)(2,1)S(1)} %get-tuple-element.68), channel_id=1, source_target_pairs={{0,2},{2,0},{1,3},{3,1},{4,6},{6,4},{5,7},{7,5},{8,10},{10,8},{9,1... | collective-permute-start | bytes 786440 | tf_op jit(solution)/shard_map/ppermute | solution.py:549
  20.3 23.5 %collective-permute-start.5 = (bf16[32,4096]{1,0:T(8,128)(2,1)S(1)}, bf16[32,4096]{1,0:T(8,128)(2,1)S(1)}, u32[]{:S(2)}, u32[]{:S(2)}) collective-permute-start(bf16[32,4096]{1,0:T(8,128)(2,1)S(1)} %get-tuple-element.70), channel_id=1, source_target_pairs={{0,4},{4,8},{8,12},{12,0},{1,5},{5,9},{9,13},{13,1},{2,6},{6,10},{... | collective-permute-start | bytes 786440 | tf_op jit(solution)/shard_map/ppermute | solution.py:549
  21.8 22.2 %collective-permute-start.6 = (bf16[32,4096]{1,0:T(8,128)(2,1)S(1)}, bf16[32,4096]{1,0:T(8,128)(2,1)S(1)}, u32[]{:S(2)}, u32[]{:S(2)}) collective-permute-start(bf16[32,4096]{1,0:T(8,128)(2,1)S(1)} %get-tuple-element.71), channel_id=1, source_target_pairs={{0,12},{4,0},{8,4},{12,8},{1,13},{5,1},{9,5},{13,9},{2,14},{6,2},{... | collective-permute-start | bytes 786440 | tf_op jit(solution)/shard_map/ppermute | solution.py:549
  22.4 34.2 %collective-permute-start.2 = (bf16[32,4096]{1,0:T(8,128)(2,1)S(1)}, bf16[32,4096]{1,0:T(8,128)(2,1)S(1)}, u32[]{:S(2)}, u32[]{:S(2)}) collective-permute-start(bf16[32,4096]{1,0:T(8,128)(2,1)S(1)} %get-tuple-element.65), channel_id=1, source_target_pairs={{0,4},{4,8},{8,12},{12,0},{1,5},{5,9},{9,13},{13,1},{2,6},{6,10},{... | collective-permute-start | bytes 786440 | tf_op jit(solution)/shard_map/ppermute | solution.py:549
  23.9 32.7 %collective-permute-start.3 = (bf16[32,4096]{1,0:T(8,128)(2,1)S(1)}, bf16[32,4096]{1,0:T(8,128)(2,1)S(1)}, u32[]{:S(2)}, u32[]{:S(2)}) collective-permute-start(bf16[32,4096]{1,0:T(8,128)(2,1)S(1)} %get-tuple-element.66), channel_id=1, source_target_pairs={{0,12},{4,0},{8,4},{12,8},{1,13},{5,1},{9,5},{13,9},{2,14},{6,2},{... | collective-permute-start | bytes 786440 | tf_op jit(solution)/shard_map/ppermute | solution.py:549
  44.1 12.4 %collective-permute-start.7 = (bf16[32,4096]{1,0:T(8,128)(2,1)S(1)}, bf16[32,4096]{1,0:T(8,128)(2,1)S(1)}, u32[]{:S(2)}, u32[]{:S(2)}) collective-permute-start(bf16[32,4096]{1,0:T(8,128)(2,1)S(1)} %add_convert_fusion.1), channel_id=1, source_target_pairs={{0,8},{4,12},{8,0},{12,4},{1,9},{5,13},{9,1},{13,5},{2,10},{6,14},... | collective-permute-start | bytes 786440 | tf_op jit(solution)/shard_map/ppermute | solution.py:549
  46.1 10.4 %collective-permute-start.8 = (bf16[32,4096]{1,0:T(8,128)(2,1)S(1)}, bf16[32,4096]{1,0:T(8,128)(2,1)S(1)}, u32[]{:S(2)}, u32[]{:S(2)}) collective-permute-start(bf16[32,4096]{1,0:T(8,128)(2,1)S(1)} %add_convert_fusion), channel_id=1, source_target_pairs={{0,2},{2,0},{1,3},{3,1},{4,6},{6,4},{5,7},{7,5},{8,10},{10,8},{9,1... | collective-permute-start | bytes 786440 | tf_op jit(solution)/shard_map/ppermute | solution.py:549
  46.8 9.7 %copy-start.5 = (bf16[1,32,4096]{2,1,0:T(8,128)(2,1)S(1)}, bf16[1,32,4096]{2,1,0:T(8,128)(2,1)}, u32[]{:S(2)}) copy-start(bf16[1,32,4096]{2,1,0:T(8,128)(2,1)} %param.11) | copy-start | bytes 786436
  46.8 10.1 %copy-start.9 = (f32[4096]{0:T(1024)S(1)}, f32[4096]{0:T(1024)}, u32[]{:S(2)}) copy-start(f32[4096]{0:T(1024)} %param.13) | copy-start | bytes 49156
  57.2 7.7 %collective-permute-start.9 = (bf16[32,4096]{1,0:T(8,128)(2,1)S(1)}, bf16[32,4096]{1,0:T(8,128)(2,1)S(1)}, u32[]{:S(2)}, u32[]{:S(2)}) collective-permute-start(bf16[32,4096]{1,0:T(8,128)(2,1)S(1)} %multiply_convert_fusion.refs_0_), channel_id=1, source_target_pairs={{0,2},{2,0},{1,3},{3,1},{4,6},{6,4},{5,7},{7,5},{8,10},{10,8},{9,1... | collective-permute-start | bytes 786440 | tf_op jit(solution)/shard_map/ppermute | solution.py:549
  58.6 10.7 %collective-permute-start.12 = (bf16[32,4096]{1,0:T(8,128)(2,1)S(1)}, bf16[32,4096]{1,0:T(8,128)(2,1)S(1)}, u32[]{:S(2)}, u32[]{:S(2)}) collective-permute-start(bf16[32,4096]{1,0:T(8,128)(2,1)S(1)} %multiply_convert_fusion.refs_0_), channel_id=1, source_target_pairs={{0,8},{4,12},{8,0},{12,4},{1,9},{5,13},{9,1},{13,5},{2,10},{6,14},... | collective-permute-start | bytes 786440 | tf_op jit(solution)/shard_map/ppermute | solution.py:549
  60.2 12.6 %collective-permute-start.10 = (bf16[32,4096]{1,0:T(8,128)(2,1)S(1)}, bf16[32,4096]{1,0:T(8,128)(2,1)S(1)}, u32[]{:S(2)}, u32[]{:S(2)}) collective-permute-start(bf16[32,4096]{1,0:T(8,128)(2,1)S(1)} %multiply_convert_fusion.refs_0_), channel_id=1, source_target_pairs={{0,12},{4,0},{8,4},{12,8},{1,13},{5,1},{9,5},{13,9},{2,14},{6,2},{... | collective-permute-start | bytes 786440 | tf_op jit(solution)/shard_map/ppermute | solution.py:549
  62.0 12.9 %collective-permute-start.13 = (bf16[32,4096]{1,0:T(8,128)(2,1)S(1)}, bf16[32,4096]{1,0:T(8,128)(2,1)S(1)}, u32[]{:S(2)}, u32[]{:S(2)}) collective-permute-start(bf16[32,4096]{1,0:T(8,128)(2,1)S(1)} %multiply_convert_fusion.refs_0_), channel_id=1, source_target_pairs={{0,4},{4,8},{8,12},{12,0},{1,5},{5,9},{9,13},{13,1},{2,6},{6,10},{... | collective-permute-start | bytes 786440 | tf_op jit(solution)/shard_map/ppermute | solution.py:549
  64.9 13.4 %collective-permute-start.11 = (bf16[32,4096]{1,0:T(8,128)(2,1)S(1)}, bf16[32,4096]{1,0:T(8,128)(2,1)S(1)}, u32[]{:S(2)}, u32[]{:S(2)}) collective-permute-start(bf16[32,4096]{1,0:T(8,128)(2,1)S(1)} %collective-permute-done.9.refs_1_), channel_id=1, source_target_pairs={{0,12},{4,0},{8,4},{12,8},{1,13},{5,1},{9,5},{13,9},{2,14},{6,2},{... | collective-permute-start | bytes 786440 | tf_op jit(solution)/shard_map/ppermute | solution.py:549
  66.6 12.7 %collective-permute-start.15 = (bf16[32,4096]{1,0:T(8,128)(2,1)S(1)}, bf16[32,4096]{1,0:T(8,128)(2,1)S(1)}, u32[]{:S(2)}, u32[]{:S(2)}) collective-permute-start(bf16[32,4096]{1,0:T(8,128)(2,1)S(1)} %collective-permute-done.9.refs_1_), channel_id=1, source_target_pairs={{0,4},{4,8},{8,12},{12,0},{1,5},{5,9},{9,13},{13,1},{2,6},{6,10},{... | collective-permute-start | bytes 786440 | tf_op jit(solution)/shard_map/ppermute | solution.py:549
  69.3 9.5 %collective-permute-start.14 = (bf16[32,4096]{1,0:T(8,128)(2,1)S(1)}, bf16[32,4096]{1,0:T(8,128)(2,1)S(1)}, u32[]{:S(2)}, u32[]{:S(2)}) collective-permute-start(bf16[32,4096]{1,0:T(8,128)(2,1)S(1)} %collective-permute-done.12.refs_4_), channel_id=1, source_target_pairs={{0,2},{2,0},{1,3},{3,1},{4,6},{6,4},{5,7},{7,5},{8,10},{10,8},{9,1... | collective-permute-start | bytes 786440 | tf_op jit(solution)/shard_map/ppermute | solution.py:549
  78.3 1.5 collective-permute-start.16
  78.3 1.9 %collective-permute-start.17 = (bf16[32,4096]{1,0:T(8,128)(2,1)S(1)}, bf16[32,4096]{1,0:T(8,128)(2,1)S(1)}, u32[]{:S(2)}, u32[]{:S(2)}) collective-permute-start(bf16[32,4096]{1,0:T(8,128)(2,1)S(1)} %collective-permute-done.9.refs_1_), channel_id=1, source_target_pairs={{0,1},{1,0},{2,3},{3,2},{4,5},{5,4},{6,7},{7,6},{8,9},{9,8},{10,11... | collective-permute-start | bytes 786440 | tf_op jit(solution)/shard_map/ppermute | solution.py:549
  78.8 1.8 collective-permute-start.18
  78.8 2.5 %collective-permute-start.19 = (bf16[32,4096]{1,0:T(8,128)(2,1)S(1)}, bf16[32,4096]{1,0:T(8,128)(2,1)S(1)}, u32[]{:S(2)}, u32[]{:S(2)}) collective-permute-start(bf16[32,4096]{1,0:T(8,128)(2,1)S(1)} %collective-permute-done.11.refs_3_), channel_id=1, source_target_pairs={{0,1},{1,0},{2,3},{3,2},{4,5},{5,4},{6,7},{7,6},{8,9},{9,8},{10,11... | collective-permute-start | bytes 786440 | tf_op jit(solution)/shard_map/ppermute | solution.py:549
  79.3 2.1 %collective-permute-start.20 = (bf16[32,4096]{1,0:T(8,128)(2,1)S(1)}, bf16[32,4096]{1,0:T(8,128)(2,1)S(1)}, u32[]{:S(2)}, u32[]{:S(2)}) collective-permute-start(bf16[32,4096]{1,0:T(8,128)(2,1)S(1)} %collective-permute-done.12.refs_4_), channel_id=1, source_target_pairs={{0,1},{1,0},{2,3},{3,2},{4,5},{5,4},{6,7},{7,6},{8,9},{9,8},{10,11... | collective-permute-start | bytes 786440 | tf_op jit(solution)/shard_map/ppermute | solution.py:549
  79.8 1.9 %collective-permute-start.22 = (bf16[32,4096]{1,0:T(8,128)(2,1)S(1)}, bf16[32,4096]{1,0:T(8,128)(2,1)S(1)}, u32[]{:S(2)}, u32[]{:S(2)}) collective-permute-start(bf16[32,4096]{1,0:T(8,128)(2,1)S(1)} %collective-permute-done.13.refs_6_), channel_id=1, source_target_pairs={{0,1},{1,0},{2,3},{3,2},{4,5},{5,4},{6,7},{7,6},{8,9},{9,8},{10,11... | collective-permute-start | bytes 786440 | tf_op jit(solution)/shard_map/ppermute | solution.py:549
  80.2 1.9 %collective-permute-start.21 = (bf16[32,4096]{1,0:T(8,128)(2,1)S(1)}, bf16[32,4096]{1,0:T(8,128)(2,1)S(1)}, u32[]{:S(2)}, u32[]{:S(2)}) collective-permute-start(bf16[32,4096]{1,0:T(8,128)(2,1)S(1)} %collective-permute-done.14.refs_5_), channel_id=1, source_target_pairs={{0,1},{1,0},{2,3},{3,2},{4,5},{5,4},{6,7},{7,6},{8,9},{9,8},{10,11... | collective-permute-start | bytes 786440 | tf_op jit(solution)/shard_map/ppermute | solution.py:549
  80.6 1.9 %collective-permute-start.23 = (bf16[32,4096]{1,0:T(8,128)(2,1)S(1)}, bf16[32,4096]{1,0:T(8,128)(2,1)S(1)}, u32[]{:S(2)}, u32[]{:S(2)}) collective-permute-start(bf16[32,4096]{1,0:T(8,128)(2,1)S(1)} %collective-permute-done.15.refs_7_), channel_id=1, source_target_pairs={{0,1},{1,0},{2,3},{3,2},{4,5},{5,4},{6,7},{7,6},{8,9},{9,8},{10,11... | collective-permute-start | bytes 786440 | tf_op jit(solution)/shard_map/ppermute | solution.py:549
  89.2 28.7 %collective-permute-start.24 = (bf16[256,1024]{1,0:T(8,128)(2,1)}, bf16[256,1024]{1,0:T(8,128)(2,1)}, u32[]{:S(2)}, u32[]{:S(2)}) collective-permute-start(bf16[256,1024]{1,0:T(8,128)(2,1)} %get-tuple-element.90), channel_id=1, source_target_pairs={{0,16},{16,32},{32,48},{48,0},{1,17},{17,33},{33,49},{49,1},{2,18}... | collective-permute-start | bytes 1572872 | tf_op jit(solution)/shard_map/ppermute | solution.py:549
  90.5 27.4 %collective-permute-start.25 = (bf16[256,1024]{1,0:T(8,128)(2,1)}, bf16[256,1024]{1,0:T(8,128)(2,1)}, u32[]{:S(2)}, u32[]{:S(2)}) collective-permute-start(bf16[256,1024]{1,0:T(8,128)(2,1)} %get-tuple-element.91), channel_id=1, source_target_pairs={{0,32},{16,48},{32,0},{48,16},{1,33},{17,49},{33,1},{49,17},{2,34}... | collective-permute-start | bytes 1572872 | tf_op jit(solution)/shard_map/ppermute | solution.py:549
  93.3 24.7 %collective-permute-start.26 = (bf16[256,1024]{1,0:T(8,128)(2,1)}, bf16[256,1024]{1,0:T(8,128)(2,1)}, u32[]{:S(2)}, u32[]{:S(2)}) collective-permute-start(bf16[256,1024]{1,0:T(8,128)(2,1)} %get-tuple-element.92), channel_id=1, source_target_pairs={{0,48},{16,0},{32,16},{48,32},{1,49},{17,1},{33,17},{49,33},{2,50}... | collective-permute-start | bytes 1572872 | tf_op jit(solution)/shard_map/ppermute | solution.py:549
  118.0 5.4 %copy-start.7 = (bf16[512,384]{1,0:T(8,128)(2,1)S(1)}, bf16[512,384]{1,0:T(8,128)(2,1)}, u32[]{:S(2)}) copy-start(bf16[512,384]{1,0:T(8,128)(2,1)} %get-tuple-element.108.own_ref) | copy-start | bytes 1179652
  118.0 47.8 %all-to-all-start.1 = ((bf16[16,144,512]{2,1,0:T(8,128)(2,1)}), bf16[16,144,512]{2,1,0:T(8,128)(2,1)S(1)}, u32[]{:S(2)}, u32[]{:S(2)}) async-start(bf16[16,144,512]{2,1,0:T(8,128)(2,1)} %get-tuple-element.113), calls=%async_computation.1 | async-start | bytes 4718592 | tf_op jit(solution)/shard_map/all_to_all | solution.py:680
  122.7 3.3 %collective-permute-start.27 = (bf16[256,1024]{1,0:T(8,128)(2,1)}, bf16[256,1024]{1,0:T(8,128)(2,1)S(1)}, u32[]{:S(2)}, u32[]{:S(2)}) collective-permute-start(bf16[256,1024]{1,0:T(8,128)(2,1)} %collective-permute-done.24.near_ref), channel_id=1, source_target_pairs={{0,1},{1,0},{2,3},{3,2},{4,5},{5,4},{6,7},{7,6},{8,9},{9,8},{10,11... | collective-permute-start | bytes 1572872 | tf_op jit(solution)/shard_map/ppermute | solution.py:549
  122.9 3.2 %collective-permute-start.28 = (bf16[256,1024]{1,0:T(8,128)(2,1)}, bf16[256,1024]{1,0:T(8,128)(2,1)S(1)}, u32[]{:S(2)}, u32[]{:S(2)}) collective-permute-start(bf16[256,1024]{1,0:T(8,128)(2,1)} %collective-permute-done.25.refs_0_), channel_id=1, source_target_pairs={{0,1},{1,0},{2,3},{3,2},{4,5},{5,4},{6,7},{7,6},{8,9},{9,8},{10,11... | collective-permute-start | bytes 1572872 | tf_op jit(solution)/shard_map/ppermute | solution.py:549
  123.2 3.1 %collective-permute-start.29 = (bf16[256,1024]{1,0:T(8,128)(2,1)}, bf16[256,1024]{1,0:T(8,128)(2,1)S(1)}, u32[]{:S(2)}, u32[]{:S(2)}) collective-permute-start(bf16[256,1024]{1,0:T(8,128)(2,1)} %collective-permute-done.26.refs_1_), channel_id=1, source_target_pairs={{0,1},{1,0},{2,3},{3,2},{4,5},{5,4},{6,7},{7,6},{8,9},{9,8},{10,11... | collective-permute-start | bytes 1572872 | tf_op jit(solution)/shard_map/ppermute | solution.py:549
  123.4 21.0 %collective-permute-start.30 = (bf16[512,384]{1,0:T(8,128)(2,1)S(1)}, bf16[512,384]{1,0:T(8,128)(2,1)S(1)}, u32[]{:S(2)}, u32[]{:S(2)}) collective-permute-start(bf16[512,384]{1,0:T(8,128)(2,1)S(1)} %copy-done.7), channel_id=1, source_target_pairs={{0,16},{16,32},{32,48},{48,0},{1,17},{17,33},{33,49},{49,1},{2,18}... | collective-permute-start | bytes 1179656 | tf_op jit(solution)/shard_map/ppermute | solution.py:549
  124.0 25.7 %collective-permute-start.31 = (bf16[512,384]{1,0:T(8,128)(2,1)S(1)}, bf16[512,384]{1,0:T(8,128)(2,1)S(1)}, u32[]{:S(2)}, u32[]{:S(2)}) collective-permute-start(bf16[512,384]{1,0:T(8,128)(2,1)S(1)} %copy-done.7), channel_id=1, source_target_pairs={{0,32},{16,48},{32,0},{48,16},{1,33},{17,49},{33,1},{49,17},{2,34}... | collective-permute-start | bytes 1179656 | tf_op jit(solution)/shard_map/ppermute | solution.py:549
  126.0 18.4 %copy-start.6 = (bf16[256,1024]{1,0:T(8,128)(2,1)}, bf16[256,1024]{1,0:T(8,128)(2,1)S(1)}, u32[]{:S(2)}) copy-start(bf16[256,1024]{1,0:T(8,128)(2,1)S(1)} %collective-permute-done.27.far_ref) | copy-start | bytes 1572868
  126.0 18.4 %copy-start.10 = (bf16[256,1024]{1,0:T(8,128)(2,1)}, bf16[256,1024]{1,0:T(8,128)(2,1)S(1)}, u32[]{:S(2)}) copy-start(bf16[256,1024]{1,0:T(8,128)(2,1)S(1)} %collective-permute-done.28.refs_2_) | copy-start | bytes 1572868
  126.3 18.1 %copy-start.11 = (bf16[256,1024]{1,0:T(8,128)(2,1)}, bf16[256,1024]{1,0:T(8,128)(2,1)S(1)}, u32[]{:S(2)}) copy-start(bf16[256,1024]{1,0:T(8,128)(2,1)S(1)} %collective-permute-done.29.refs_3_) | copy-start | bytes 1572868
  126.3 23.4 %collective-permute-start.32 = (bf16[512,384]{1,0:T(8,128)(2,1)S(1)}, bf16[512,384]{1,0:T(8,128)(2,1)}, u32[]{:S(2)}, u32[]{:S(2)}) collective-permute-start(bf16[512,384]{1,0:T(8,128)(2,1)S(1)} %copy-done.7), channel_id=1, source_target_pairs={{0,48},{16,0},{32,16},{48,32},{1,49},{17,1},{33,17},{49,33},{2,50}... | collective-permute-start | bytes 1179656 | tf_op jit(solution)/shard_map/ppermute | solution.py:549
  155.3 26.0 %copy-start.1 = (f32[384,256]{1,0:T(8,128)S(1)}, f32[384,256]{1,0:T(8,128)}, u32[]{:S(2)}) copy-start(f32[384,256]{1,0:T(8,128)} %get-tuple-element.120.kept_ref) | copy-start | bytes 1179652
  155.4 12.1 %collective-permute-start.33 = (bf16[384,256]{1,0:T(8,128)(2,1)}, bf16[384,256]{1,0:T(8,128)(2,1)S(1)}, u32[]{:S(2)}, u32[]{:S(2)}) collective-permute-start(bf16[384,256]{1,0:T(8,128)(2,1)} %get-tuple-element.110), channel_id=1, source_target_pairs={{0,64},{64,128},{128,192},{192,0},{1,65},{65,129},{129,193},{193,1... | collective-permute-start | bytes 589832 | tf_op jit(solution)/shard_map/ppermute | solution.py:549
  158.6 14.4 %collective-permute-start.34 = (bf16[384,256]{1,0:T(8,128)(2,1)}, bf16[384,256]{1,0:T(8,128)(2,1)S(1)}, u32[]{:S(2)}, u32[]{:S(2)}) collective-permute-start(bf16[384,256]{1,0:T(8,128)(2,1)} %get-tuple-element.111), channel_id=1, source_target_pairs={{0,128},{64,192},{128,0},{192,64},{1,129},{65,193},{129,1},{193,65... | collective-permute-start | bytes 589832 | tf_op jit(solution)/shard_map/ppermute | solution.py:549
  163.1 18.2 %collective-permute-start.35 = (bf16[384,256]{1,0:T(8,128)(2,1)}, bf16[384,256]{1,0:T(8,128)(2,1)S(1)}, u32[]{:S(2)}, u32[]{:S(2)}) collective-permute-start(bf16[384,256]{1,0:T(8,128)(2,1)} %get-tuple-element.112), channel_id=1, source_target_pairs={{0,192},{64,0},{128,64},{192,128},{1,193},{65,1},{129,65},{193,129... | collective-permute-start | bytes 589832 | tf_op jit(solution)/shard_map/ppermute | solution.py:549
  (3 other events, 2.2 us)

commit v2 on v0

--- a/solution.py
+++ b/solution.py
@@ -531,7 +531,6 @@
 def encode(place, context, residual, weight, gain, packed, order):
     other_weight = shift(weight, "core", 1)
     other = shift(context, "core", 1)
-    other_weight, packed = lax.optimization_barrier((other_weight, packed))
     packed = lax.all_to_all(packed, SEQ, split_axis=0, concat_axis=0, tiled=True)
     chunks = whole_call(
         partial_kernel,

time: 180 us -> 179 us (level)
  waiting for transfers between devices: 72.5 us -> 70.5 us
    ppermute x36, waiting for transfers between devices: 72.5 us -> 70.5 us  [shift(): lax.ppermute(rows, axis, [(i, (i + step) % size) for i in range(size)])]
  transfers between devices with their start and end apart: 38 -> 38, of which waited for: 20 -> 20; matrix products, arithmetic and copies ran while one was open for 0% -> 0% of each run, Pallas kernels for 27% -> 25%
where the time goes in v2:
time: 179 us; the launch traced here: 177 us
  waiting for transfers between devices  70.5 us (39%)
  Pallas kernels  53.8 us (30%)
  starting transfers between devices  49.9 us (28%)
    ppermute x36, waiting for transfers between devices, shift(): lax.ppermute(rows, axis, [(i, (i + step) % size) for i in range(size)])  70.5 us
    ppermute x36, starting transfers between devices, shift(): lax.ppermute(rows, axis, [(i, (i + step) % size) for i in range(size)])  38.8 us
    pallas_call x1, Pallas kernels, attention(): grid_call(attention_kernel, 1 + IMAGE // FORWARD_ROWS, [IN_SMEM, IN_SMEM,...  23.2 us
    pallas_call x1, Pallas kernels, image_forward(): grid_call(image_forward_kernel, IMAGE // FORWARD_ROWS, [IN_SMEM, fixed(HE...  9.72 us
    all_to_all x1, starting transfers between devices, encode(): lax.all_to_all(packed, SEQ, split_axis=0, concat_axis=0, tiled=True)  6.54 us
    pallas_call x1, Pallas kernels, weight_sums(): whole_call(weight_kernel, [total] + [rows_of(columns, FEATURES)] * 3, 1,...  6.15 us
    pallas_call x1, Pallas kernels, project(): pl.pallas_call(text_kernel, out_shape=[rows_of(PROMPT, columns), rows_of(...  5.31 us
    all_to_all x1, starting transfers between devices, on_device(): lax.all_to_all(sent, SEQ, split_axis=0, concat_axis=0, tiled=True)  4.55 us
  transfers between devices with their start and end apart: 38, of which 20 were waited for; matrix products, arithmetic and copies ran while one was open for 0% of the time, Pallas kernels for 25%

profile of v2, /device:TPU:8, one launch (start us, length us, event | category | flops | bytes accessed | tf_op | source)
XLA Modules:
  0.0 177.3 jit_solution(598610421085468193)
XLA Ops:
  0.6 2.8 %shard_map.130 = bf16[16,144,512]{2,1,0:T(8,128)(2,1)} custom-call(bf16[128,6144]{1,0:T(8,128)(2,1)} %bitcast.22, bf16[128,2048]{1,0:T(8,128)(2,1)} %bitcast.23, bf16[32,2048]{1,0:T(8,128)(2,1)} %bitcast.24), custom_call_target="tpu_custom_call" | custom-call | bytes 4194304 | tf_op jit(solution)/shard_map/pallas_call | solution.py:113
  3.4 6.5 %all-to-all-start = ((bf16[16,144,512]{2,1,0:T(8,128)(2,1)}), bf16[16,144,512]{2,1,0:T(8,128)(2,1)}, u32[]{:S(2)}, u32[]{:S(2)}) async-start(bf16[16,144,512]{2,1,0:T(8,128)(2,1)} %shard_map.130), calls=%async_computation | async-start | bytes 4718592 | tf_op jit(solution)/shard_map/all_to_all | solution.py:534
  10.7 3.7 %collective-permute-done.other_ref = bf16[512,256]{1,0:T(8,128)(2,1)S(1)} collective-permute-done((bf16[512,256]{1,0:T(8,128)(2,1)S(1)}, bf16[512,256]{1,0:T(8,128)(2,1)S(1)}, u32[]{:S(2)}, u32[]{:S(2)}) %collective-permute-start) | collective-permute-done | bytes 262176 | tf_op jit(solution)/shard_map/ppermute | solution.py:524
  14.7 4.1 %shard_map.129 = (bf16[32,4096]{1,0:T(8,128)(2,1)S(1)}, bf16[32,4096]{1,0:T(8,128)(2,1)S(1)}, bf16[32,4096]{1,0:T(8,128)(2,1)S(1)}, bf16[32,4096]{1,0:T(8,128)(2...) custom-call(s32[5]{0:T(128)S(1)} %stack.23.place_ref, ...), custom_call_target="tpu_custom_call" | custom-call | flops 1073741824 | bytes 8388608 | tf_op jit(solution)/shard_map/pallas_call | solution.py:535
  18.8 1.6 collective-permute-start.4
  20.4 1.5 collective-permute-start.5
  21.9 0.5 collective-permute-start.6
  22.4 1.5 collective-permute-start.2
  23.9 0.5 collective-permute-start.3
  24.4 19.4 %collective-permute-done.4 = bf16[32,4096]{1,0:T(8,128)(2,1)S(1)} collective-permute-done((bf16[32,4096]{1,0:T(8,128)(2,1)S(1)}, bf16[32,4096]{1,0:T(8,128)(2,1)S(1)}, u32[]{:S(2)}, u32[]{:S(2)}) %collective-permute-start.4) | collective-permute-done | bytes 262176 | tf_op jit(solution)/shard_map/ppermute | solution.py:524
  44.1 2.0 %collective-permute-start.7 = (bf16[32,4096]{1,0:T(8,128)(2,1)S(1)}, bf16[32,4096]{1,0:T(8,128)(2,1)S(1)}, u32[]{:S(2)}, u32[]{:S(2)}) collective-permute-start(bf16[32,4096]{1,0:T(8,128)(2,1)S(1)} %add_convert_fusion.1), channel_id=1, source_target_pairs={{0,8},{4,12},{8,0},{12,4},{1,9},{5,13},{9,1},{13,5},{2,10},{6,14},... | collective-permute-start | bytes 786440 | tf_op jit(solution)/shard_map/ppermute | solution.py:524
  46.1 0.7 collective-permute-start.8
  46.9 9.7 %shard_map.131 = (bf16[2048,2048]{1,0:T(8,128)(2,1)}, bf16[2048,512]{1,0:T(8,128)(2,1)}, f32[2048,128]{1,0:T(8,128)}, f32[2048,128]{1,0:T(8,128)}, f32[2048,128]{1,0:T(8,128)}, /*index=5*/bf16[512,128]{1,0:T(8,128)(2,1)}) custom-call(s32[32]{0:T(128)} %bitcast.28, bf16[16,144,512]{2,1,0:T(8,128)(2,1)} %all-to-all-done.packed_ref), custom_call_target="tpu_custom_call" | custom-call | flops 64424509440 | bytes 536870912 | tf_op jit(solution)/shard_map/pallas_call | solution.py:492
  57.2 1.4 collective-permute-start.9
  58.6 1.6 collective-permute-start.12
  60.3 1.8 %collective-permute-start.10 = (bf16[32,4096]{1,0:T(8,128)(2,1)S(1)}, bf16[32,4096]{1,0:T(8,128)(2,1)S(1)}, u32[]{:S(2)}, u32[]{:S(2)}) collective-permute-start(bf16[32,4096]{1,0:T(8,128)(2,1)S(1)} %multiply_convert_fusion.refs_0_), channel_id=1, source_target_pairs={{0,12},{4,0},{8,4},{12,8},{1,13},{5,1},{9,5},{13,9},{2,14},{6,2},{... | collective-permute-start | bytes 786440 | tf_op jit(solution)/shard_map/ppermute | solution.py:524
  62.3 2.7 %collective-permute-done.9.refs_1_ = bf16[32,4096]{1,0:T(8,128)(2,1)S(1)} collective-permute-done((bf16[32,4096]{1,0:T(8,128)(2,1)S(1)}, bf16[32,4096]{1,0:T(8,128)(2,1)S(1)}, u32[]{:S(2)}, u32[]{:S(2)}) %collective-permute-start.9) | collective-permute-done | bytes 262176 | tf_op jit(solution)/shard_map/ppermute | solution.py:524
  65.0 1.8 %collective-permute-start.11 = (bf16[32,4096]{1,0:T(8,128)(2,1)S(1)}, bf16[32,4096]{1,0:T(8,128)(2,1)S(1)}, u32[]{:S(2)}, u32[]{:S(2)}) collective-permute-start(bf16[32,4096]{1,0:T(8,128)(2,1)S(1)} %collective-permute-done.9.refs_1_), channel_id=1, source_target_pairs={{0,12},{4,0},{8,4},{12,8},{1,13},{5,1},{9,5},{13,9},{2,14},{6,2},{... | collective-permute-start | bytes 786440 | tf_op jit(solution)/shard_map/ppermute | solution.py:524
  67.0 2.4 %collective-permute-done.12.refs_4_ = bf16[32,4096]{1,0:T(8,128)(2,1)S(1)} collective-permute-done((bf16[32,4096]{1,0:T(8,128)(2,1)S(1)}, bf16[32,4096]{1,0:T(8,128)(2,1)S(1)}, u32[]{:S(2)}, u32[]{:S(2)}) %collective-permute-start.12) | collective-permute-done | bytes 262176 | tf_op jit(solution)/shard_map/ppermute | solution.py:524
  69.4 0.7 collective-permute-start.14
  70.1 2.8 %collective-permute-done.10.refs_2_ = bf16[32,4096]{1,0:T(8,128)(2,1)S(1)} collective-permute-done((bf16[32,4096]{1,0:T(8,128)(2,1)S(1)}, bf16[32,4096]{1,0:T(8,128)(2,1)S(1)}, u32[]{:S(2)}, u32[]{:S(2)}) %collective-permute-start.10) | collective-permute-done | bytes 262176 | tf_op jit(solution)/shard_map/ppermute | solution.py:524
  72.9 2.1 %collective-permute-done.13.refs_6_ = bf16[32,4096]{1,0:T(8,128)(2,1)S(1)} collective-permute-done((bf16[32,4096]{1,0:T(8,128)(2,1)S(1)}, bf16[32,4096]{1,0:T(8,128)(2,1)S(1)}, u32[]{:S(2)}, u32[]{:S(2)}) %collective-permute-start.13) | collective-permute-done | bytes 262176 | tf_op jit(solution)/shard_map/ppermute | solution.py:524
  74.9 3.5 %collective-permute-done.11.refs_3_ = bf16[32,4096]{1,0:T(8,128)(2,1)S(1)} collective-permute-done((bf16[32,4096]{1,0:T(8,128)(2,1)S(1)}, bf16[32,4096]{1,0:T(8,128)(2,1)S(1)}, u32[]{:S(2)}, u32[]{:S(2)}) %collective-permute-start.11) | collective-permute-done | bytes 262176 | tf_op jit(solution)/shard_map/ppermute | solution.py:524
  78.4 0.5 collective-permute-start.17
  78.9 0.5 collective-permute-start.19
  79.5 0.4 collective-permute-done.16.refs_8_
  81.8 0.4 collective-permute-done.21.refs_13_
  82.2 0.4 collective-permute-done.23.refs_15_
  82.6 5.3 %shard_map.132 = (bf16[512,384]{1,0:T(8,128)(2,1)S(1)}, bf16[512,1024]{1,0:T(8,128)(2,1)}, bf16[256,1024]{1,0:T(8,128)(2,1)}, bf16[256,1024]{1,0:T(8,128)(2,1)}, bf16[256,1024]{1,0:T(8,128)(2,1)}) custom-call(s32[5]{0:T(128)S(1)} %stack.23.place_ref, bf16[32,4096]{1,0:T(8,128)(2,1)S(1)} %multiply_convert_fusion.refs_0_, ...), custom_call_target="tpu_custom_call" | custom-call | flops 1610612736 | bytes 8388608 | tf_op jit(solution)/shard_map/pallas_call | solution.py:580
  87.9 0.7 copy-done.4
  88.6 1.3 collective-permute-start.24
  89.9 2.7 %collective-permute-start.25 = (bf16[256,1024]{1,0:T(8,128)(2,1)}, bf16[256,1024]{1,0:T(8,128)(2,1)}, u32[]{:S(2)}, u32[]{:S(2)}) collective-permute-start(bf16[256,1024]{1,0:T(8,128)(2,1)} %get-tuple-element.91), channel_id=1, source_target_pairs={{0,32},{16,48},{32,0},{48,16},{1,33},{17,49},{33,1},{49,17},{2,34}... | collective-permute-start | bytes 1572872 | tf_op jit(solution)/shard_map/ppermute | solution.py:524
  92.6 1.4 collective-permute-start.26
  94.1 23.2 %shard_map.133 = (bf16[16,144,512]{2,1,0:T(8,128)(2,1)}, bf16[512,384]{1,0:T(8,128)(2,1)}) custom-call(s32[1]{0:T(128)S(6)} %copy.14.length_ref, s32[32]{0:T(128)} %bitcast.29, bf16[512,384]{1,0:T(8,128)(2,1)} %copy-done.4, bf16[512,128]{1,0:T(8,128)(2,1)} %get-tuple-element.94.text_do_ref, bf16[2048,512]{1,0:T(8,128)(2,1)} %get-tuple-element.95.rows_ref, ...), custom_call_target="tpu_custom_call" | custom-call | flops 237565378560 | bytes 536870912 | tf_op jit(solution)/shard_map/pallas_call | solution.py:509
  117.4 4.6 %all-to-all-start.1 = ((bf16[16,144,512]{2,1,0:T(8,128)(2,1)}), bf16[16,144,512]{2,1,0:T(8,128)(2,1)S(1)}, u32[]{:S(2)}, u32[]{:S(2)}) async-start(bf16[16,144,512]{2,1,0:T(8,128)(2,1)} %get-tuple-element.113), calls=%async_computation.1 | async-start | bytes 4718592 | tf_op jit(solution)/shard_map/all_to_all | solution.py:648
  122.6 0.6 collective-permute-start.30
  123.2 2.1 %collective-permute-start.31 = (bf16[512,384]{1,0:T(8,128)(2,1)}, bf16[512,384]{1,0:T(8,128)(2,1)}, u32[]{:S(2)}, u32[]{:S(2)}) collective-permute-start(bf16[512,384]{1,0:T(8,128)(2,1)} %get-tuple-element.108.refs_6_), channel_id=1, source_target_pairs={{0,32},{16,48},{32,0},{48,16},{1,33},{17,49},{33,1},{49,17},{2,34}... | collective-permute-start | bytes 1179656 | tf_op jit(solution)/shard_map/ppermute | solution.py:524
  125.5 1.2 collective-permute-start.32
  126.8 17.1 %collective-permute-done.30.refs_7_ = bf16[512,384]{1,0:T(8,128)(2,1)} collective-permute-done((bf16[512,384]{1,0:T(8,128)(2,1)}, bf16[512,384]{1,0:T(8,128)(2,1)}, u32[]{:S(2)}, u32[]{:S(2)}) %collective-permute-start.30) | collective-permute-done | bytes 393248 | tf_op jit(solution)/shard_map/ppermute | solution.py:524
  143.9 0.6 collective-permute-done.32.refs_9_
  144.5 6.1 %shard_map.134 = (f32[384,256]{1,0:T(8,128)}, bf16[384,256]{1,0:T(8,128)(2,1)}, bf16[384,256]{1,0:T(8,128)(2,1)}, bf16[384,256]{1,0:T(8,128)(2,1)}) custom-call(s32[5]{0:T(128)} %copy-done.3, bf16[512,1024]{1,0:T(8,128)(2,1)} %get-tuple-element.89.kept_ref, bf16[256,1024]{1,0:T(8,128)(2,1)} %collective-permute-done.24.refs_0_, ...), custom_call_target="tpu_custom_call" | custom-call | flops 19327352832 | bytes 8388608 | tf_op jit(solution)/shard_map/pallas_call | solution.py:601
  150.7 3.3 %collective-permute-start.33 = (bf16[384,256]{1,0:T(8,128)(2,1)}, bf16[384,256]{1,0:T(8,128)(2,1)S(1)}, u32[]{:S(2)}, u32[]{:S(2)}) collective-permute-start(bf16[384,256]{1,0:T(8,128)(2,1)} %get-tuple-element.110), channel_id=1, source_target_pairs={{0,64},{64,128},{128,192},{192,0},{1,65},{65,129},{129,193},{193,1... | collective-permute-start | bytes 589832 | tf_op jit(solution)/shard_map/ppermute | solution.py:524
  154.0 4.5 %collective-permute-start.34 = (bf16[384,256]{1,0:T(8,128)(2,1)}, bf16[384,256]{1,0:T(8,128)(2,1)S(1)}, u32[]{:S(2)}, u32[]{:S(2)}) collective-permute-start(bf16[384,256]{1,0:T(8,128)(2,1)} %get-tuple-element.111), channel_id=1, source_target_pairs={{0,128},{64,192},{128,0},{192,64},{1,129},{65,193},{129,1},{193,65... | collective-permute-start | bytes 589832 | tf_op jit(solution)/shard_map/ppermute | solution.py:524
  158.5 2.7 %collective-permute-start.35 = (bf16[384,256]{1,0:T(8,128)(2,1)}, bf16[384,256]{1,0:T(8,128)(2,1)S(1)}, u32[]{:S(2)}, u32[]{:S(2)}) collective-permute-start(bf16[384,256]{1,0:T(8,128)(2,1)} %get-tuple-element.112), channel_id=1, source_target_pairs={{0,192},{64,0},{128,64},{192,128},{1,193},{65,1},{129,65},{193,129... | collective-permute-start | bytes 589832 | tf_op jit(solution)/shard_map/ppermute | solution.py:524
  161.2 1.7 shard_map.135
  162.8 5.4 %collective-permute-done.34.refs_1_ = bf16[384,256]{1,0:T(8,128)(2,1)S(1)} collective-permute-done((bf16[384,256]{1,0:T(8,128)(2,1)}, bf16[384,256]{1,0:T(8,128)(2,1)S(1)}, u32[]{:S(2)}, u32[]{:S(2)}) %collective-permute-start.34) | collective-permute-done | bytes 196640 | tf_op jit(solution)/shard_map/ppermute | solution.py:524
  168.2 8.2 %collective-permute-done.35.refs_2_ = bf16[384,256]{1,0:T(8,128)(2,1)S(1)} collective-permute-done((bf16[384,256]{1,0:T(8,128)(2,1)}, bf16[384,256]{1,0:T(8,128)(2,1)S(1)}, u32[]{:S(2)}, u32[]{:S(2)}) %collective-permute-start.35) | collective-permute-done | bytes 196640 | tf_op jit(solution)/shard_map/ppermute | solution.py:524
  176.4 0.9 shard_map.136
  (62 shorter events, 4.7 us)
Async XLA Ops:
  3.4 6.6 %copy-start = (bf16[256,4096]{1,0:T(8,128)(2,1)S(1)}, bf16[256,4096]{1,0:T(8,128)(2,1)}, u32[]{:S(2)}) copy-start(bf16[256,4096]{1,0:T(8,128)(2,1)} %own_weight_ref.1) | copy-start | bytes 6291460
  3.4 6.8 %copy-start.2 = (bf16[1,512,256]{2,1,0:T(8,128)(2,1)S(1)}, bf16[1,512,256]{2,1,0:T(8,128)(2,1)}, u32[]{:S(2)}) copy-start(bf16[1,512,256]{2,1,0:T(8,128)(2,1)} %param.10) | copy-start | bytes 786436
  3.4 40.7 %all-to-all-start = ((bf16[16,144,512]{2,1,0:T(8,128)(2,1)}), bf16[16,144,512]{2,1,0:T(8,128)(2,1)}, u32[]{:S(2)}, u32[]{:S(2)}) async-start(bf16[16,144,512]{2,1,0:T(8,128)(2,1)} %shard_map.130), calls=%async_computation | async-start | bytes 4718592 | tf_op jit(solution)/shard_map/all_to_all | solution.py:534
  10.0 4.8 %collective-permute-start.1 = (bf16[256,4096]{1,0:T(8,128)(2,1)S(1)}, bf16[256,4096]{1,0:T(8,128)(2,1)}, u32[]{:S(2)}, u32[]{:S(2)}) collective-permute-start(bf16[256,4096]{1,0:T(8,128)(2,1)S(1)} %copy-done), channel_id=1, source_target_pairs={{0,1},{1,0},{2,3},{3,2},{4,5},{5,4},{6,7},{7,6},{8,9},{9,8},{10,11... | collective-permute-start | bytes 6291464 | tf_op jit(solution)/shard_map/ppermute | solution.py:524
  10.2 4.2 %collective-permute-start = (bf16[512,256]{1,0:T(8,128)(2,1)S(1)}, bf16[512,256]{1,0:T(8,128)(2,1)S(1)}, u32[]{:S(2)}, u32[]{:S(2)}) collective-permute-start(bf16[512,256]{1,0:T(8,128)(2,1)S(1)} %bitcast.20), channel_id=1, source_target_pairs={{0,1},{1,0},{2,3},{3,2},{4,5},{5,4},{6,7},{7,6},{8,9},{9,8},{10,11... | collective-permute-start | bytes 786440 | tf_op jit(solution)/shard_map/ppermute | solution.py:524
  10.7 71.9 %copy-start.3 = (s32[5]{0:T(128)}, s32[5]{0:T(128)S(1)}, u32[]{:S(2)}) copy-start(s32[5]{0:T(128)S(1)} %stack.23.place_ref) | copy-start | bytes 64
  18.8 25.0 %collective-permute-start.4 = (bf16[32,4096]{1,0:T(8,128)(2,1)S(1)}, bf16[32,4096]{1,0:T(8,128)(2,1)S(1)}, u32[]{:S(2)}, u32[]{:S(2)}) collective-permute-start(bf16[32,4096]{1,0:T(8,128)(2,1)S(1)} %get-tuple-element.68), channel_id=1, source_target_pairs={{0,2},{2,0},{1,3},{3,1},{4,6},{6,4},{5,7},{7,5},{8,10},{10,8},{9,1... | collective-permute-start | bytes 786440 | tf_op jit(solution)/shard_map/ppermute | solution.py:524
  20.4 23.5 %collective-permute-start.5 = (bf16[32,4096]{1,0:T(8,128)(2,1)S(1)}, bf16[32,4096]{1,0:T(8,128)(2,1)S(1)}, u32[]{:S(2)}, u32[]{:S(2)}) collective-permute-start(bf16[32,4096]{1,0:T(8,128)(2,1)S(1)} %get-tuple-element.70), channel_id=1, source_target_pairs={{0,4},{4,8},{8,12},{12,0},{1,5},{5,9},{9,13},{13,1},{2,6},{6,10},{... | collective-permute-start | bytes 786440 | tf_op jit(solution)/shard_map/ppermute | solution.py:524
  21.9 22.2 %collective-permute-start.6 = (bf16[32,4096]{1,0:T(8,128)(2,1)S(1)}, bf16[32,4096]{1,0:T(8,128)(2,1)S(1)}, u32[]{:S(2)}, u32[]{:S(2)}) collective-permute-start(bf16[32,4096]{1,0:T(8,128)(2,1)S(1)} %get-tuple-element.71), channel_id=1, source_target_pairs={{0,12},{4,0},{8,4},{12,8},{1,13},{5,1},{9,5},{13,9},{2,14},{6,2},{... | collective-permute-start | bytes 786440 | tf_op jit(solution)/shard_map/ppermute | solution.py:524
  22.4 34.2 %collective-permute-start.2 = (bf16[32,4096]{1,0:T(8,128)(2,1)S(1)}, bf16[32,4096]{1,0:T(8,128)(2,1)S(1)}, u32[]{:S(2)}, u32[]{:S(2)}) collective-permute-start(bf16[32,4096]{1,0:T(8,128)(2,1)S(1)} %get-tuple-element.65), channel_id=1, source_target_pairs={{0,4},{4,8},{8,12},{12,0},{1,5},{5,9},{9,13},{13,1},{2,6},{6,10},{... | collective-permute-start | bytes 786440 | tf_op jit(solution)/shard_map/ppermute | solution.py:524
  23.9 32.7 %collective-permute-start.3 = (bf16[32,4096]{1,0:T(8,128)(2,1)S(1)}, bf16[32,4096]{1,0:T(8,128)(2,1)S(1)}, u32[]{:S(2)}, u32[]{:S(2)}) collective-permute-start(bf16[32,4096]{1,0:T(8,128)(2,1)S(1)} %get-tuple-element.66), channel_id=1, source_target_pairs={{0,12},{4,0},{8,4},{12,8},{1,13},{5,1},{9,5},{13,9},{2,14},{6,2},{... | collective-permute-start | bytes 786440 | tf_op jit(solution)/shard_map/ppermute | solution.py:524
  44.1 12.4 %collective-permute-start.7 = (bf16[32,4096]{1,0:T(8,128)(2,1)S(1)}, bf16[32,4096]{1,0:T(8,128)(2,1)S(1)}, u32[]{:S(2)}, u32[]{:S(2)}) collective-permute-start(bf16[32,4096]{1,0:T(8,128)(2,1)S(1)} %add_convert_fusion.1), channel_id=1, source_target_pairs={{0,8},{4,12},{8,0},{12,4},{1,9},{5,13},{9,1},{13,5},{2,10},{6,14},... | collective-permute-start | bytes 786440 | tf_op jit(solution)/shard_map/ppermute | solution.py:524
  46.1 10.5 %collective-permute-start.8 = (bf16[32,4096]{1,0:T(8,128)(2,1)S(1)}, bf16[32,4096]{1,0:T(8,128)(2,1)S(1)}, u32[]{:S(2)}, u32[]{:S(2)}) collective-permute-start(bf16[32,4096]{1,0:T(8,128)(2,1)S(1)} %add_convert_fusion), channel_id=1, source_target_pairs={{0,2},{2,0},{1,3},{3,1},{4,6},{6,4},{5,7},{7,5},{8,10},{10,8},{9,1... | collective-permute-start | bytes 786440 | tf_op jit(solution)/shard_map/ppermute | solution.py:524
  46.9 9.8 %copy-start.5 = (bf16[1,32,4096]{2,1,0:T(8,128)(2,1)S(1)}, bf16[1,32,4096]{2,1,0:T(8,128)(2,1)}, u32[]{:S(2)}) copy-start(bf16[1,32,4096]{2,1,0:T(8,128)(2,1)} %param.11) | copy-start | bytes 786436
  46.9 10.1 %copy-start.6 = (f32[4096]{0:T(1024)S(1)}, f32[4096]{0:T(1024)}, u32[]{:S(2)}) copy-start(f32[4096]{0:T(1024)} %param.13) | copy-start | bytes 49156
  57.2 7.7 %collective-permute-start.9 = (bf16[32,4096]{1,0:T(8,128)(2,1)S(1)}, bf16[32,4096]{1,0:T(8,128)(2,1)S(1)}, u32[]{:S(2)}, u32[]{:S(2)}) collective-permute-start(bf16[32,4096]{1,0:T(8,128)(2,1)S(1)} %multiply_convert_fusion.refs_0_), channel_id=1, source_target_pairs={{0,2},{2,0},{1,3},{3,1},{4,6},{6,4},{5,7},{7,5},{8,10},{10,8},{9,1... | collective-permute-start | bytes 786440 | tf_op jit(solution)/shard_map/ppermute | solution.py:524
  58.6 10.7 %collective-permute-start.12 = (bf16[32,4096]{1,0:T(8,128)(2,1)S(1)}, bf16[32,4096]{1,0:T(8,128)(2,1)S(1)}, u32[]{:S(2)}, u32[]{:S(2)}) collective-permute-start(bf16[32,4096]{1,0:T(8,128)(2,1)S(1)} %multiply_convert_fusion.refs_0_), channel_id=1, source_target_pairs={{0,8},{4,12},{8,0},{12,4},{1,9},{5,13},{9,1},{13,5},{2,10},{6,14},... | collective-permute-start | bytes 786440 | tf_op jit(solution)/shard_map/ppermute | solution.py:524
  60.3 12.6 %collective-permute-start.10 = (bf16[32,4096]{1,0:T(8,128)(2,1)S(1)}, bf16[32,4096]{1,0:T(8,128)(2,1)S(1)}, u32[]{:S(2)}, u32[]{:S(2)}) collective-permute-start(bf16[32,4096]{1,0:T(8,128)(2,1)S(1)} %multiply_convert_fusion.refs_0_), channel_id=1, source_target_pairs={{0,12},{4,0},{8,4},{12,8},{1,13},{5,1},{9,5},{13,9},{2,14},{6,2},{... | collective-permute-start | bytes 786440 | tf_op jit(solution)/shard_map/ppermute | solution.py:524
  62.1 12.9 %collective-permute-start.13 = (bf16[32,4096]{1,0:T(8,128)(2,1)S(1)}, bf16[32,4096]{1,0:T(8,128)(2,1)S(1)}, u32[]{:S(2)}, u32[]{:S(2)}) collective-permute-start(bf16[32,4096]{1,0:T(8,128)(2,1)S(1)} %multiply_convert_fusion.refs_0_), channel_id=1, source_target_pairs={{0,4},{4,8},{8,12},{12,0},{1,5},{5,9},{9,13},{13,1},{2,6},{6,10},{... | collective-permute-start | bytes 786440 | tf_op jit(solution)/shard_map/ppermute | solution.py:524
  65.0 13.4 %collective-permute-start.11 = (bf16[32,4096]{1,0:T(8,128)(2,1)S(1)}, bf16[32,4096]{1,0:T(8,128)(2,1)S(1)}, u32[]{:S(2)}, u32[]{:S(2)}) collective-permute-start(bf16[32,4096]{1,0:T(8,128)(2,1)S(1)} %collective-permute-done.9.refs_1_), channel_id=1, source_target_pairs={{0,12},{4,0},{8,4},{12,8},{1,13},{5,1},{9,5},{13,9},{2,14},{6,2},{... | collective-permute-start | bytes 786440 | tf_op jit(solution)/shard_map/ppermute | solution.py:524
  66.8 12.7 %collective-permute-start.15 = (bf16[32,4096]{1,0:T(8,128)(2,1)S(1)}, bf16[32,4096]{1,0:T(8,128)(2,1)S(1)}, u32[]{:S(2)}, u32[]{:S(2)}) collective-permute-start(bf16[32,4096]{1,0:T(8,128)(2,1)S(1)} %collective-permute-done.9.refs_1_), channel_id=1, source_target_pairs={{0,4},{4,8},{8,12},{12,0},{1,5},{5,9},{9,13},{13,1},{2,6},{6,10},{... | collective-permute-start | bytes 786440 | tf_op jit(solution)/shard_map/ppermute | solution.py:524
  69.4 9.5 %collective-permute-start.14 = (bf16[32,4096]{1,0:T(8,128)(2,1)S(1)}, bf16[32,4096]{1,0:T(8,128)(2,1)S(1)}, u32[]{:S(2)}, u32[]{:S(2)}) collective-permute-start(bf16[32,4096]{1,0:T(8,128)(2,1)S(1)} %collective-permute-done.12.refs_4_), channel_id=1, source_target_pairs={{0,2},{2,0},{1,3},{3,1},{4,6},{6,4},{5,7},{7,5},{8,10},{10,8},{9,1... | collective-permute-start | bytes 786440 | tf_op jit(solution)/shard_map/ppermute | solution.py:524
  78.4 1.5 collective-permute-start.16
  78.4 1.9 %collective-permute-start.17 = (bf16[32,4096]{1,0:T(8,128)(2,1)S(1)}, bf16[32,4096]{1,0:T(8,128)(2,1)S(1)}, u32[]{:S(2)}, u32[]{:S(2)}) collective-permute-start(bf16[32,4096]{1,0:T(8,128)(2,1)S(1)} %collective-permute-done.9.refs_1_), channel_id=1, source_target_pairs={{0,1},{1,0},{2,3},{3,2},{4,5},{5,4},{6,7},{7,6},{8,9},{9,8},{10,11... | collective-permute-start | bytes 786440 | tf_op jit(solution)/shard_map/ppermute | solution.py:524
  78.9 1.8 %collective-permute-start.18 = (bf16[32,4096]{1,0:T(8,128)(2,1)S(1)}, bf16[32,4096]{1,0:T(8,128)(2,1)S(1)}, u32[]{:S(2)}, u32[]{:S(2)}) collective-permute-start(bf16[32,4096]{1,0:T(8,128)(2,1)S(1)} %collective-permute-done.10.refs_2_), channel_id=1, source_target_pairs={{0,1},{1,0},{2,3},{3,2},{4,5},{5,4},{6,7},{7,6},{8,9},{9,8},{10,11... | collective-permute-start | bytes 786440 | tf_op jit(solution)/shard_map/ppermute | solution.py:524
  78.9 2.5 %collective-permute-start.19 = (bf16[32,4096]{1,0:T(8,128)(2,1)S(1)}, bf16[32,4096]{1,0:T(8,128)(2,1)S(1)}, u32[]{:S(2)}, u32[]{:S(2)}) collective-permute-start(bf16[32,4096]{1,0:T(8,128)(2,1)S(1)} %collective-permute-done.11.refs_3_), channel_id=1, source_target_pairs={{0,1},{1,0},{2,3},{3,2},{4,5},{5,4},{6,7},{7,6},{8,9},{9,8},{10,11... | collective-permute-start | bytes 786440 | tf_op jit(solution)/shard_map/ppermute | solution.py:524
  79.4 2.1 %collective-permute-start.20 = (bf16[32,4096]{1,0:T(8,128)(2,1)S(1)}, bf16[32,4096]{1,0:T(8,128)(2,1)S(1)}, u32[]{:S(2)}, u32[]{:S(2)}) collective-permute-start(bf16[32,4096]{1,0:T(8,128)(2,1)S(1)} %collective-permute-done.12.refs_4_), channel_id=1, source_target_pairs={{0,1},{1,0},{2,3},{3,2},{4,5},{5,4},{6,7},{7,6},{8,9},{9,8},{10,11... | collective-permute-start | bytes 786440 | tf_op jit(solution)/shard_map/ppermute | solution.py:524
  79.9 1.9 %collective-permute-start.22 = (bf16[32,4096]{1,0:T(8,128)(2,1)S(1)}, bf16[32,4096]{1,0:T(8,128)(2,1)S(1)}, u32[]{:S(2)}, u32[]{:S(2)}) collective-permute-start(bf16[32,4096]{1,0:T(8,128)(2,1)S(1)} %collective-permute-done.13.refs_6_), channel_id=1, source_target_pairs={{0,1},{1,0},{2,3},{3,2},{4,5},{5,4},{6,7},{7,6},{8,9},{9,8},{10,11... | collective-permute-start | bytes 786440 | tf_op jit(solution)/shard_map/ppermute | solution.py:524
  80.3 1.9 %collective-permute-start.21 = (bf16[32,4096]{1,0:T(8,128)(2,1)S(1)}, bf16[32,4096]{1,0:T(8,128)(2,1)S(1)}, u32[]{:S(2)}, u32[]{:S(2)}) collective-permute-start(bf16[32,4096]{1,0:T(8,128)(2,1)S(1)} %collective-permute-done.14.refs_5_), channel_id=1, source_target_pairs={{0,1},{1,0},{2,3},{3,2},{4,5},{5,4},{6,7},{7,6},{8,9},{9,8},{10,11... | collective-permute-start | bytes 786440 | tf_op jit(solution)/shard_map/ppermute | solution.py:524
  80.7 1.9 %collective-permute-start.23 = (bf16[32,4096]{1,0:T(8,128)(2,1)S(1)}, bf16[32,4096]{1,0:T(8,128)(2,1)S(1)}, u32[]{:S(2)}, u32[]{:S(2)}) collective-permute-start(bf16[32,4096]{1,0:T(8,128)(2,1)S(1)} %collective-permute-done.15.refs_7_), channel_id=1, source_target_pairs={{0,1},{1,0},{2,3},{3,2},{4,5},{5,4},{6,7},{7,6},{8,9},{9,8},{10,11... | collective-permute-start | bytes 786440 | tf_op jit(solution)/shard_map/ppermute | solution.py:524
  87.9 0.7 copy-start.4
  88.6 28.7 %collective-permute-start.24 = (bf16[256,1024]{1,0:T(8,128)(2,1)}, bf16[256,1024]{1,0:T(8,128)(2,1)}, u32[]{:S(2)}, u32[]{:S(2)}) collective-permute-start(bf16[256,1024]{1,0:T(8,128)(2,1)} %get-tuple-element.90), channel_id=1, source_target_pairs={{0,16},{16,32},{32,48},{48,0},{1,17},{17,33},{33,49},{49,1},{2,18}... | collective-permute-start | bytes 1572872 | tf_op jit(solution)/shard_map/ppermute | solution.py:524
  89.9 27.4 %collective-permute-start.25 = (bf16[256,1024]{1,0:T(8,128)(2,1)}, bf16[256,1024]{1,0:T(8,128)(2,1)}, u32[]{:S(2)}, u32[]{:S(2)}) collective-permute-start(bf16[256,1024]{1,0:T(8,128)(2,1)} %get-tuple-element.91), channel_id=1, source_target_pairs={{0,32},{16,48},{32,0},{48,16},{1,33},{17,49},{33,1},{49,17},{2,34}... | collective-permute-start | bytes 1572872 | tf_op jit(solution)/shard_map/ppermute | solution.py:524
  92.6 24.7 %collective-permute-start.26 = (bf16[256,1024]{1,0:T(8,128)(2,1)}, bf16[256,1024]{1,0:T(8,128)(2,1)}, u32[]{:S(2)}, u32[]{:S(2)}) collective-permute-start(bf16[256,1024]{1,0:T(8,128)(2,1)} %get-tuple-element.92), channel_id=1, source_target_pairs={{0,48},{16,0},{32,16},{48,32},{1,49},{17,1},{33,17},{49,33},{2,50}... | collective-permute-start | bytes 1572872 | tf_op jit(solution)/shard_map/ppermute | solution.py:524
  117.4 43.8 %all-to-all-start.1 = ((bf16[16,144,512]{2,1,0:T(8,128)(2,1)}), bf16[16,144,512]{2,1,0:T(8,128)(2,1)S(1)}, u32[]{:S(2)}, u32[]{:S(2)}) async-start(bf16[16,144,512]{2,1,0:T(8,128)(2,1)} %get-tuple-element.113), calls=%async_computation.1 | async-start | bytes 4718592 | tf_op jit(solution)/shard_map/all_to_all | solution.py:648
  121.9 3.4 %collective-permute-start.27 = (bf16[256,1024]{1,0:T(8,128)(2,1)}, bf16[256,1024]{1,0:T(8,128)(2,1)S(1)}, u32[]{:S(2)}, u32[]{:S(2)}) collective-permute-start(bf16[256,1024]{1,0:T(8,128)(2,1)} %collective-permute-done.24.refs_0_), channel_id=1, source_target_pairs={{0,1},{1,0},{2,3},{3,2},{4,5},{5,4},{6,7},{7,6},{8,9},{9,8},{10,11... | collective-permute-start | bytes 1572872 | tf_op jit(solution)/shard_map/ppermute | solution.py:524
  122.1 3.2 %collective-permute-start.28 = (bf16[256,1024]{1,0:T(8,128)(2,1)}, bf16[256,1024]{1,0:T(8,128)(2,1)S(1)}, u32[]{:S(2)}, u32[]{:S(2)}) collective-permute-start(bf16[256,1024]{1,0:T(8,128)(2,1)} %collective-permute-done.25.refs_1_), channel_id=1, source_target_pairs={{0,1},{1,0},{2,3},{3,2},{4,5},{5,4},{6,7},{7,6},{8,9},{9,8},{10,11... | collective-permute-start | bytes 1572872 | tf_op jit(solution)/shard_map/ppermute | solution.py:524
  122.4 3.1 %collective-permute-start.29 = (bf16[256,1024]{1,0:T(8,128)(2,1)}, bf16[256,1024]{1,0:T(8,128)(2,1)S(1)}, u32[]{:S(2)}, u32[]{:S(2)}) collective-permute-start(bf16[256,1024]{1,0:T(8,128)(2,1)} %collective-permute-done.26.refs_2_), channel_id=1, source_target_pairs={{0,1},{1,0},{2,3},{3,2},{4,5},{5,4},{6,7},{7,6},{8,9},{9,8},{10,11... | collective-permute-start | bytes 1572872 | tf_op jit(solution)/shard_map/ppermute | solution.py:524
  122.6 21.3 %collective-permute-start.30 = (bf16[512,384]{1,0:T(8,128)(2,1)}, bf16[512,384]{1,0:T(8,128)(2,1)}, u32[]{:S(2)}, u32[]{:S(2)}) collective-permute-start(bf16[512,384]{1,0:T(8,128)(2,1)} %get-tuple-element.108.refs_6_), channel_id=1, source_target_pairs={{0,16},{16,32},{32,48},{48,0},{1,17},{17,33},{33,49},{49,1},{2,18}... | collective-permute-start | bytes 1179656 | tf_op jit(solution)/shard_map/ppermute | solution.py:524
  123.2 20.7 %collective-permute-start.31 = (bf16[512,384]{1,0:T(8,128)(2,1)}, bf16[512,384]{1,0:T(8,128)(2,1)}, u32[]{:S(2)}, u32[]{:S(2)}) collective-permute-start(bf16[512,384]{1,0:T(8,128)(2,1)} %get-tuple-element.108.refs_6_), channel_id=1, source_target_pairs={{0,32},{16,48},{32,0},{48,16},{1,33},{17,49},{33,1},{49,17},{2,34}... | collective-permute-start | bytes 1179656 | tf_op jit(solution)/shard_map/ppermute | solution.py:524
  125.3 19.3 %copy-start.7 = (bf16[256,1024]{1,0:T(8,128)(2,1)}, bf16[256,1024]{1,0:T(8,128)(2,1)S(1)}, u32[]{:S(2)}) copy-start(bf16[256,1024]{1,0:T(8,128)(2,1)S(1)} %collective-permute-done.27.refs_3_) | copy-start | bytes 1572868
  125.3 19.3 %copy-start.8 = (bf16[256,1024]{1,0:T(8,128)(2,1)}, bf16[256,1024]{1,0:T(8,128)(2,1)S(1)}, u32[]{:S(2)}) copy-start(bf16[256,1024]{1,0:T(8,128)(2,1)S(1)} %collective-permute-done.28.refs_4_) | copy-start | bytes 1572868
  125.5 19.0 %copy-start.9 = (bf16[256,1024]{1,0:T(8,128)(2,1)}, bf16[256,1024]{1,0:T(8,128)(2,1)S(1)}, u32[]{:S(2)}) copy-start(bf16[256,1024]{1,0:T(8,128)(2,1)S(1)} %collective-permute-done.29.refs_5_) | copy-start | bytes 1572868
  125.5 19.0 %collective-permute-start.32 = (bf16[512,384]{1,0:T(8,128)(2,1)}, bf16[512,384]{1,0:T(8,128)(2,1)}, u32[]{:S(2)}, u32[]{:S(2)}) collective-permute-start(bf16[512,384]{1,0:T(8,128)(2,1)} %get-tuple-element.108.refs_6_), channel_id=1, source_target_pairs={{0,48},{16,0},{32,16},{48,32},{1,49},{17,1},{33,17},{49,33},{2,50}... | collective-permute-start | bytes 1179656 | tf_op jit(solution)/shard_map/ppermute | solution.py:524
  150.7 25.7 %copy-start.1 = (f32[384,256]{1,0:T(8,128)S(1)}, f32[384,256]{1,0:T(8,128)}, u32[]{:S(2)}) copy-start(f32[384,256]{1,0:T(8,128)} %get-tuple-element.120.kept_ref) | copy-start | bytes 1179652
  150.7 12.1 %collective-permute-start.33 = (bf16[384,256]{1,0:T(8,128)(2,1)}, bf16[384,256]{1,0:T(8,128)(2,1)S(1)}, u32[]{:S(2)}, u32[]{:S(2)}) collective-permute-start(bf16[384,256]{1,0:T(8,128)(2,1)} %get-tuple-element.110), channel_id=1, source_target_pairs={{0,64},{64,128},{128,192},{192,0},{1,65},{65,129},{129,193},{193,1... | collective-permute-start | bytes 589832 | tf_op jit(solution)/shard_map/ppermute | solution.py:524
  154.0 14.2 %collective-permute-start.34 = (bf16[384,256]{1,0:T(8,128)(2,1)}, bf16[384,256]{1,0:T(8,128)(2,1)S(1)}, u32[]{:S(2)}, u32[]{:S(2)}) collective-permute-start(bf16[384,256]{1,0:T(8,128)(2,1)} %get-tuple-element.111), channel_id=1, source_target_pairs={{0,128},{64,192},{128,0},{192,64},{1,129},{65,193},{129,1},{193,65... | collective-permute-start | bytes 589832 | tf_op jit(solution)/shard_map/ppermute | solution.py:524
  158.5 17.9 %collective-permute-start.35 = (bf16[384,256]{1,0:T(8,128)(2,1)}, bf16[384,256]{1,0:T(8,128)(2,1)S(1)}, u32[]{:S(2)}, u32[]{:S(2)}) collective-permute-start(bf16[384,256]{1,0:T(8,128)(2,1)} %get-tuple-element.112), channel_id=1, source_target_pairs={{0,192},{64,0},{128,64},{192,128},{1,193},{65,1},{129,65},{193,129... | collective-permute-start | bytes 589832 | tf_op jit(solution)/shard_map/ppermute | solution.py:524

commit v3 on v2

--- a/solution.py
+++ b/solution.py
@@ -216,7 +216,7 @@
         totals_ref[ahead] = total
         return carry
 
-    lax.fori_loop(0, 4, body, 0)
+    lax.fori_loop(0, 4, body, 0, unroll=2)
     kept_sum_ref[...] = totals_ref[0]
     for step, sent_ref in enumerate(sent_refs):
         sent_ref[...] = totals_ref[step + 1].astype(BF16)

time: 179 us -> 178 us (level)
  no operation moved by 1% of the time
where the time goes in v3:
time: 178 us; the launch traced here: 177 us
  waiting for transfers between devices  70.5 us (40%)
  Pallas kernels  53.3 us (30%)
  starting transfers between devices  49.9 us (28%)
    ppermute x36, waiting for transfers between devices, shift(): lax.ppermute(rows, axis, [(i, (i + step) % size) for i in range(size)])  70.5 us
    ppermute x36, starting transfers between devices, shift(): lax.ppermute(rows, axis, [(i, (i + step) % size) for i in range(size)])  38.8 us
    pallas_call x1, Pallas kernels, attention(): grid_call(attention_kernel, 1 + IMAGE // FORWARD_ROWS, [IN_SMEM, IN_SMEM,...  23.2 us
    pallas_call x1, Pallas kernels, image_forward(): grid_call(image_forward_kernel, IMAGE // FORWARD_ROWS, [IN_SMEM, fixed(HE...  9.72 us
    all_to_all x1, starting transfers between devices, encode(): lax.all_to_all(packed, SEQ, split_axis=0, concat_axis=0, tiled=True)  6.54 us
    pallas_call x1, Pallas kernels, weight_sums(): whole_call(weight_kernel, [total] + [rows_of(columns, FEATURES)] * 3, 1,...  5.68 us
    pallas_call x1, Pallas kernels, project(): pl.pallas_call(text_kernel, out_shape=[rows_of(PROMPT, columns), rows_of(...  5.31 us
    all_to_all x1, starting transfers between devices, on_device(): lax.all_to_all(sent, SEQ, split_axis=0, concat_axis=0, tiled=True)  4.55 us
  transfers between devices with their start and end apart: 38, of which 20 were waited for; matrix products, arithmetic and copies ran while one was open for 0% of the time, Pallas kernels for 25%

profile of v3, /device:TPU:8, one launch (start us, length us, event | category | flops | bytes accessed | tf_op | source)
XLA Modules:
  0.0 176.8 jit_solution(6513686917713142205)
XLA Ops:
  0.6 2.8 %shard_map.130 = bf16[16,144,512]{2,1,0:T(8,128)(2,1)} custom-call(bf16[128,6144]{1,0:T(8,128)(2,1)} %bitcast.22, bf16[128,2048]{1,0:T(8,128)(2,1)} %bitcast.23, bf16[32,2048]{1,0:T(8,128)(2,1)} %bitcast.24), custom_call_target="tpu_custom_call" | custom-call | bytes 4194304 | tf_op jit(solution)/shard_map/pallas_call | solution.py:113
  3.4 6.5 %all-to-all-start = ((bf16[16,144,512]{2,1,0:T(8,128)(2,1)}), bf16[16,144,512]{2,1,0:T(8,128)(2,1)}, u32[]{:S(2)}, u32[]{:S(2)}) async-start(bf16[16,144,512]{2,1,0:T(8,128)(2,1)} %shard_map.130), calls=%async_computation | async-start | bytes 4718592 | tf_op jit(solution)/shard_map/all_to_all | solution.py:534
  10.7 3.7 %collective-permute-done.other_ref = bf16[512,256]{1,0:T(8,128)(2,1)S(1)} collective-permute-done((bf16[512,256]{1,0:T(8,128)(2,1)S(1)}, bf16[512,256]{1,0:T(8,128)(2,1)S(1)}, u32[]{:S(2)}, u32[]{:S(2)}) %collective-permute-start) | collective-permute-done | bytes 262176 | tf_op jit(solution)/shard_map/ppermute | solution.py:524
  14.7 4.1 %shard_map.129 = (bf16[32,4096]{1,0:T(8,128)(2,1)S(1)}, bf16[32,4096]{1,0:T(8,128)(2,1)S(1)}, bf16[32,4096]{1,0:T(8,128)(2,1)S(1)}, bf16[32,4096]{1,0:T(8,128)(2...) custom-call(s32[5]{0:T(128)S(1)} %stack.23.place_ref, ...), custom_call_target="tpu_custom_call" | custom-call | flops 1073741824 | bytes 8388608 | tf_op jit(solution)/shard_map/pallas_call | solution.py:535
  18.8 1.6 collective-permute-start.4
  20.4 1.5 collective-permute-start.5
  21.9 0.5 collective-permute-start.6
  22.4 1.5 collective-permute-start.2
  23.9 0.5 collective-permute-start.3
  24.4 19.4 %collective-permute-done.4 = bf16[32,4096]{1,0:T(8,128)(2,1)S(1)} collective-permute-done((bf16[32,4096]{1,0:T(8,128)(2,1)S(1)}, bf16[32,4096]{1,0:T(8,128)(2,1)S(1)}, u32[]{:S(2)}, u32[]{:S(2)}) %collective-permute-start.4) | collective-permute-done | bytes 262176 | tf_op jit(solution)/shard_map/ppermute | solution.py:524
  44.1 2.0 %collective-permute-start.7 = (bf16[32,4096]{1,0:T(8,128)(2,1)S(1)}, bf16[32,4096]{1,0:T(8,128)(2,1)S(1)}, u32[]{:S(2)}, u32[]{:S(2)}) collective-permute-start(bf16[32,4096]{1,0:T(8,128)(2,1)S(1)} %add_convert_fusion.1), channel_id=1, source_target_pairs={{0,8},{4,12},{8,0},{12,4},{1,9},{5,13},{9,1},{13,5},{2,10},{6,14},... | collective-permute-start | bytes 786440 | tf_op jit(solution)/shard_map/ppermute | solution.py:524
  46.1 0.7 collective-permute-start.8
  46.9 9.7 %shard_map.131 = (bf16[2048,2048]{1,0:T(8,128)(2,1)}, bf16[2048,512]{1,0:T(8,128)(2,1)}, f32[2048,128]{1,0:T(8,128)}, f32[2048,128]{1,0:T(8,128)}, f32[2048,128]{1,0:T(8,128)}, /*index=5*/bf16[512,128]{1,0:T(8,128)(2,1)}) custom-call(s32[32]{0:T(128)} %bitcast.28, bf16[16,144,512]{2,1,0:T(8,128)(2,1)} %all-to-all-done.packed_ref), custom_call_target="tpu_custom_call" | custom-call | flops 64424509440 | bytes 536870912 | tf_op jit(solution)/shard_map/pallas_call | solution.py:492
  57.2 1.4 collective-permute-start.9
  58.6 1.6 collective-permute-start.12
  60.3 1.8 %collective-permute-start.10 = (bf16[32,4096]{1,0:T(8,128)(2,1)S(1)}, bf16[32,4096]{1,0:T(8,128)(2,1)S(1)}, u32[]{:S(2)}, u32[]{:S(2)}) collective-permute-start(bf16[32,4096]{1,0:T(8,128)(2,1)S(1)} %multiply_convert_fusion.refs_0_), channel_id=1, source_target_pairs={{0,12},{4,0},{8,4},{12,8},{1,13},{5,1},{9,5},{13,9},{2,14},{6,2},{... | collective-permute-start | bytes 786440 | tf_op jit(solution)/shard_map/ppermute | solution.py:524
  62.3 2.7 %collective-permute-done.9.refs_1_ = bf16[32,4096]{1,0:T(8,128)(2,1)S(1)} collective-permute-done((bf16[32,4096]{1,0:T(8,128)(2,1)S(1)}, bf16[32,4096]{1,0:T(8,128)(2,1)S(1)}, u32[]{:S(2)}, u32[]{:S(2)}) %collective-permute-start.9) | collective-permute-done | bytes 262176 | tf_op jit(solution)/shard_map/ppermute | solution.py:524
  65.0 1.8 %collective-permute-start.11 = (bf16[32,4096]{1,0:T(8,128)(2,1)S(1)}, bf16[32,4096]{1,0:T(8,128)(2,1)S(1)}, u32[]{:S(2)}, u32[]{:S(2)}) collective-permute-start(bf16[32,4096]{1,0:T(8,128)(2,1)S(1)} %collective-permute-done.9.refs_1_), channel_id=1, source_target_pairs={{0,12},{4,0},{8,4},{12,8},{1,13},{5,1},{9,5},{13,9},{2,14},{6,2},{... | collective-permute-start | bytes 786440 | tf_op jit(solution)/shard_map/ppermute | solution.py:524
  67.0 2.4 %collective-permute-done.12.refs_4_ = bf16[32,4096]{1,0:T(8,128)(2,1)S(1)} collective-permute-done((bf16[32,4096]{1,0:T(8,128)(2,1)S(1)}, bf16[32,4096]{1,0:T(8,128)(2,1)S(1)}, u32[]{:S(2)}, u32[]{:S(2)}) %collective-permute-start.12) | collective-permute-done | bytes 262176 | tf_op jit(solution)/shard_map/ppermute | solution.py:524
  69.4 0.7 collective-permute-start.14
  70.1 2.8 %collective-permute-done.10.refs_2_ = bf16[32,4096]{1,0:T(8,128)(2,1)S(1)} collective-permute-done((bf16[32,4096]{1,0:T(8,128)(2,1)S(1)}, bf16[32,4096]{1,0:T(8,128)(2,1)S(1)}, u32[]{:S(2)}, u32[]{:S(2)}) %collective-permute-start.10) | collective-permute-done | bytes 262176 | tf_op jit(solution)/shard_map/ppermute | solution.py:524
  72.9 2.1 %collective-permute-done.13.refs_6_ = bf16[32,4096]{1,0:T(8,128)(2,1)S(1)} collective-permute-done((bf16[32,4096]{1,0:T(8,128)(2,1)S(1)}, bf16[32,4096]{1,0:T(8,128)(2,1)S(1)}, u32[]{:S(2)}, u32[]{:S(2)}) %collective-permute-start.13) | collective-permute-done | bytes 262176 | tf_op jit(solution)/shard_map/ppermute | solution.py:524
  74.9 3.5 %collective-permute-done.11.refs_3_ = bf16[32,4096]{1,0:T(8,128)(2,1)S(1)} collective-permute-done((bf16[32,4096]{1,0:T(8,128)(2,1)S(1)}, bf16[32,4096]{1,0:T(8,128)(2,1)S(1)}, u32[]{:S(2)}, u32[]{:S(2)}) %collective-permute-start.11) | collective-permute-done | bytes 262176 | tf_op jit(solution)/shard_map/ppermute | solution.py:524
  78.4 0.5 collective-permute-start.17
  78.9 0.5 collective-permute-start.19
  79.5 0.4 collective-permute-done.16.refs_8_
  81.8 0.4 collective-permute-done.21.refs_13_
  82.2 0.4 collective-permute-done.23.refs_15_
  82.6 5.3 %shard_map.132 = (bf16[512,384]{1,0:T(8,128)(2,1)S(1)}, bf16[512,1024]{1,0:T(8,128)(2,1)}, bf16[256,1024]{1,0:T(8,128)(2,1)}, bf16[256,1024]{1,0:T(8,128)(2,1)}, bf16[256,1024]{1,0:T(8,128)(2,1)}) custom-call(s32[5]{0:T(128)S(1)} %stack.23.place_ref, bf16[32,4096]{1,0:T(8,128)(2,1)S(1)} %multiply_convert_fusion.refs_0_, ...), custom_call_target="tpu_custom_call" | custom-call | flops 1610612736 | bytes 8388608 | tf_op jit(solution)/shard_map/pallas_call | solution.py:580
  87.9 0.7 copy-done.4
  88.6 1.3 collective-permute-start.24
  89.9 2.7 %collective-permute-start.25 = (bf16[256,1024]{1,0:T(8,128)(2,1)}, bf16[256,1024]{1,0:T(8,128)(2,1)}, u32[]{:S(2)}, u32[]{:S(2)}) collective-permute-start(bf16[256,1024]{1,0:T(8,128)(2,1)} %get-tuple-element.91), channel_id=1, source_target_pairs={{0,32},{16,48},{32,0},{48,16},{1,33},{17,49},{33,1},{49,17},{2,34}... | collective-permute-start | bytes 1572872 | tf_op jit(solution)/shard_map/ppermute | solution.py:524
  92.6 1.4 collective-permute-start.26
  94.1 23.2 %shard_map.133 = (bf16[16,144,512]{2,1,0:T(8,128)(2,1)}, bf16[512,384]{1,0:T(8,128)(2,1)}) custom-call(s32[1]{0:T(128)S(6)} %copy.14.length_ref, s32[32]{0:T(128)} %bitcast.29, bf16[512,384]{1,0:T(8,128)(2,1)} %copy-done.4, bf16[512,128]{1,0:T(8,128)(2,1)} %get-tuple-element.94.text_do_ref, bf16[2048,512]{1,0:T(8,128)(2,1)} %get-tuple-element.95.rows_ref, ...), custom_call_target="tpu_custom_call" | custom-call | flops 237565378560 | bytes 536870912 | tf_op jit(solution)/shard_map/pallas_call | solution.py:509
  117.4 4.6 %all-to-all-start.1 = ((bf16[16,144,512]{2,1,0:T(8,128)(2,1)}), bf16[16,144,512]{2,1,0:T(8,128)(2,1)S(1)}, u32[]{:S(2)}, u32[]{:S(2)}) async-start(bf16[16,144,512]{2,1,0:T(8,128)(2,1)} %get-tuple-element.113), calls=%async_computation.1 | async-start | bytes 4718592 | tf_op jit(solution)/shard_map/all_to_all | solution.py:648
  122.6 0.6 collective-permute-start.30
  123.2 2.1 %collective-permute-start.31 = (bf16[512,384]{1,0:T(8,128)(2,1)}, bf16[512,384]{1,0:T(8,128)(2,1)}, u32[]{:S(2)}, u32[]{:S(2)}) collective-permute-start(bf16[512,384]{1,0:T(8,128)(2,1)} %get-tuple-element.108.refs_6_), channel_id=1, source_target_pairs={{0,32},{16,48},{32,0},{48,16},{1,33},{17,49},{33,1},{49,17},{2,34}... | collective-permute-start | bytes 1179656 | tf_op jit(solution)/shard_map/ppermute | solution.py:524
  125.5 1.2 collective-permute-start.32
  126.8 17.1 %collective-permute-done.30.refs_7_ = bf16[512,384]{1,0:T(8,128)(2,1)} collective-permute-done((bf16[512,384]{1,0:T(8,128)(2,1)}, bf16[512,384]{1,0:T(8,128)(2,1)}, u32[]{:S(2)}, u32[]{:S(2)}) %collective-permute-start.30) | collective-permute-done | bytes 393248 | tf_op jit(solution)/shard_map/ppermute | solution.py:524
  143.9 0.6 collective-permute-done.32.refs_9_
  144.5 5.7 %shard_map.134 = (f32[384,256]{1,0:T(8,128)}, bf16[384,256]{1,0:T(8,128)(2,1)}, bf16[384,256]{1,0:T(8,128)(2,1)}, bf16[384,256]{1,0:T(8,128)(2,1)}) custom-call(s32[5]{0:T(128)} %copy-done.3, bf16[512,1024]{1,0:T(8,128)(2,1)} %get-tuple-element.89.kept_ref, bf16[256,1024]{1,0:T(8,128)(2,1)} %collective-permute-done.24.refs_0_, ...), custom_call_target="tpu_custom_call" | custom-call | flops 19327352832 | bytes 8388608 | tf_op jit(solution)/shard_map/pallas_call | solution.py:601
  150.2 3.3 %collective-permute-start.33 = (bf16[384,256]{1,0:T(8,128)(2,1)}, bf16[384,256]{1,0:T(8,128)(2,1)S(1)}, u32[]{:S(2)}, u32[]{:S(2)}) collective-permute-start(bf16[384,256]{1,0:T(8,128)(2,1)} %get-tuple-element.110), channel_id=1, source_target_pairs={{0,64},{64,128},{128,192},{192,0},{1,65},{65,129},{129,193},{193,1... | collective-permute-start | bytes 589832 | tf_op jit(solution)/shard_map/ppermute | solution.py:524
  153.5 4.5 %collective-permute-start.34 = (bf16[384,256]{1,0:T(8,128)(2,1)}, bf16[384,256]{1,0:T(8,128)(2,1)S(1)}, u32[]{:S(2)}, u32[]{:S(2)}) collective-permute-start(bf16[384,256]{1,0:T(8,128)(2,1)} %get-tuple-element.111), channel_id=1, source_target_pairs={{0,128},{64,192},{128,0},{192,64},{1,129},{65,193},{129,1},{193,65... | collective-permute-start | bytes 589832 | tf_op jit(solution)/shard_map/ppermute | solution.py:524
  158.0 2.7 %collective-permute-start.35 = (bf16[384,256]{1,0:T(8,128)(2,1)}, bf16[384,256]{1,0:T(8,128)(2,1)S(1)}, u32[]{:S(2)}, u32[]{:S(2)}) collective-permute-start(bf16[384,256]{1,0:T(8,128)(2,1)} %get-tuple-element.112), channel_id=1, source_target_pairs={{0,192},{64,0},{128,64},{192,128},{1,193},{65,1},{129,65},{193,129... | collective-permute-start | bytes 589832 | tf_op jit(solution)/shard_map/ppermute | solution.py:524
  160.7 1.7 shard_map.135
  162.4 5.3 %collective-permute-done.34.refs_1_ = bf16[384,256]{1,0:T(8,128)(2,1)S(1)} collective-permute-done((bf16[384,256]{1,0:T(8,128)(2,1)}, bf16[384,256]{1,0:T(8,128)(2,1)S(1)}, u32[]{:S(2)}, u32[]{:S(2)}) %collective-permute-start.34) | collective-permute-done | bytes 196640 | tf_op jit(solution)/shard_map/ppermute | solution.py:524
  167.7 8.2 %collective-permute-done.35.refs_2_ = bf16[384,256]{1,0:T(8,128)(2,1)S(1)} collective-permute-done((bf16[384,256]{1,0:T(8,128)(2,1)}, bf16[384,256]{1,0:T(8,128)(2,1)S(1)}, u32[]{:S(2)}, u32[]{:S(2)}) %collective-permute-start.35) | collective-permute-done | bytes 196640 | tf_op jit(solution)/shard_map/ppermute | solution.py:524
  175.9 0.9 shard_map.136
  (62 shorter events, 4.7 us)
Async XLA Ops:
  3.4 6.6 %copy-start = (bf16[256,4096]{1,0:T(8,128)(2,1)S(1)}, bf16[256,4096]{1,0:T(8,128)(2,1)}, u32[]{:S(2)}) copy-start(bf16[256,4096]{1,0:T(8,128)(2,1)} %own_weight_ref.1) | copy-start | bytes 6291460
  3.4 6.8 %copy-start.2 = (bf16[1,512,256]{2,1,0:T(8,128)(2,1)S(1)}, bf16[1,512,256]{2,1,0:T(8,128)(2,1)}, u32[]{:S(2)}) copy-start(bf16[1,512,256]{2,1,0:T(8,128)(2,1)} %param.10) | copy-start | bytes 786436
  3.4 40.7 %all-to-all-start = ((bf16[16,144,512]{2,1,0:T(8,128)(2,1)}), bf16[16,144,512]{2,1,0:T(8,128)(2,1)}, u32[]{:S(2)}, u32[]{:S(2)}) async-start(bf16[16,144,512]{2,1,0:T(8,128)(2,1)} %shard_map.130), calls=%async_computation | async-start | bytes 4718592 | tf_op jit(solution)/shard_map/all_to_all | solution.py:534
  10.0 4.8 %collective-permute-start.1 = (bf16[256,4096]{1,0:T(8,128)(2,1)S(1)}, bf16[256,4096]{1,0:T(8,128)(2,1)}, u32[]{:S(2)}, u32[]{:S(2)}) collective-permute-start(bf16[256,4096]{1,0:T(8,128)(2,1)S(1)} %copy-done), channel_id=1, source_target_pairs={{0,1},{1,0},{2,3},{3,2},{4,5},{5,4},{6,7},{7,6},{8,9},{9,8},{10,11... | collective-permute-start | bytes 6291464 | tf_op jit(solution)/shard_map/ppermute | solution.py:524
  10.2 4.2 %collective-permute-start = (bf16[512,256]{1,0:T(8,128)(2,1)S(1)}, bf16[512,256]{1,0:T(8,128)(2,1)S(1)}, u32[]{:S(2)}, u32[]{:S(2)}) collective-permute-start(bf16[512,256]{1,0:T(8,128)(2,1)S(1)} %bitcast.20), channel_id=1, source_target_pairs={{0,1},{1,0},{2,3},{3,2},{4,5},{5,4},{6,7},{7,6},{8,9},{9,8},{10,11... | collective-permute-start | bytes 786440 | tf_op jit(solution)/shard_map/ppermute | solution.py:524
  10.7 71.9 %copy-start.3 = (s32[5]{0:T(128)}, s32[5]{0:T(128)S(1)}, u32[]{:S(2)}) copy-start(s32[5]{0:T(128)S(1)} %stack.23.place_ref) | copy-start | bytes 64
  18.8 25.0 %collective-permute-start.4 = (bf16[32,4096]{1,0:T(8,128)(2,1)S(1)}, bf16[32,4096]{1,0:T(8,128)(2,1)S(1)}, u32[]{:S(2)}, u32[]{:S(2)}) collective-permute-start(bf16[32,4096]{1,0:T(8,128)(2,1)S(1)} %get-tuple-element.68), channel_id=1, source_target_pairs={{0,2},{2,0},{1,3},{3,1},{4,6},{6,4},{5,7},{7,5},{8,10},{10,8},{9,1... | collective-permute-start | bytes 786440 | tf_op jit(solution)/shard_map/ppermute | solution.py:524
  20.4 23.5 %collective-permute-start.5 = (bf16[32,4096]{1,0:T(8,128)(2,1)S(1)}, bf16[32,4096]{1,0:T(8,128)(2,1)S(1)}, u32[]{:S(2)}, u32[]{:S(2)}) collective-permute-start(bf16[32,4096]{1,0:T(8,128)(2,1)S(1)} %get-tuple-element.70), channel_id=1, source_target_pairs={{0,4},{4,8},{8,12},{12,0},{1,5},{5,9},{9,13},{13,1},{2,6},{6,10},{... | collective-permute-start | bytes 786440 | tf_op jit(solution)/shard_map/ppermute | solution.py:524
  21.9 22.2 %collective-permute-start.6 = (bf16[32,4096]{1,0:T(8,128)(2,1)S(1)}, bf16[32,4096]{1,0:T(8,128)(2,1)S(1)}, u32[]{:S(2)}, u32[]{:S(2)}) collective-permute-start(bf16[32,4096]{1,0:T(8,128)(2,1)S(1)} %get-tuple-element.71), channel_id=1, source_target_pairs={{0,12},{4,0},{8,4},{12,8},{1,13},{5,1},{9,5},{13,9},{2,14},{6,2},{... | collective-permute-start | bytes 786440 | tf_op jit(solution)/shard_map/ppermute | solution.py:524
  22.4 34.2 %collective-permute-start.2 = (bf16[32,4096]{1,0:T(8,128)(2,1)S(1)}, bf16[32,4096]{1,0:T(8,128)(2,1)S(1)}, u32[]{:S(2)}, u32[]{:S(2)}) collective-permute-start(bf16[32,4096]{1,0:T(8,128)(2,1)S(1)} %get-tuple-element.65), channel_id=1, source_target_pairs={{0,4},{4,8},{8,12},{12,0},{1,5},{5,9},{9,13},{13,1},{2,6},{6,10},{... | collective-permute-start | bytes 786440 | tf_op jit(solution)/shard_map/ppermute | solution.py:524
  23.9 32.7 %collective-permute-start.3 = (bf16[32,4096]{1,0:T(8,128)(2,1)S(1)}, bf16[32,4096]{1,0:T(8,128)(2,1)S(1)}, u32[]{:S(2)}, u32[]{:S(2)}) collective-permute-start(bf16[32,4096]{1,0:T(8,128)(2,1)S(1)} %get-tuple-element.66), channel_id=1, source_target_pairs={{0,12},{4,0},{8,4},{12,8},{1,13},{5,1},{9,5},{13,9},{2,14},{6,2},{... | collective-permute-start | bytes 786440 | tf_op jit(solution)/shard_map/ppermute | solution.py:524
  44.1 12.4 %collective-permute-start.7 = (bf16[32,4096]{1,0:T(8,128)(2,1)S(1)}, bf16[32,4096]{1,0:T(8,128)(2,1)S(1)}, u32[]{:S(2)}, u32[]{:S(2)}) collective-permute-start(bf16[32,4096]{1,0:T(8,128)(2,1)S(1)} %add_convert_fusion.1), channel_id=1, source_target_pairs={{0,8},{4,12},{8,0},{12,4},{1,9},{5,13},{9,1},{13,5},{2,10},{6,14},... | collective-permute-start | bytes 786440 | tf_op jit(solution)/shard_map/ppermute | solution.py:524
  46.1 10.5 %collective-permute-start.8 = (bf16[32,4096]{1,0:T(8,128)(2,1)S(1)}, bf16[32,4096]{1,0:T(8,128)(2,1)S(1)}, u32[]{:S(2)}, u32[]{:S(2)}) collective-permute-start(bf16[32,4096]{1,0:T(8,128)(2,1)S(1)} %add_convert_fusion), channel_id=1, source_target_pairs={{0,2},{2,0},{1,3},{3,1},{4,6},{6,4},{5,7},{7,5},{8,10},{10,8},{9,1... | collective-permute-start | bytes 786440 | tf_op jit(solution)/shard_map/ppermute | solution.py:524
  46.9 9.8 %copy-start.5 = (bf16[1,32,4096]{2,1,0:T(8,128)(2,1)S(1)}, bf16[1,32,4096]{2,1,0:T(8,128)(2,1)}, u32[]{:S(2)}) copy-start(bf16[1,32,4096]{2,1,0:T(8,128)(2,1)} %param.11) | copy-start | bytes 786436
  46.9 10.1 %copy-start.6 = (f32[4096]{0:T(1024)S(1)}, f32[4096]{0:T(1024)}, u32[]{:S(2)}) copy-start(f32[4096]{0:T(1024)} %param.13) | copy-start | bytes 49156
  57.2 7.7 %collective-permute-start.9 = (bf16[32,4096]{1,0:T(8,128)(2,1)S(1)}, bf16[32,4096]{1,0:T(8,128)(2,1)S(1)}, u32[]{:S(2)}, u32[]{:S(2)}) collective-permute-start(bf16[32,4096]{1,0:T(8,128)(2,1)S(1)} %multiply_convert_fusion.refs_0_), channel_id=1, source_target_pairs={{0,2},{2,0},{1,3},{3,1},{4,6},{6,4},{5,7},{7,5},{8,10},{10,8},{9,1... | collective-permute-start | bytes 786440 | tf_op jit(solution)/shard_map/ppermute | solution.py:524
  58.6 10.7 %collective-permute-start.12 = (bf16[32,4096]{1,0:T(8,128)(2,1)S(1)}, bf16[32,4096]{1,0:T(8,128)(2,1)S(1)}, u32[]{:S(2)}, u32[]{:S(2)}) collective-permute-start(bf16[32,4096]{1,0:T(8,128)(2,1)S(1)} %multiply_convert_fusion.refs_0_), channel_id=1, source_target_pairs={{0,8},{4,12},{8,0},{12,4},{1,9},{5,13},{9,1},{13,5},{2,10},{6,14},... | collective-permute-start | bytes 786440 | tf_op jit(solution)/shard_map/ppermute | solution.py:524
  60.3 12.6 %collective-permute-start.10 = (bf16[32,4096]{1,0:T(8,128)(2,1)S(1)}, bf16[32,4096]{1,0:T(8,128)(2,1)S(1)}, u32[]{:S(2)}, u32[]{:S(2)}) collective-permute-start(bf16[32,4096]{1,0:T(8,128)(2,1)S(1)} %multiply_convert_fusion.refs_0_), channel_id=1, source_target_pairs={{0,12},{4,0},{8,4},{12,8},{1,13},{5,1},{9,5},{13,9},{2,14},{6,2},{... | collective-permute-start | bytes 786440 | tf_op jit(solution)/shard_map/ppermute | solution.py:524
  62.1 12.9 %collective-permute-start.13 = (bf16[32,4096]{1,0:T(8,128)(2,1)S(1)}, bf16[32,4096]{1,0:T(8,128)(2,1)S(1)}, u32[]{:S(2)}, u32[]{:S(2)}) collective-permute-start(bf16[32,4096]{1,0:T(8,128)(2,1)S(1)} %multiply_convert_fusion.refs_0_), channel_id=1, source_target_pairs={{0,4},{4,8},{8,12},{12,0},{1,5},{5,9},{9,13},{13,1},{2,6},{6,10},{... | collective-permute-start | bytes 786440 | tf_op jit(solution)/shard_map/ppermute | solution.py:524
  65.0 13.4 %collective-permute-start.11 = (bf16[32,4096]{1,0:T(8,128)(2,1)S(1)}, bf16[32,4096]{1,0:T(8,128)(2,1)S(1)}, u32[]{:S(2)}, u32[]{:S(2)}) collective-permute-start(bf16[32,4096]{1,0:T(8,128)(2,1)S(1)} %collective-permute-done.9.refs_1_), channel_id=1, source_target_pairs={{0,12},{4,0},{8,4},{12,8},{1,13},{5,1},{9,5},{13,9},{2,14},{6,2},{... | collective-permute-start | bytes 786440 | tf_op jit(solution)/shard_map/ppermute | solution.py:524
  66.8 12.7 %collective-permute-start.15 = (bf16[32,4096]{1,0:T(8,128)(2,1)S(1)}, bf16[32,4096]{1,0:T(8,128)(2,1)S(1)}, u32[]{:S(2)}, u32[]{:S(2)}) collective-permute-start(bf16[32,4096]{1,0:T(8,128)(2,1)S(1)} %collective-permute-done.9.refs_1_), channel_id=1, source_target_pairs={{0,4},{4,8},{8,12},{12,0},{1,5},{5,9},{9,13},{13,1},{2,6},{6,10},{... | collective-permute-start | bytes 786440 | tf_op jit(solution)/shard_map/ppermute | solution.py:524
  69.4 9.5 %collective-permute-start.14 = (bf16[32,4096]{1,0:T(8,128)(2,1)S(1)}, bf16[32,4096]{1,0:T(8,128)(2,1)S(1)}, u32[]{:S(2)}, u32[]{:S(2)}) collective-permute-start(bf16[32,4096]{1,0:T(8,128)(2,1)S(1)} %collective-permute-done.12.refs_4_), channel_id=1, source_target_pairs={{0,2},{2,0},{1,3},{3,1},{4,6},{6,4},{5,7},{7,5},{8,10},{10,8},{9,1... | collective-permute-start | bytes 786440 | tf_op jit(solution)/shard_map/ppermute | solution.py:524
  78.4 1.5 collective-permute-start.16
  78.4 1.9 %collective-permute-start.17 = (bf16[32,4096]{1,0:T(8,128)(2,1)S(1)}, bf16[32,4096]{1,0:T(8,128)(2,1)S(1)}, u32[]{:S(2)}, u32[]{:S(2)}) collective-permute-start(bf16[32,4096]{1,0:T(8,128)(2,1)S(1)} %collective-permute-done.9.refs_1_), channel_id=1, source_target_pairs={{0,1},{1,0},{2,3},{3,2},{4,5},{5,4},{6,7},{7,6},{8,9},{9,8},{10,11... | collective-permute-start | bytes 786440 | tf_op jit(solution)/shard_map/ppermute | solution.py:524
  78.9 1.8 %collective-permute-start.18 = (bf16[32,4096]{1,0:T(8,128)(2,1)S(1)}, bf16[32,4096]{1,0:T(8,128)(2,1)S(1)}, u32[]{:S(2)}, u32[]{:S(2)}) collective-permute-start(bf16[32,4096]{1,0:T(8,128)(2,1)S(1)} %collective-permute-done.10.refs_2_), channel_id=1, source_target_pairs={{0,1},{1,0},{2,3},{3,2},{4,5},{5,4},{6,7},{7,6},{8,9},{9,8},{10,11... | collective-permute-start | bytes 786440 | tf_op jit(solution)/shard_map/ppermute | solution.py:524
  78.9 2.5 %collective-permute-start.19 = (bf16[32,4096]{1,0:T(8,128)(2,1)S(1)}, bf16[32,4096]{1,0:T(8,128)(2,1)S(1)}, u32[]{:S(2)}, u32[]{:S(2)}) collective-permute-start(bf16[32,4096]{1,0:T(8,128)(2,1)S(1)} %collective-permute-done.11.refs_3_), channel_id=1, source_target_pairs={{0,1},{1,0},{2,3},{3,2},{4,5},{5,4},{6,7},{7,6},{8,9},{9,8},{10,11... | collective-permute-start | bytes 786440 | tf_op jit(solution)/shard_map/ppermute | solution.py:524
  79.4 2.1 %collective-permute-start.20 = (bf16[32,4096]{1,0:T(8,128)(2,1)S(1)}, bf16[32,4096]{1,0:T(8,128)(2,1)S(1)}, u32[]{:S(2)}, u32[]{:S(2)}) collective-permute-start(bf16[32,4096]{1,0:T(8,128)(2,1)S(1)} %collective-permute-done.12.refs_4_), channel_id=1, source_target_pairs={{0,1},{1,0},{2,3},{3,2},{4,5},{5,4},{6,7},{7,6},{8,9},{9,8},{10,11... | collective-permute-start | bytes 786440 | tf_op jit(solution)/shard_map/ppermute | solution.py:524
  79.9 1.9 %collective-permute-start.22 = (bf16[32,4096]{1,0:T(8,128)(2,1)S(1)}, bf16[32,4096]{1,0:T(8,128)(2,1)S(1)}, u32[]{:S(2)}, u32[]{:S(2)}) collective-permute-start(bf16[32,4096]{1,0:T(8,128)(2,1)S(1)} %collective-permute-done.13.refs_6_), channel_id=1, source_target_pairs={{0,1},{1,0},{2,3},{3,2},{4,5},{5,4},{6,7},{7,6},{8,9},{9,8},{10,11... | collective-permute-start | bytes 786440 | tf_op jit(solution)/shard_map/ppermute | solution.py:524
  80.3 1.9 %collective-permute-start.21 = (bf16[32,4096]{1,0:T(8,128)(2,1)S(1)}, bf16[32,4096]{1,0:T(8,128)(2,1)S(1)}, u32[]{:S(2)}, u32[]{:S(2)}) collective-permute-start(bf16[32,4096]{1,0:T(8,128)(2,1)S(1)} %collective-permute-done.14.refs_5_), channel_id=1, source_target_pairs={{0,1},{1,0},{2,3},{3,2},{4,5},{5,4},{6,7},{7,6},{8,9},{9,8},{10,11... | collective-permute-start | bytes 786440 | tf_op jit(solution)/shard_map/ppermute | solution.py:524
  80.7 1.9 %collective-permute-start.23 = (bf16[32,4096]{1,0:T(8,128)(2,1)S(1)}, bf16[32,4096]{1,0:T(8,128)(2,1)S(1)}, u32[]{:S(2)}, u32[]{:S(2)}) collective-permute-start(bf16[32,4096]{1,0:T(8,128)(2,1)S(1)} %collective-permute-done.15.refs_7_), channel_id=1, source_target_pairs={{0,1},{1,0},{2,3},{3,2},{4,5},{5,4},{6,7},{7,6},{8,9},{9,8},{10,11... | collective-permute-start | bytes 786440 | tf_op jit(solution)/shard_map/ppermute | solution.py:524
  87.9 0.7 copy-start.4
  88.6 28.7 %collective-permute-start.24 = (bf16[256,1024]{1,0:T(8,128)(2,1)}, bf16[256,1024]{1,0:T(8,128)(2,1)}, u32[]{:S(2)}, u32[]{:S(2)}) collective-permute-start(bf16[256,1024]{1,0:T(8,128)(2,1)} %get-tuple-element.90), channel_id=1, source_target_pairs={{0,16},{16,32},{32,48},{48,0},{1,17},{17,33},{33,49},{49,1},{2,18}... | collective-permute-start | bytes 1572872 | tf_op jit(solution)/shard_map/ppermute | solution.py:524
  89.9 27.4 %collective-permute-start.25 = (bf16[256,1024]{1,0:T(8,128)(2,1)}, bf16[256,1024]{1,0:T(8,128)(2,1)}, u32[]{:S(2)}, u32[]{:S(2)}) collective-permute-start(bf16[256,1024]{1,0:T(8,128)(2,1)} %get-tuple-element.91), channel_id=1, source_target_pairs={{0,32},{16,48},{32,0},{48,16},{1,33},{17,49},{33,1},{49,17},{2,34}... | collective-permute-start | bytes 1572872 | tf_op jit(solution)/shard_map/ppermute | solution.py:524
  92.6 24.7 %collective-permute-start.26 = (bf16[256,1024]{1,0:T(8,128)(2,1)}, bf16[256,1024]{1,0:T(8,128)(2,1)}, u32[]{:S(2)}, u32[]{:S(2)}) collective-permute-start(bf16[256,1024]{1,0:T(8,128)(2,1)} %get-tuple-element.92), channel_id=1, source_target_pairs={{0,48},{16,0},{32,16},{48,32},{1,49},{17,1},{33,17},{49,33},{2,50}... | collective-permute-start | bytes 1572872 | tf_op jit(solution)/shard_map/ppermute | solution.py:524
  117.4 43.3 %all-to-all-start.1 = ((bf16[16,144,512]{2,1,0:T(8,128)(2,1)}), bf16[16,144,512]{2,1,0:T(8,128)(2,1)S(1)}, u32[]{:S(2)}, u32[]{:S(2)}) async-start(bf16[16,144,512]{2,1,0:T(8,128)(2,1)} %get-tuple-element.113), calls=%async_computation.1 | async-start | bytes 4718592 | tf_op jit(solution)/shard_map/all_to_all | solution.py:648
  121.9 3.4 %collective-permute-start.27 = (bf16[256,1024]{1,0:T(8,128)(2,1)}, bf16[256,1024]{1,0:T(8,128)(2,1)S(1)}, u32[]{:S(2)}, u32[]{:S(2)}) collective-permute-start(bf16[256,1024]{1,0:T(8,128)(2,1)} %collective-permute-done.24.refs_0_), channel_id=1, source_target_pairs={{0,1},{1,0},{2,3},{3,2},{4,5},{5,4},{6,7},{7,6},{8,9},{9,8},{10,11... | collective-permute-start | bytes 1572872 | tf_op jit(solution)/shard_map/ppermute | solution.py:524
  122.1 3.2 %collective-permute-start.28 = (bf16[256,1024]{1,0:T(8,128)(2,1)}, bf16[256,1024]{1,0:T(8,128)(2,1)S(1)}, u32[]{:S(2)}, u32[]{:S(2)}) collective-permute-start(bf16[256,1024]{1,0:T(8,128)(2,1)} %collective-permute-done.25.refs_1_), channel_id=1, source_target_pairs={{0,1},{1,0},{2,3},{3,2},{4,5},{5,4},{6,7},{7,6},{8,9},{9,8},{10,11... | collective-permute-start | bytes 1572872 | tf_op jit(solution)/shard_map/ppermute | solution.py:524
  122.4 3.1 %collective-permute-start.29 = (bf16[256,1024]{1,0:T(8,128)(2,1)}, bf16[256,1024]{1,0:T(8,128)(2,1)S(1)}, u32[]{:S(2)}, u32[]{:S(2)}) collective-permute-start(bf16[256,1024]{1,0:T(8,128)(2,1)} %collective-permute-done.26.refs_2_), channel_id=1, source_target_pairs={{0,1},{1,0},{2,3},{3,2},{4,5},{5,4},{6,7},{7,6},{8,9},{9,8},{10,11... | collective-permute-start | bytes 1572872 | tf_op jit(solution)/shard_map/ppermute | solution.py:524
  122.6 21.3 %collective-permute-start.30 = (bf16[512,384]{1,0:T(8,128)(2,1)}, bf16[512,384]{1,0:T(8,128)(2,1)}, u32[]{:S(2)}, u32[]{:S(2)}) collective-permute-start(bf16[512,384]{1,0:T(8,128)(2,1)} %get-tuple-element.108.refs_6_), channel_id=1, source_target_pairs={{0,16},{16,32},{32,48},{48,0},{1,17},{17,33},{33,49},{49,1},{2,18}... | collective-permute-start | bytes 1179656 | tf_op jit(solution)/shard_map/ppermute | solution.py:524
  123.2 20.7 %collective-permute-start.31 = (bf16[512,384]{1,0:T(8,128)(2,1)}, bf16[512,384]{1,0:T(8,128)(2,1)}, u32[]{:S(2)}, u32[]{:S(2)}) collective-permute-start(bf16[512,384]{1,0:T(8,128)(2,1)} %get-tuple-element.108.refs_6_), channel_id=1, source_target_pairs={{0,32},{16,48},{32,0},{48,16},{1,33},{17,49},{33,1},{49,17},{2,34}... | collective-permute-start | bytes 1179656 | tf_op jit(solution)/shard_map/ppermute | solution.py:524
  125.3 19.3 %copy-start.7 = (bf16[256,1024]{1,0:T(8,128)(2,1)}, bf16[256,1024]{1,0:T(8,128)(2,1)S(1)}, u32[]{:S(2)}) copy-start(bf16[256,1024]{1,0:T(8,128)(2,1)S(1)} %collective-permute-done.27.refs_3_) | copy-start | bytes 1572868
  125.3 19.3 %copy-start.8 = (bf16[256,1024]{1,0:T(8,128)(2,1)}, bf16[256,1024]{1,0:T(8,128)(2,1)S(1)}, u32[]{:S(2)}) copy-start(bf16[256,1024]{1,0:T(8,128)(2,1)S(1)} %collective-permute-done.28.refs_4_) | copy-start | bytes 1572868
  125.5 19.0 %copy-start.9 = (bf16[256,1024]{1,0:T(8,128)(2,1)}, bf16[256,1024]{1,0:T(8,128)(2,1)S(1)}, u32[]{:S(2)}) copy-start(bf16[256,1024]{1,0:T(8,128)(2,1)S(1)} %collective-permute-done.29.refs_5_) | copy-start | bytes 1572868
  125.5 19.0 %collective-permute-start.32 = (bf16[512,384]{1,0:T(8,128)(2,1)}, bf16[512,384]{1,0:T(8,128)(2,1)}, u32[]{:S(2)}, u32[]{:S(2)}) collective-permute-start(bf16[512,384]{1,0:T(8,128)(2,1)} %get-tuple-element.108.refs_6_), channel_id=1, source_target_pairs={{0,48},{16,0},{32,16},{48,32},{1,49},{17,1},{33,17},{49,33},{2,50}... | collective-permute-start | bytes 1179656 | tf_op jit(solution)/shard_map/ppermute | solution.py:524
  150.2 25.7 %copy-start.1 = (f32[384,256]{1,0:T(8,128)S(1)}, f32[384,256]{1,0:T(8,128)}, u32[]{:S(2)}) copy-start(f32[384,256]{1,0:T(8,128)} %get-tuple-element.120.kept_ref) | copy-start | bytes 1179652
  150.2 12.1 %collective-permute-start.33 = (bf16[384,256]{1,0:T(8,128)(2,1)}, bf16[384,256]{1,0:T(8,128)(2,1)S(1)}, u32[]{:S(2)}, u32[]{:S(2)}) collective-permute-start(bf16[384,256]{1,0:T(8,128)(2,1)} %get-tuple-element.110), channel_id=1, source_target_pairs={{0,64},{64,128},{128,192},{192,0},{1,65},{65,129},{129,193},{193,1... | collective-permute-start | bytes 589832 | tf_op jit(solution)/shard_map/ppermute | solution.py:524
  153.5 14.2 %collective-permute-start.34 = (bf16[384,256]{1,0:T(8,128)(2,1)}, bf16[384,256]{1,0:T(8,128)(2,1)S(1)}, u32[]{:S(2)}, u32[]{:S(2)}) collective-permute-start(bf16[384,256]{1,0:T(8,128)(2,1)} %get-tuple-element.111), channel_id=1, source_target_pairs={{0,128},{64,192},{128,0},{192,64},{1,129},{65,193},{129,1},{193,65... | collective-permute-start | bytes 589832 | tf_op jit(solution)/shard_map/ppermute | solution.py:524
  158.0 17.9 %collective-permute-start.35 = (bf16[384,256]{1,0:T(8,128)(2,1)}, bf16[384,256]{1,0:T(8,128)(2,1)S(1)}, u32[]{:S(2)}, u32[]{:S(2)}) collective-permute-start(bf16[384,256]{1,0:T(8,128)(2,1)} %get-tuple-element.112), channel_id=1, source_target_pairs={{0,192},{64,0},{128,64},{192,128},{1,193},{65,1},{129,65},{193,129... | collective-permute-start | bytes 589832 | tf_op jit(solution)/shard_map/ppermute | solution.py:524
